TPU v7x, 512 devices: a whole 4x4x16 slice. The times are simulated.
512 devices in a mesh: seq: 16 (over x, y_hi, core), res: 32 (over y_lo, z).
Axes of the slice: x: 4, y: 4 (y_hi: 2, y_lo: 2; y = y_hi * 2 + y_lo), z: 16, core: 2. Of those that a mesh axis runs over, the one named last changes fastest.
Arguments:
- alignment_features: bfloat16 [64, 4096, 256], P('seq', 'res'), may hold values from -6 to 6
- coupling_logit_offset: bfloat16 [8, 4096, 4096], P(None, 'res', 'seq'), may hold values from -310 to 310
- contact_tile_filter: int32 [32, 32], replicated, may hold values from 0 to 1, as said below
- standard_scale_array: float32 [256], replicated, may hold values from 0.25 to 1.75
- standard_offset_array: float32 [256], replicated, may hold values from -3 to 3
- probe_projection: bfloat16 [256, 256], replicated, may hold values from -0.375 to 0.375
- lookup_projection: bfloat16 [256, 256], replicated, may hold values from -0.375 to 0.375
- content_projection: bfloat16 [256, 256], replicated, may hold values from -0.375 to 0.375
- sigmoid_projection: bfloat16 [256, 256], replicated, may hold values from -0.375 to 0.375
- sigmoid_offset_array: float32 [256], replicated, may hold values from -4 to 4
- result_projection: bfloat16 [256, 256], replicated, may hold values from -0.375 to 0.375
- result_offset: float32 [256], replicated, may hold values from -3 to 3
Outputs:
- update: bfloat16 [64, 4096, 256], P('seq', 'res')
Inputs may be any that keep to these rules, and one draw needn't show every extreme that they name: `contact_tile_filter`: every diagonal entry is 1.
All inputs are finite; a program needn't handle non-finite values.
Results may differ from a plain program's by a relative error of at most 0.006.
Values may be sent and summed in bfloat16 or wider, within the bound.
No kernel may reach another device: no remote copies, remote signals or barrier semaphores. Data moves between devices by JAX's collectives and lax.ppermute only.
A program may use at most 64 MiB of HBM per device.

v0:
```python
import jax
import jax.numpy as jnp
from jax import lax
from jax.sharding import PartitionSpec as P

H = 8
DH = 32
BLOCK = 128


def from_behind(value, axis, steps):
    count = lax.axis_size(axis)
    pairs = [(source, (source + steps) % count) for source in range(count)]
    return lax.ppermute(value, axis, pairs)


def standardize_features(source, standard_scale_array, standard_offset_array):
    values_f = source.astype(jnp.float32)
    center = jnp.mean(values_f, axis=-1, keepdims=True)
    spread = jnp.mean((values_f - center) ** 2, axis=-1, keepdims=True)
    return (values_f - center) * lax.rsqrt(
        spread + 1e-05
    ) * standard_scale_array + standard_offset_array


def on_device(
    alignment_features,
    coupling_logit_offset,
    contact_tile_filter,
    standard_scale_array,
    standard_offset_array,
    probe_projection,
    lookup_projection,
    content_projection,
    sigmoid_projection,
    sigmoid_offset_array,
    result_projection,
    result_offset,
):
    alignment_depth, amino_positions, feature_width = alignment_features.shape
    cycle_size = lax.axis_size("res")
    own_index = lax.axis_index("res")
    standardized_features = standardize_features(
        alignment_features, standard_scale_array, standard_offset_array
    ).astype(jnp.bfloat16)
    flat_rows = standardized_features.reshape(-1, feature_width)
    queries = (
        jnp.dot(flat_rows, probe_projection, preferred_element_type=jnp.float32) * (1.0 / DH**0.5)
    ).astype(jnp.bfloat16)
    queries = queries.reshape(alignment_depth, amino_positions, H, DH)
    gate_val = jax.nn.sigmoid(
        jnp.dot(flat_rows, sigmoid_projection, preferred_element_type=jnp.float32)
        + sigmoid_offset_array
    )
    full_bias = lax.all_gather(coupling_logit_offset, "seq", axis=2, tiled=True)
    block_ids = jnp.arange(cycle_size, dtype=jnp.int32)
    mask_line = jnp.sum(
        contact_tile_filter * (block_ids == own_index)[:, None].astype(jnp.int32), axis=0
    )

    def allowed(first, span_len):
        col_blocks = (first + jnp.arange(span_len, dtype=jnp.int32)) // BLOCK
        hits = (col_blocks[:, None] == block_ids[None, :]).astype(jnp.int32) * mask_line[None, :]
        return jnp.sum(hits, axis=1) > 0

    def update(current, normed_part, first, live_cols):
        maxima, totals, accum = current
        span_len = normed_part.shape[1]
        part_flat = normed_part.reshape(-1, feature_width)
        key_four = (
            jnp.dot(part_flat, lookup_projection, preferred_element_type=jnp.float32)
            .astype(jnp.bfloat16)
            .reshape(alignment_depth, span_len, H, DH)
        )
        value_four = (
            jnp.dot(part_flat, content_projection, preferred_element_type=jnp.float32)
            .astype(jnp.bfloat16)
            .reshape(alignment_depth, span_len, H, DH)
        )
        bias_part = lax.dynamic_slice_in_dim(full_bias, first, span_len, 2).astype(jnp.float32)
        scores = (
            jnp.einsum("sihd,sjhd->shij", queries, key_four, preferred_element_type=jnp.float32)
            + bias_part[None]
        )
        scores = jnp.where(live_cols[None, None, None, :], scores, -1000000000.0)
        new_max = jnp.maximum(maxima, jnp.max(scores, axis=-1))
        rescale = jnp.exp(maxima - new_max)
        weights_exp = jnp.exp(scores - new_max[..., None])
        totals = totals * rescale + jnp.sum(weights_exp, axis=-1)
        accum = accum * rescale[..., None] + jnp.einsum(
            "shij,sjhd->shid",
            weights_exp.astype(jnp.bfloat16),
            value_four,
            preferred_element_type=jnp.float32,
        )
        return (new_max, totals, accum)

    def attend(current, normed_part, first):
        live_cols = allowed(first, normed_part.shape[1])
        return update(current, normed_part, first, live_cols)

    start_state = (
        jnp.full((alignment_depth, H, amino_positions), -1e30, jnp.float32),
        jnp.zeros((alignment_depth, H, amino_positions), jnp.float32),
        jnp.zeros((alignment_depth, H, amino_positions, DH), jnp.float32),
    )
    own_first = own_index * amino_positions
    soft_state = attend(start_state, standardized_features, own_first)

    def cycle_step(turn, carry):
        travel_rows, current = carry
        travel_rows = from_behind(travel_rows, "res", 1)
        source = (own_index - turn) % cycle_size
        current = attend(current, travel_rows, source * amino_positions)
        return (travel_rows, current)

    cycle_out = lax.fori_loop(1, cycle_size, cycle_step, (standardized_features, soft_state))
    soft_state = cycle_out[1]
    maxima, totals, accum = soft_state
    attended = (
        (accum / totals[..., None])
        .transpose(0, 2, 1, 3)
        .reshape(alignment_depth * amino_positions, feature_width)
    )
    gated = (gate_val * attended).astype(jnp.bfloat16)
    result = jnp.dot(gated, result_projection, preferred_element_type=jnp.float32) + result_offset
    return result.astype(jnp.bfloat16).reshape(alignment_depth, amino_positions, feature_width)


def solution(mesh):
    return jax.shard_map(
        on_device,
        mesh=mesh,
        in_specs=(
            P("seq", "res", None),
            P(None, "res", "seq"),
            P(),
            P(),
            P(),
            P(),
            P(),
            P(),
            P(),
            P(),
            P(),
            P(),
        ),
        out_specs=P("seq", "res", None),
        check_vma=False,
    )
```

profile of v0, /device:TPU:8, one launch (start us, length us, event | category | flops | bytes accessed | tf_op | source)
XLA Modules:
  0.0 530.8 jit_solution(4863219814315033627)
XLA Ops:
  13.1 89.3 %all-gather.2.cloned.1.call-done = bf16[8,128,4096]{1,2,0:T(8,128)(2,1)} async-done(((bf16[8,128,256]{1,2,0:T(8,128)(2,1)}), bf16[8,128,4096]{1,2,0:T(8,128)(2,1)}) %all-gather.2.cloned.1.call-update) | async-done | bytes 8388624 | tf_op jit(solution)/shard_map/all_gather | solution.py:55
  105.2 416.6 %while.22 = (s32[]{:T(128)}, bf16[4,128,256]{2,1,0:T(8,128)(2,1)S(1)}, f32[4,8,128]{2,1,0:T(8,128)S(1)}, f32[4,8,128]{2,1,0:T(8,128)S(1)}, f32[4,8,128,32]{2,3,1...) while((s32[]{:T(128)}, ...), condition=%wide.region_10.11_spmd.clone, body=%wide.region_6.10_spmd.clone.sunk | while | flops 205674512 | bytes 14682868 | solution.py:117
  109.8 8.9 %collective-permute-done = bf16[4,128,256]{2,1,0:T(8,128)(2,1)S(1)} collective-permute-done((bf16[4,128,256]{2,1,0:T(8,128)(2,1)S(1)}, bf16[4,128,256]{2,1,0:T(8,128)(2,1)S(1)}, u32[]{:S(2)}, u32[]{:S(2)}) %collective-permute-start) | collective-permute-done | bytes 262176 | tf_op jit(solution)/shard_map/while/body/eval_jaxpr/ppermute | solution.py:14
  124.2 8.9 %collective-permute-done = bf16[4,128,256]{2,1,0:T(8,128)(2,1)S(1)} collective-permute-done((bf16[4,128,256]{2,1,0:T(8,128)(2,1)S(1)}, bf16[4,128,256]{2,1,0:T(8,128)(2,1)S(1)}, u32[]{:S(2)}, u32[]{:S(2)}) %collective-permute-start) | collective-permute-done | bytes 262176 | tf_op jit(solution)/shard_map/while/body/eval_jaxpr/ppermute | solution.py:14
  138.6 8.0 %collective-permute-done = bf16[4,128,256]{2,1,0:T(8,128)(2,1)S(1)} collective-permute-done((bf16[4,128,256]{2,1,0:T(8,128)(2,1)S(1)}, bf16[4,128,256]{2,1,0:T(8,128)(2,1)S(1)}, u32[]{:S(2)}, u32[]{:S(2)}) %collective-permute-start) | collective-permute-done | bytes 262176 | tf_op jit(solution)/shard_map/while/body/eval_jaxpr/ppermute | solution.py:14
  152.1 7.3 %collective-permute-done = bf16[4,128,256]{2,1,0:T(8,128)(2,1)S(1)} collective-permute-done((bf16[4,128,256]{2,1,0:T(8,128)(2,1)S(1)}, bf16[4,128,256]{2,1,0:T(8,128)(2,1)S(1)}, u32[]{:S(2)}, u32[]{:S(2)}) %collective-permute-start) | collective-permute-done | bytes 262176 | tf_op jit(solution)/shard_map/while/body/eval_jaxpr/ppermute | solution.py:14
  164.9 7.3 %collective-permute-done = bf16[4,128,256]{2,1,0:T(8,128)(2,1)S(1)} collective-permute-done((bf16[4,128,256]{2,1,0:T(8,128)(2,1)S(1)}, bf16[4,128,256]{2,1,0:T(8,128)(2,1)S(1)}, u32[]{:S(2)}, u32[]{:S(2)}) %collective-permute-start) | collective-permute-done | bytes 262176 | tf_op jit(solution)/shard_map/while/body/eval_jaxpr/ppermute | solution.py:14
  177.6 7.3 %collective-permute-done = bf16[4,128,256]{2,1,0:T(8,128)(2,1)S(1)} collective-permute-done((bf16[4,128,256]{2,1,0:T(8,128)(2,1)S(1)}, bf16[4,128,256]{2,1,0:T(8,128)(2,1)S(1)}, u32[]{:S(2)}, u32[]{:S(2)}) %collective-permute-start) | collective-permute-done | bytes 262176 | tf_op jit(solution)/shard_map/while/body/eval_jaxpr/ppermute | solution.py:14
  190.4 7.3 %collective-permute-done = bf16[4,128,256]{2,1,0:T(8,128)(2,1)S(1)} collective-permute-done((bf16[4,128,256]{2,1,0:T(8,128)(2,1)S(1)}, bf16[4,128,256]{2,1,0:T(8,128)(2,1)S(1)}, u32[]{:S(2)}, u32[]{:S(2)}) %collective-permute-start) | collective-permute-done | bytes 262176 | tf_op jit(solution)/shard_map/while/body/eval_jaxpr/ppermute | solution.py:14
  203.2 7.3 %collective-permute-done = bf16[4,128,256]{2,1,0:T(8,128)(2,1)S(1)} collective-permute-done((bf16[4,128,256]{2,1,0:T(8,128)(2,1)S(1)}, bf16[4,128,256]{2,1,0:T(8,128)(2,1)S(1)}, u32[]{:S(2)}, u32[]{:S(2)}) %collective-permute-start) | collective-permute-done | bytes 262176 | tf_op jit(solution)/shard_map/while/body/eval_jaxpr/ppermute | solution.py:14
  216.0 7.3 %collective-permute-done = bf16[4,128,256]{2,1,0:T(8,128)(2,1)S(1)} collective-permute-done((bf16[4,128,256]{2,1,0:T(8,128)(2,1)S(1)}, bf16[4,128,256]{2,1,0:T(8,128)(2,1)S(1)}, u32[]{:S(2)}, u32[]{:S(2)}) %collective-permute-start) | collective-permute-done | bytes 262176 | tf_op jit(solution)/shard_map/while/body/eval_jaxpr/ppermute | solution.py:14
  228.8 8.3 %collective-permute-done = bf16[4,128,256]{2,1,0:T(8,128)(2,1)S(1)} collective-permute-done((bf16[4,128,256]{2,1,0:T(8,128)(2,1)S(1)}, bf16[4,128,256]{2,1,0:T(8,128)(2,1)S(1)}, u32[]{:S(2)}, u32[]{:S(2)}) %collective-permute-start) | collective-permute-done | bytes 262176 | tf_op jit(solution)/shard_map/while/body/eval_jaxpr/ppermute | solution.py:14
  242.6 9.5 %collective-permute-done = bf16[4,128,256]{2,1,0:T(8,128)(2,1)S(1)} collective-permute-done((bf16[4,128,256]{2,1,0:T(8,128)(2,1)S(1)}, bf16[4,128,256]{2,1,0:T(8,128)(2,1)S(1)}, u32[]{:S(2)}, u32[]{:S(2)}) %collective-permute-start) | collective-permute-done | bytes 262176 | tf_op jit(solution)/shard_map/while/body/eval_jaxpr/ppermute | solution.py:14
  257.6 9.6 %collective-permute-done = bf16[4,128,256]{2,1,0:T(8,128)(2,1)S(1)} collective-permute-done((bf16[4,128,256]{2,1,0:T(8,128)(2,1)S(1)}, bf16[4,128,256]{2,1,0:T(8,128)(2,1)S(1)}, u32[]{:S(2)}, u32[]{:S(2)}) %collective-permute-start) | collective-permute-done | bytes 262176 | tf_op jit(solution)/shard_map/while/body/eval_jaxpr/ppermute | solution.py:14
  272.6 8.8 %collective-permute-done = bf16[4,128,256]{2,1,0:T(8,128)(2,1)S(1)} collective-permute-done((bf16[4,128,256]{2,1,0:T(8,128)(2,1)S(1)}, bf16[4,128,256]{2,1,0:T(8,128)(2,1)S(1)}, u32[]{:S(2)}, u32[]{:S(2)}) %collective-permute-start) | collective-permute-done | bytes 262176 | tf_op jit(solution)/shard_map/while/body/eval_jaxpr/ppermute | solution.py:14
  286.9 7.9 %collective-permute-done = bf16[4,128,256]{2,1,0:T(8,128)(2,1)S(1)} collective-permute-done((bf16[4,128,256]{2,1,0:T(8,128)(2,1)S(1)}, bf16[4,128,256]{2,1,0:T(8,128)(2,1)S(1)}, u32[]{:S(2)}, u32[]{:S(2)}) %collective-permute-start) | collective-permute-done | bytes 262176 | tf_op jit(solution)/shard_map/while/body/eval_jaxpr/ppermute | solution.py:14
  300.3 7.3 %collective-permute-done = bf16[4,128,256]{2,1,0:T(8,128)(2,1)S(1)} collective-permute-done((bf16[4,128,256]{2,1,0:T(8,128)(2,1)S(1)}, bf16[4,128,256]{2,1,0:T(8,128)(2,1)S(1)}, u32[]{:S(2)}, u32[]{:S(2)}) %collective-permute-start) | collective-permute-done | bytes 262176 | tf_op jit(solution)/shard_map/while/body/eval_jaxpr/ppermute | solution.py:14
  313.0 7.3 %collective-permute-done = bf16[4,128,256]{2,1,0:T(8,128)(2,1)S(1)} collective-permute-done((bf16[4,128,256]{2,1,0:T(8,128)(2,1)S(1)}, bf16[4,128,256]{2,1,0:T(8,128)(2,1)S(1)}, u32[]{:S(2)}, u32[]{:S(2)}) %collective-permute-start) | collective-permute-done | bytes 262176 | tf_op jit(solution)/shard_map/while/body/eval_jaxpr/ppermute | solution.py:14
  364.2 7.3 %collective-permute-done = bf16[4,128,256]{2,1,0:T(8,128)(2,1)S(1)} collective-permute-done((bf16[4,128,256]{2,1,0:T(8,128)(2,1)S(1)}, bf16[4,128,256]{2,1,0:T(8,128)(2,1)S(1)}, u32[]{:S(2)}, u32[]{:S(2)}) %collective-permute-start) | collective-permute-done | bytes 262176 | tf_op jit(solution)/shard_map/while/body/eval_jaxpr/ppermute | solution.py:14
  377.0 8.4 %collective-permute-done = bf16[4,128,256]{2,1,0:T(8,128)(2,1)S(1)} collective-permute-done((bf16[4,128,256]{2,1,0:T(8,128)(2,1)S(1)}, bf16[4,128,256]{2,1,0:T(8,128)(2,1)S(1)}, u32[]{:S(2)}, u32[]{:S(2)}) %collective-permute-start) | collective-permute-done | bytes 262176 | tf_op jit(solution)/shard_map/while/body/eval_jaxpr/ppermute | solution.py:14
  390.9 9.6 %collective-permute-done = bf16[4,128,256]{2,1,0:T(8,128)(2,1)S(1)} collective-permute-done((bf16[4,128,256]{2,1,0:T(8,128)(2,1)S(1)}, bf16[4,128,256]{2,1,0:T(8,128)(2,1)S(1)}, u32[]{:S(2)}, u32[]{:S(2)}) %collective-permute-start) | collective-permute-done | bytes 262176 | tf_op jit(solution)/shard_map/while/body/eval_jaxpr/ppermute | solution.py:14
  406.0 9.4 %collective-permute-done = bf16[4,128,256]{2,1,0:T(8,128)(2,1)S(1)} collective-permute-done((bf16[4,128,256]{2,1,0:T(8,128)(2,1)S(1)}, bf16[4,128,256]{2,1,0:T(8,128)(2,1)S(1)}, u32[]{:S(2)}, u32[]{:S(2)}) %collective-permute-start) | collective-permute-done | bytes 262176 | tf_op jit(solution)/shard_map/while/body/eval_jaxpr/ppermute | solution.py:14
  420.9 8.6 %collective-permute-done = bf16[4,128,256]{2,1,0:T(8,128)(2,1)S(1)} collective-permute-done((bf16[4,128,256]{2,1,0:T(8,128)(2,1)S(1)}, bf16[4,128,256]{2,1,0:T(8,128)(2,1)S(1)}, u32[]{:S(2)}, u32[]{:S(2)}) %collective-permute-start) | collective-permute-done | bytes 262176 | tf_op jit(solution)/shard_map/while/body/eval_jaxpr/ppermute | solution.py:14
  435.0 7.7 %collective-permute-done = bf16[4,128,256]{2,1,0:T(8,128)(2,1)S(1)} collective-permute-done((bf16[4,128,256]{2,1,0:T(8,128)(2,1)S(1)}, bf16[4,128,256]{2,1,0:T(8,128)(2,1)S(1)}, u32[]{:S(2)}, u32[]{:S(2)}) %collective-permute-start) | collective-permute-done | bytes 262176 | tf_op jit(solution)/shard_map/while/body/eval_jaxpr/ppermute | solution.py:14
  (624 shorter events, 243.9 us)
Async XLA Ops:
  6.5 95.8 %all-gather.2.cloned.1.call-start = ((), (), s32[]{:S(2)}) async-start(), calls=%async_computation | async-start | bytes 8912896 | tf_op jit(solution)/shard_map/all_gather | solution.py:55
  105.2 13.5 %collective-permute-start = (bf16[4,128,256]{2,1,0:T(8,128)(2,1)S(1)}, bf16[4,128,256]{2,1,0:T(8,128)(2,1)S(1)}, u32[]{:S(2)}, u32[]{:S(2)}) collective-permute-start(bf16[4,128,256]{2,1,0:T(8,128)(2,1)S(1)} %get-tuple-element.477), channel_id=1, source_target_pairs={{0,1},{1,2},{2,3},{3,4},{4,5},{5,6},{6,7},{7,8},{8,9},{9,10},{10,1... | collective-permute-start | bytes 786440 | tf_op jit(solution)/shard_map/while/body/eval_jaxpr/ppermute | solution.py:14
  121.1 12.0 %collective-permute-start = (bf16[4,128,256]{2,1,0:T(8,128)(2,1)S(1)}, bf16[4,128,256]{2,1,0:T(8,128)(2,1)S(1)}, u32[]{:S(2)}, u32[]{:S(2)}) collective-permute-start(bf16[4,128,256]{2,1,0:T(8,128)(2,1)S(1)} %get-tuple-element.477), channel_id=1, source_target_pairs={{0,1},{1,2},{2,3},{3,4},{4,5},{5,6},{6,7},{7,8},{8,9},{9,10},{10,1... | collective-permute-start | bytes 786440 | tf_op jit(solution)/shard_map/while/body/eval_jaxpr/ppermute | solution.py:14
  135.5 11.1 %collective-permute-start = (bf16[4,128,256]{2,1,0:T(8,128)(2,1)S(1)}, bf16[4,128,256]{2,1,0:T(8,128)(2,1)S(1)}, u32[]{:S(2)}, u32[]{:S(2)}) collective-permute-start(bf16[4,128,256]{2,1,0:T(8,128)(2,1)S(1)} %get-tuple-element.477), channel_id=1, source_target_pairs={{0,1},{1,2},{2,3},{3,4},{4,5},{5,6},{6,7},{7,8},{8,9},{9,10},{10,1... | collective-permute-start | bytes 786440 | tf_op jit(solution)/shard_map/while/body/eval_jaxpr/ppermute | solution.py:14
  149.0 10.4 %collective-permute-start = (bf16[4,128,256]{2,1,0:T(8,128)(2,1)S(1)}, bf16[4,128,256]{2,1,0:T(8,128)(2,1)S(1)}, u32[]{:S(2)}, u32[]{:S(2)}) collective-permute-start(bf16[4,128,256]{2,1,0:T(8,128)(2,1)S(1)} %get-tuple-element.477), channel_id=1, source_target_pairs={{0,1},{1,2},{2,3},{3,4},{4,5},{5,6},{6,7},{7,8},{8,9},{9,10},{10,1... | collective-permute-start | bytes 786440 | tf_op jit(solution)/shard_map/while/body/eval_jaxpr/ppermute | solution.py:14
  161.8 10.4 %collective-permute-start = (bf16[4,128,256]{2,1,0:T(8,128)(2,1)S(1)}, bf16[4,128,256]{2,1,0:T(8,128)(2,1)S(1)}, u32[]{:S(2)}, u32[]{:S(2)}) collective-permute-start(bf16[4,128,256]{2,1,0:T(8,128)(2,1)S(1)} %get-tuple-element.477), channel_id=1, source_target_pairs={{0,1},{1,2},{2,3},{3,4},{4,5},{5,6},{6,7},{7,8},{8,9},{9,10},{10,1... | collective-permute-start | bytes 786440 | tf_op jit(solution)/shard_map/while/body/eval_jaxpr/ppermute | solution.py:14
  174.6 10.4 %collective-permute-start = (bf16[4,128,256]{2,1,0:T(8,128)(2,1)S(1)}, bf16[4,128,256]{2,1,0:T(8,128)(2,1)S(1)}, u32[]{:S(2)}, u32[]{:S(2)}) collective-permute-start(bf16[4,128,256]{2,1,0:T(8,128)(2,1)S(1)} %get-tuple-element.477), channel_id=1, source_target_pairs={{0,1},{1,2},{2,3},{3,4},{4,5},{5,6},{6,7},{7,8},{8,9},{9,10},{10,1... | collective-permute-start | bytes 786440 | tf_op jit(solution)/shard_map/while/body/eval_jaxpr/ppermute | solution.py:14
  187.4 10.4 %collective-permute-start = (bf16[4,128,256]{2,1,0:T(8,128)(2,1)S(1)}, bf16[4,128,256]{2,1,0:T(8,128)(2,1)S(1)}, u32[]{:S(2)}, u32[]{:S(2)}) collective-permute-start(bf16[4,128,256]{2,1,0:T(8,128)(2,1)S(1)} %get-tuple-element.477), channel_id=1, source_target_pairs={{0,1},{1,2},{2,3},{3,4},{4,5},{5,6},{6,7},{7,8},{8,9},{9,10},{10,1... | collective-permute-start | bytes 786440 | tf_op jit(solution)/shard_map/while/body/eval_jaxpr/ppermute | solution.py:14
  200.1 10.4 %collective-permute-start = (bf16[4,128,256]{2,1,0:T(8,128)(2,1)S(1)}, bf16[4,128,256]{2,1,0:T(8,128)(2,1)S(1)}, u32[]{:S(2)}, u32[]{:S(2)}) collective-permute-start(bf16[4,128,256]{2,1,0:T(8,128)(2,1)S(1)} %get-tuple-element.477), channel_id=1, source_target_pairs={{0,1},{1,2},{2,3},{3,4},{4,5},{5,6},{6,7},{7,8},{8,9},{9,10},{10,1... | collective-permute-start | bytes 786440 | tf_op jit(solution)/shard_map/while/body/eval_jaxpr/ppermute | solution.py:14
  212.9 10.4 %collective-permute-start = (bf16[4,128,256]{2,1,0:T(8,128)(2,1)S(1)}, bf16[4,128,256]{2,1,0:T(8,128)(2,1)S(1)}, u32[]{:S(2)}, u32[]{:S(2)}) collective-permute-start(bf16[4,128,256]{2,1,0:T(8,128)(2,1)S(1)} %get-tuple-element.477), channel_id=1, source_target_pairs={{0,1},{1,2},{2,3},{3,4},{4,5},{5,6},{6,7},{7,8},{8,9},{9,10},{10,1... | collective-permute-start | bytes 786440 | tf_op jit(solution)/shard_map/while/body/eval_jaxpr/ppermute | solution.py:14
  225.7 11.4 %collective-permute-start = (bf16[4,128,256]{2,1,0:T(8,128)(2,1)S(1)}, bf16[4,128,256]{2,1,0:T(8,128)(2,1)S(1)}, u32[]{:S(2)}, u32[]{:S(2)}) collective-permute-start(bf16[4,128,256]{2,1,0:T(8,128)(2,1)S(1)} %get-tuple-element.477), channel_id=1, source_target_pairs={{0,1},{1,2},{2,3},{3,4},{4,5},{5,6},{6,7},{7,8},{8,9},{9,10},{10,1... | collective-permute-start | bytes 786440 | tf_op jit(solution)/shard_map/while/body/eval_jaxpr/ppermute | solution.py:14
  239.5 12.6 %collective-permute-start = (bf16[4,128,256]{2,1,0:T(8,128)(2,1)S(1)}, bf16[4,128,256]{2,1,0:T(8,128)(2,1)S(1)}, u32[]{:S(2)}, u32[]{:S(2)}) collective-permute-start(bf16[4,128,256]{2,1,0:T(8,128)(2,1)S(1)} %get-tuple-element.477), channel_id=1, source_target_pairs={{0,1},{1,2},{2,3},{3,4},{4,5},{5,6},{6,7},{7,8},{8,9},{9,10},{10,1... | collective-permute-start | bytes 786440 | tf_op jit(solution)/shard_map/while/body/eval_jaxpr/ppermute | solution.py:14
  254.5 12.6 %collective-permute-start = (bf16[4,128,256]{2,1,0:T(8,128)(2,1)S(1)}, bf16[4,128,256]{2,1,0:T(8,128)(2,1)S(1)}, u32[]{:S(2)}, u32[]{:S(2)}) collective-permute-start(bf16[4,128,256]{2,1,0:T(8,128)(2,1)S(1)} %get-tuple-element.477), channel_id=1, source_target_pairs={{0,1},{1,2},{2,3},{3,4},{4,5},{5,6},{6,7},{7,8},{8,9},{9,10},{10,1... | collective-permute-start | bytes 786440 | tf_op jit(solution)/shard_map/while/body/eval_jaxpr/ppermute | solution.py:14
  269.5 11.9 %collective-permute-start = (bf16[4,128,256]{2,1,0:T(8,128)(2,1)S(1)}, bf16[4,128,256]{2,1,0:T(8,128)(2,1)S(1)}, u32[]{:S(2)}, u32[]{:S(2)}) collective-permute-start(bf16[4,128,256]{2,1,0:T(8,128)(2,1)S(1)} %get-tuple-element.477), channel_id=1, source_target_pairs={{0,1},{1,2},{2,3},{3,4},{4,5},{5,6},{6,7},{7,8},{8,9},{9,10},{10,1... | collective-permute-start | bytes 786440 | tf_op jit(solution)/shard_map/while/body/eval_jaxpr/ppermute | solution.py:14
  283.8 11.0 %collective-permute-start = (bf16[4,128,256]{2,1,0:T(8,128)(2,1)S(1)}, bf16[4,128,256]{2,1,0:T(8,128)(2,1)S(1)}, u32[]{:S(2)}, u32[]{:S(2)}) collective-permute-start(bf16[4,128,256]{2,1,0:T(8,128)(2,1)S(1)} %get-tuple-element.477), channel_id=1, source_target_pairs={{0,1},{1,2},{2,3},{3,4},{4,5},{5,6},{6,7},{7,8},{8,9},{9,10},{10,1... | collective-permute-start | bytes 786440 | tf_op jit(solution)/shard_map/while/body/eval_jaxpr/ppermute | solution.py:14
  297.2 10.4 %collective-permute-start = (bf16[4,128,256]{2,1,0:T(8,128)(2,1)S(1)}, bf16[4,128,256]{2,1,0:T(8,128)(2,1)S(1)}, u32[]{:S(2)}, u32[]{:S(2)}) collective-permute-start(bf16[4,128,256]{2,1,0:T(8,128)(2,1)S(1)} %get-tuple-element.477), channel_id=1, source_target_pairs={{0,1},{1,2},{2,3},{3,4},{4,5},{5,6},{6,7},{7,8},{8,9},{9,10},{10,1... | collective-permute-start | bytes 786440 | tf_op jit(solution)/shard_map/while/body/eval_jaxpr/ppermute | solution.py:14
  310.0 10.4 %collective-permute-start = (bf16[4,128,256]{2,1,0:T(8,128)(2,1)S(1)}, bf16[4,128,256]{2,1,0:T(8,128)(2,1)S(1)}, u32[]{:S(2)}, u32[]{:S(2)}) collective-permute-start(bf16[4,128,256]{2,1,0:T(8,128)(2,1)S(1)} %get-tuple-element.477), channel_id=1, source_target_pairs={{0,1},{1,2},{2,3},{3,4},{4,5},{5,6},{6,7},{7,8},{8,9},{9,10},{10,1... | collective-permute-start | bytes 786440 | tf_op jit(solution)/shard_map/while/body/eval_jaxpr/ppermute | solution.py:14
  361.1 10.4 %collective-permute-start = (bf16[4,128,256]{2,1,0:T(8,128)(2,1)S(1)}, bf16[4,128,256]{2,1,0:T(8,128)(2,1)S(1)}, u32[]{:S(2)}, u32[]{:S(2)}) collective-permute-start(bf16[4,128,256]{2,1,0:T(8,128)(2,1)S(1)} %get-tuple-element.477), channel_id=1, source_target_pairs={{0,1},{1,2},{2,3},{3,4},{4,5},{5,6},{6,7},{7,8},{8,9},{9,10},{10,1... | collective-permute-start | bytes 786440 | tf_op jit(solution)/shard_map/while/body/eval_jaxpr/ppermute | solution.py:14
  373.9 11.5 %collective-permute-start = (bf16[4,128,256]{2,1,0:T(8,128)(2,1)S(1)}, bf16[4,128,256]{2,1,0:T(8,128)(2,1)S(1)}, u32[]{:S(2)}, u32[]{:S(2)}) collective-permute-start(bf16[4,128,256]{2,1,0:T(8,128)(2,1)S(1)} %get-tuple-element.477), channel_id=1, source_target_pairs={{0,1},{1,2},{2,3},{3,4},{4,5},{5,6},{6,7},{7,8},{8,9},{9,10},{10,1... | collective-permute-start | bytes 786440 | tf_op jit(solution)/shard_map/while/body/eval_jaxpr/ppermute | solution.py:14
  387.8 12.7 %collective-permute-start = (bf16[4,128,256]{2,1,0:T(8,128)(2,1)S(1)}, bf16[4,128,256]{2,1,0:T(8,128)(2,1)S(1)}, u32[]{:S(2)}, u32[]{:S(2)}) collective-permute-start(bf16[4,128,256]{2,1,0:T(8,128)(2,1)S(1)} %get-tuple-element.477), channel_id=1, source_target_pairs={{0,1},{1,2},{2,3},{3,4},{4,5},{5,6},{6,7},{7,8},{8,9},{9,10},{10,1... | collective-permute-start | bytes 786440 | tf_op jit(solution)/shard_map/while/body/eval_jaxpr/ppermute | solution.py:14
  402.9 12.5 %collective-permute-start = (bf16[4,128,256]{2,1,0:T(8,128)(2,1)S(1)}, bf16[4,128,256]{2,1,0:T(8,128)(2,1)S(1)}, u32[]{:S(2)}, u32[]{:S(2)}) collective-permute-start(bf16[4,128,256]{2,1,0:T(8,128)(2,1)S(1)} %get-tuple-element.477), channel_id=1, source_target_pairs={{0,1},{1,2},{2,3},{3,4},{4,5},{5,6},{6,7},{7,8},{8,9},{9,10},{10,1... | collective-permute-start | bytes 786440 | tf_op jit(solution)/shard_map/while/body/eval_jaxpr/ppermute | solution.py:14
  417.8 11.7 %collective-permute-start = (bf16[4,128,256]{2,1,0:T(8,128)(2,1)S(1)}, bf16[4,128,256]{2,1,0:T(8,128)(2,1)S(1)}, u32[]{:S(2)}, u32[]{:S(2)}) collective-permute-start(bf16[4,128,256]{2,1,0:T(8,128)(2,1)S(1)} %get-tuple-element.477), channel_id=1, source_target_pairs={{0,1},{1,2},{2,3},{3,4},{4,5},{5,6},{6,7},{7,8},{8,9},{9,10},{10,1... | collective-permute-start | bytes 786440 | tf_op jit(solution)/shard_map/while/body/eval_jaxpr/ppermute | solution.py:14
  432.0 10.8 %collective-permute-start = (bf16[4,128,256]{2,1,0:T(8,128)(2,1)S(1)}, bf16[4,128,256]{2,1,0:T(8,128)(2,1)S(1)}, u32[]{:S(2)}, u32[]{:S(2)}) collective-permute-start(bf16[4,128,256]{2,1,0:T(8,128)(2,1)S(1)} %get-tuple-element.477), channel_id=1, source_target_pairs={{0,1},{1,2},{2,3},{3,4},{4,5},{5,6},{6,7},{7,8},{8,9},{9,10},{10,1... | collective-permute-start | bytes 786440 | tf_op jit(solution)/shard_map/while/body/eval_jaxpr/ppermute | solution.py:14
  445.2 10.4 %collective-permute-start = (bf16[4,128,256]{2,1,0:T(8,128)(2,1)S(1)}, bf16[4,128,256]{2,1,0:T(8,128)(2,1)S(1)}, u32[]{:S(2)}, u32[]{:S(2)}) collective-permute-start(bf16[4,128,256]{2,1,0:T(8,128)(2,1)S(1)} %get-tuple-element.477), channel_id=1, source_target_pairs={{0,1},{1,2},{2,3},{3,4},{4,5},{5,6},{6,7},{7,8},{8,9},{9,10},{10,1... | collective-permute-start | bytes 786440 | tf_op jit(solution)/shard_map/while/body/eval_jaxpr/ppermute | solution.py:14
  (19 other events, 110.4 us)
Sparse Core Ops, SparseCore 0:
  10.7 91.6 all-gather.1
where the time goes:
time: 533 us; the launch traced here: 531 us
  waiting for transfers between devices  334 us (63%)
  starting transfers between devices  61.1 us (11%)
  other arithmetic  51.4 us (10%)
  matrix products  48.6 us (9%)
  local copies, waits for them, and re-layouts  17.2 us (3%)
  between operations  13.7 us (3%)
    ppermute x31, waiting for transfers between devices, from_behind(): return lax.ppermute(value, axis, pairs)  245 us
    all_gather x1, waiting for transfers between devices, on_device(): full_bias = lax.all_gather(coupling_logit_offset, 'seq', axis=2, tiled=True)  89.3 us
    ppermute x31, starting transfers between devices, from_behind(): return lax.ppermute(value, axis, pairs)  61.1 us
    convert_element_type x32, other arithmetic, update(): lax.dynamic_slice_in_dim(full_bias, first, span_len, 2).astype(jnp.float32)  31.8 us
    dot_general x32, matrix products, update(): jnp.einsum('sihd,sjhd->shij', queries, key_four, preferred_element_type=j...  18.7 us
    dot_general x32, matrix products, update(): jnp.einsum('shij,sjhd->shid', weights_exp.astype(jnp.bfloat16), value_fou...  14.3 us
    reduce_sum x32, other arithmetic, update(): totals = totals * rescale + jnp.sum(weights_exp, axis=-1)  12.8 us
  transfers between devices with their start and end apart: 32, of which 32 were waited for; matrix products, arithmetic and copies ran while one was open for 7% of the time, Pallas kernels for 0%

commit v1 on v0

v1 whole, which is shorter than its diff:
```python
import jax
import jax.numpy as jnp
import numpy as np
from jax import lax
from jax.experimental import pallas as pl
from jax.experimental.pallas import tpu as pltpu
from jax.sharding import PartitionSpec as P

H = 8
DH = 32
BLOCK = 128
PAIRS = H // 2
VROWS = 2 * DH + 16
LOG2E = 1.4426950408889634
LOW = -1e30

SEQ, RES, NZ = 16, 32, 16
Z_GROUPS = [[yl * NZ + z for z in range(NZ)] for yl in range(2)]
YL_PAIRS = [(r, (r + NZ) % RES) for r in range(RES)]
C_PAIRS = [(s, s ^ 1) for s in range(SEQ)]


def bias_pairs(u, v):
    pairs = []
    for x in range(4):
        for yh in range(2):
            for c in range(2):
                for yl in range(2):
                    for z in range(NZ):
                        to_x, to_yh, to_yl = (x + 2 * yl + u) % 4, yh ^ v, x // 2
                        source = (x * 4 + yh * 2 + c) * RES + yl * NZ + z
                        target = (to_x * 4 + to_yh * 2 + c) * RES + to_yl * NZ + z
                        pairs.append((source, target))
    return pairs


def standardize_features(source, standard_scale_array, standard_offset_array):
    values_f = source.astype(jnp.float32)
    center = jnp.mean(values_f, axis=-1, keepdims=True)
    spread = jnp.mean((values_f - center) ** 2, axis=-1, keepdims=True)
    return (values_f - center) * lax.rsqrt(
        spread + 1e-05
    ) * standard_scale_array + standard_offset_array


def project_kernel(rows_ref, key_w_ref, value_wt_ref, key_ref, value_ref):
    depth, span, width = rows_ref.shape[1:]
    rows = rows_ref[0].reshape(depth * span, width)
    key_ref[0] = (
        jnp.dot(rows, key_w_ref[...], preferred_element_type=jnp.float32)
        .astype(jnp.bfloat16)
        .reshape(depth, span, width)
    )
    values = lax.dot_general(
        value_wt_ref[...], rows, (((1,), (1,)), ((), ())), preferred_element_type=jnp.float32
    ).astype(jnp.bfloat16)
    ones = jnp.ones((VROWS - 2 * DH, span), jnp.bfloat16)
    for s in range(depth):
        for p in range(PAIRS):
            value_ref[0, s, p, : 2 * DH] = values[
                p * 2 * DH : (p + 1) * 2 * DH, s * span : (s + 1) * span
            ]
            value_ref[0, s, p, 2 * DH :] = ones


def project(gathered, key_w, value_wt):
    blocks, depth, span, width = gathered.shape
    return pl.pallas_call(
        project_kernel,
        grid=(blocks,),
        in_specs=[
            pl.BlockSpec((1, depth, span, width), lambda b: (b, 0, 0, 0)),
            pl.BlockSpec((width, width), lambda b: (0, 0)),
            pl.BlockSpec((width, width), lambda b: (0, 0)),
        ],
        out_specs=[
            pl.BlockSpec((1, depth, span, width), lambda b: (b, 0, 0, 0)),
            pl.BlockSpec((1, depth, PAIRS, VROWS, span), lambda b: (b, 0, 0, 0, 0)),
        ],
        out_shape=[
            jax.ShapeDtypeStruct((blocks, depth, span, width), jnp.bfloat16),
            jax.ShapeDtypeStruct((blocks, depth, PAIRS, VROWS, span), jnp.bfloat16),
        ],
        name="project",
    )(gathered, key_w, value_wt)


def attend_kernel(
    table_ref, key_ref, value_ref, query_ref, near_ref, far_ref, out_ref, lse_ref, top_ref, acc_ref
):
    depth = key_ref.shape[1]
    live = table_ref[3, 0]
    top_ref[...] = jnp.full_like(top_ref, LOW)
    acc_ref[...] = jnp.zeros_like(acc_ref)

    def bias_of(place):
        is_far = table_ref[1, place]
        turn = table_ref[2, place]
        row = pl.multiple_of(lax.rem(table_ref[0, place], 2) * BLOCK, BLOCK)
        near = near_ref[turn, 0, pl.ds(row, BLOCK), :].astype(jnp.float32)
        far = far_ref[turn, 0, pl.ds(row, BLOCK), :].astype(jnp.float32)
        return jnp.where(is_far > 0, far, near) * LOG2E

    def step(t, carry):
        place0, place1 = 2 * t, 2 * t + 1
        z0, z1 = table_ref[0, place0], table_ref[0, place1]
        absent = jnp.where(place1 < live, 0.0, -LOW)
        bias0, bias1 = bias_of(place0), bias_of(place1)
        for s in range(depth):
            query = query_ref[s, 0]
            score0 = jnp.dot(key_ref[z0, s], query, preferred_element_type=jnp.float32) + bias0
            score1 = jnp.dot(key_ref[z1, s], query, preferred_element_type=jnp.float32) + bias1
            old = top_ref[s]
            top = jnp.maximum(
                jnp.max(score0, axis=0, keepdims=True),
                jnp.max(score1, axis=0, keepdims=True) - absent,
            )
            top = jnp.maximum(old, top)
            top_ref[s] = top
            weight = jnp.concatenate(
                [
                    jnp.exp2(score0 - top).astype(jnp.bfloat16),
                    jnp.exp2(score1 - (top + absent)).astype(jnp.bfloat16),
                ],
                axis=0,
            )
            value = jnp.concatenate([value_ref[z0, s, 0], value_ref[z1, s, 0]], axis=1)
            acc_ref[s] = acc_ref[s] * jnp.exp2(old - top) + jnp.dot(
                value, weight, preferred_element_type=jnp.float32
            )
        return carry

    lax.fori_loop(0, (live + 1) // 2, step, 0)
    for s in range(depth):
        acc = acc_ref[s]
        total = acc[2 * DH : 2 * DH + 1]
        some = total > 0.0
        safe = jnp.where(some, total, 1.0)
        mean = acc[: 2 * DH] / safe
        lse = jnp.where(some, top_ref[s] + jnp.log2(safe), LOW)
        for e in range(2):
            lanes = slice(e * BLOCK, (e + 1) * BLOCK)
            out_ref[s, e * DH : (e + 1) * DH] = mean[e * DH : (e + 1) * DH, lanes].astype(
                out_ref.dtype
            )
            lse_ref[s, 0, e : e + 1] = lse[:, lanes]


def attend(table, keys, values, queries, near, far, out_type):
    blocks, depth, span, width = keys.shape
    turns = near.shape[0]
    return pl.pallas_call(
        attend_kernel,
        grid=(PAIRS,),
        in_specs=[
            pl.BlockSpec(memory_space=pltpu.SMEM),
            pl.BlockSpec((blocks, depth, span, 128), lambda p: (0, 0, 0, p // 2)),
            pl.BlockSpec((blocks, depth, 1, VROWS, span), lambda p: (0, 0, p, 0, 0)),
            pl.BlockSpec((depth, 1, 128, 256), lambda p: (0, p, 0, 0)),
            pl.BlockSpec((turns, 1, 256, 256), lambda p: (0, p, 0, 0)),
            pl.BlockSpec((turns, 1, 256, 256), lambda p: (0, p, 0, 0)),
        ],
        out_specs=[
            pl.BlockSpec((depth, 2 * DH, BLOCK), lambda p: (0, p, 0)),
            pl.BlockSpec((depth, 1, 2, BLOCK), lambda p: (0, p, 0, 0)),
        ],
        out_shape=[
            jax.ShapeDtypeStruct((depth, width, BLOCK), out_type),
            jax.ShapeDtypeStruct((depth, PAIRS, 2, BLOCK), jnp.float32),
        ],
        scratch_shapes=[
            pltpu.VMEM((depth, 1, 256), jnp.float32),
            pltpu.VMEM((depth, VROWS, 256), jnp.float32),
        ],
        compiler_params=pltpu.CompilerParams(vmem_limit_bytes=48 * 1024 * 1024),
        name="attend",
    )(table, keys, values, queries, near, far)


def finish_kernel(
    own_ref, own_lse_ref, got_ref, got_lse_ref, rows_ref, gate_wt_ref, gate_off_ref, out_w_ref,
    out_off_ref, out_ref,
):
    width, span = own_ref.shape[1:]
    own_lse, got_lse = own_lse_ref[0], got_lse_ref[0]
    own_part = 1.0 / (1.0 + jnp.exp2(got_lse - own_lse))
    got_part = 1.0 / (1.0 + jnp.exp2(own_lse - got_lse))

    def spread(part):
        return jnp.broadcast_to(part[:, None, :], (H, DH, span)).reshape(width, span)

    attended = own_ref[0] * spread(own_part) + got_ref[0].astype(jnp.float32) * spread(got_part)
    gate = jax.nn.sigmoid(
        lax.dot_general(
            gate_wt_ref[...], rows_ref[0], (((1,), (1,)), ((), ())),
            preferred_element_type=jnp.float32,
        )
        + gate_off_ref[...]
    )
    gated = (gate * attended).T.astype(jnp.bfloat16)
    result = jnp.dot(gated, out_w_ref[...], preferred_element_type=jnp.float32)
    out_ref[0] = (result + out_off_ref[...]).astype(jnp.bfloat16)


def finish(own, own_lse, got, got_lse, rows, gate_wt, gate_off, out_w, out_off):
    depth, width, span = own.shape
    whole = lambda s: (0, 0)
    part = lambda s: (s, 0, 0)
    return pl.pallas_call(
        finish_kernel,
        grid=(depth,),
        in_specs=[
            pl.BlockSpec((1, width, span), part),
            pl.BlockSpec((1, H, span), part),
            pl.BlockSpec((1, width, span), part),
            pl.BlockSpec((1, H, span), part),
            pl.BlockSpec((1, span, width), part),
            pl.BlockSpec((width, width), whole),
            pl.BlockSpec((width, 1), whole),
            pl.BlockSpec((width, width), whole),
            pl.BlockSpec((1, width), whole),
        ],
        out_specs=pl.BlockSpec((1, span, width), part),
        out_shape=jax.ShapeDtypeStruct((depth, span, width), jnp.bfloat16),
        name="finish",
    )(own, own_lse, got, got_lse, rows, gate_wt, gate_off, out_w, out_off)


def on_device(
    alignment_features,
    coupling_logit_offset,
    contact_tile_filter,
    standard_scale_array,
    standard_offset_array,
    probe_projection,
    lookup_projection,
    content_projection,
    sigmoid_projection,
    sigmoid_offset_array,
    result_projection,
    result_offset,
):
    depth, span, width = alignment_features.shape
    seq, res = lax.axis_index("seq"), lax.axis_index("res")
    x, yh, c = seq // 4, (seq // 2) % 2, seq % 2
    half, z_own = res // NZ, res % NZ

    normed = standardize_features(
        alignment_features, standard_scale_array, standard_offset_array
    ).astype(jnp.bfloat16)
    gathered = lax.all_gather(normed, "res", axis_index_groups=Z_GROUPS)
    partner = lax.ppermute(normed, "res", YL_PAIRS)

    turned = (
        coupling_logit_offset.reshape(PAIRS, 2, span, 2 * BLOCK)
        .transpose(0, 3, 1, 2)
        .reshape(PAIRS, 2 * BLOCK, 2 * span)
    )
    near = jnp.stack(
        [lax.ppermute(turned, ("seq", "res"), bias_pairs(u, v)) for u in range(4) for v in range(2)]
    )
    far = lax.ppermute(near, "seq", C_PAIRS)

    head_of = np.arange(128) // DH
    wanted = np.array([[(2 * p + e) % 4 for e in range(2)] for p in range(PAIRS)])
    spot = jnp.asarray(head_of[None, :, None] == wanted[:, None, :], jnp.bfloat16)

    def query_tiles(rows):
        queries = (
            jnp.dot(rows.reshape(-1, width), probe_projection, preferred_element_type=jnp.float32)
            * (LOG2E / DH**0.5)
        ).astype(jnp.bfloat16)
        turned_q = queries.reshape(depth, span, 2, 128).transpose(0, 2, 3, 1)
        twice = jnp.repeat(turned_q, 2, axis=1)
        tiles = twice[:, :, :, None, :] * spot[None, :, :, :, None]
        return tiles.reshape(depth, PAIRS, 128, 2 * span)

    places = jnp.arange(NZ, dtype=jnp.int32)

    def live_table(yl):
        line = yl * NZ + z_own
        chosen = (jnp.arange(RES, dtype=jnp.int32) == line).astype(jnp.int32)
        mask_line = jnp.sum(contact_tile_filter * chosen[:, None], axis=0).reshape(2, NZ)
        live = jnp.where(half > 0, mask_line[1], mask_line[0])
        before = jnp.sum(jnp.where(places[None, :] <= places[:, None], live[None, :], 0), axis=1) - 1
        hit = (before[:, None] == places[None, :]) & (live[:, None] > 0)
        z = jnp.sum(jnp.where(hit, places[:, None], 0), axis=0)
        slot = z // 8 + 2 * yl
        turn = ((x - 2 * half - slot) % 4) * 2 + (((z // 4) % 2) ^ yh)
        is_far = ((z // 2) % 2) ^ c
        return jnp.stack([z, is_far, turn, jnp.full((NZ,), jnp.sum(live))]).astype(jnp.int32)

    keys, values = project(gathered, lookup_projection, content_projection.T)
    sent, sent_lse = attend(
        live_table(1 - half), keys, values, query_tiles(partner), near, far, jnp.bfloat16
    )
    got = lax.ppermute(sent, "res", YL_PAIRS)
    got_lse = lax.ppermute(sent_lse, "res", YL_PAIRS)
    own, own_lse = attend(
        live_table(half), keys, values, query_tiles(normed), near, far, jnp.float32
    )
    return finish(
        own,
        own_lse.reshape(depth, H, span),
        got,
        got_lse.reshape(depth, H, span),
        normed,
        sigmoid_projection.T,
        sigmoid_offset_array[:, None],
        result_projection,
        result_offset[None, :],
    )


def solution(mesh):
    return jax.shard_map(
        on_device,
        mesh=mesh,
        in_specs=(
            P("seq", "res", None),
            P(None, "res", "seq"),
            P(),
            P(),
            P(),
            P(),
            P(),
            P(),
            P(),
            P(),
            P(),
            P(),
        ),
        out_specs=P("seq", "res", None),
        check_vma=False,
    )
```

time: 533 us -> 226 us (0.42)
  the two profiles are of different devices: /device:TPU:8 before, /device:TPU:388 now
where the time goes in v1:
time: 226 us; the launch traced here: 225 us
  starting transfers between devices  70.9 us (31%)
  Pallas kernels  66.6 us (29%)
  waiting for transfers between devices  41.1 us (18%)
  local copies, waits for them, and re-layouts  24.6 us (11%)
  between operations  13.8 us (6%)
  other arithmetic  7.17 us (3%)
    pallas_call x2, Pallas kernels, attend(): pl.pallas_call(attend_kernel, grid=(PAIRS,), in_specs=[pl.BlockSpec(memor...  49.1 us
    ppermute x8, waiting for transfers between devices, on_device(): lax.ppermute(turned, ('seq', 'res'), bias_pairs(u, v))  40.6 us
    ppermute x1, starting transfers between devices, on_device(): got = lax.ppermute(sent, 'res', YL_PAIRS)  29.3 us
    ppermute x8, starting transfers between devices, on_device(): lax.ppermute(turned, ('seq', 'res'), bias_pairs(u, v))  28.6 us
    unnamed x35, local copies, waits for them, and re-layouts  13.9 us
    pallas_call x1, Pallas kernels, project(): pl.pallas_call(project_kernel, grid=(blocks,), in_specs=[pl.BlockSpec((1,...  13.2 us
    ppermute x1, starting transfers between devices, on_device(): partner = lax.ppermute(normed, 'res', YL_PAIRS)  9.24 us
    mul x6, local copies, waits for them, and re-layouts, query_tiles(): tiles = twice[:, :, :, None, :] * spot[None, :, :, :, None]  5.4 us
  transfers between devices with their start and end apart: 13, of which 5 were waited for; matrix products, arithmetic and copies ran while one was open for 10% of the time, Pallas kernels for 23%

profile of v1, /device:TPU:388, one launch (start us, length us, event | category | flops | bytes accessed | tf_op | source)
XLA Modules:
  0.0 224.6 jit_solution(12157309606222540848)
XLA Ops:
  8.9 1.9 fusion.7.rows_ref
  12.5 3.6 %collective-permute-start = (bf16[4,256,256]{2,1,0:T(8,128)(2,1)S(1)}, bf16[4,256,256]{2,1,0:T(8,128)(2,1)S(1)}, u32[]{:S(2)}, u32[]{:S(2)}) collective-permute-start(bf16[4,256,256]{2,1,0:T(8,128)(2,1)S(1)} %reshape.556), channel_id=1, source_target_pairs={{0,0},{1,1},{2,2},{3,3},{4,4},{5,5},{6,6},{7,7},{8,8},{9,9},{10,10... | collective-permute-start | bytes 1572872 | tf_op jit(solution)/shard_map/ppermute | solution.py:260
  16.1 3.9 %collective-permute-start.1 = (bf16[4,256,256]{2,1,0:T(8,128)(2,1)S(1)}, bf16[4,256,256]{2,1,0:T(8,128)(2,1)S(1)}, u32[]{:S(2)}, u32[]{:S(2)}) collective-permute-start(bf16[4,256,256]{2,1,0:T(8,128)(2,1)S(1)} %reshape.556), channel_id=1, source_target_pairs={{0,64},{1,65},{2,66},{3,67},{4,68},{5,69},{6,70},{7,71},{8,72},{9,... | collective-permute-start | bytes 1572872 | tf_op jit(solution)/shard_map/ppermute | solution.py:260
  20.0 6.0 %collective-permute-start.2 = (bf16[4,256,256]{2,1,0:T(8,128)(2,1)S(1)}, bf16[4,256,256]{2,1,0:T(8,128)(2,1)S(1)}, u32[]{:S(2)}, u32[]{:S(2)}) collective-permute-start(bf16[4,256,256]{2,1,0:T(8,128)(2,1)S(1)} %reshape.556), channel_id=1, source_target_pairs={{0,128},{1,129},{2,130},{3,131},{4,132},{5,133},{6,134},{7,135},{8... | collective-permute-start | bytes 1572872 | tf_op jit(solution)/shard_map/ppermute | solution.py:260
  26.0 2.8 %collective-permute-start.3 = (bf16[4,256,256]{2,1,0:T(8,128)(2,1)S(1)}, bf16[4,256,256]{2,1,0:T(8,128)(2,1)S(1)}, u32[]{:S(2)}, u32[]{:S(2)}) collective-permute-start(bf16[4,256,256]{2,1,0:T(8,128)(2,1)S(1)} %reshape.556), channel_id=1, source_target_pairs={{0,192},{1,193},{2,194},{3,195},{4,196},{5,197},{6,198},{7,199},{8... | collective-permute-start | bytes 1572872 | tf_op jit(solution)/shard_map/ppermute | solution.py:260
  28.9 4.1 %collective-permute-start.4 = (bf16[4,256,256]{2,1,0:T(8,128)(2,1)S(1)}, bf16[4,256,256]{2,1,0:T(8,128)(2,1)S(1)}, u32[]{:S(2)}, u32[]{:S(2)}) collective-permute-start(bf16[4,256,256]{2,1,0:T(8,128)(2,1)S(1)} %reshape.556), channel_id=1, source_target_pairs={{0,256},{1,257},{2,258},{3,259},{4,260},{5,261},{6,262},{7,263},{8... | collective-permute-start | bytes 1572872 | tf_op jit(solution)/shard_map/ppermute | solution.py:260
  33.0 3.4 %collective-permute-start.5 = (bf16[4,256,256]{2,1,0:T(8,128)(2,1)S(1)}, bf16[4,256,256]{2,1,0:T(8,128)(2,1)S(1)}, u32[]{:S(2)}, u32[]{:S(2)}) collective-permute-start(bf16[4,256,256]{2,1,0:T(8,128)(2,1)S(1)} %reshape.556), channel_id=1, source_target_pairs={{0,320},{1,321},{2,322},{3,323},{4,324},{5,325},{6,326},{7,327},{8... | collective-permute-start | bytes 1572872 | tf_op jit(solution)/shard_map/ppermute | solution.py:260
  37.2 14.9 %collective-permute-done.1 = bf16[4,256,256]{2,1,0:T(8,128)(2,1)S(1)} collective-permute-done((bf16[4,256,256]{2,1,0:T(8,128)(2,1)S(1)}, bf16[4,256,256]{2,1,0:T(8,128)(2,1)S(1)}, u32[]{:S(2)}, u32[]{:S(2)}) %collective-permute-start.1) | collective-permute-done | bytes 524320 | tf_op jit(solution)/shard_map/ppermute | solution.py:260
  52.0 1.9 collective-permute-start.6
  54.8 2.9 %collective-permute-start.7 = (bf16[4,256,256]{2,1,0:T(8,128)(2,1)S(1)}, bf16[4,256,256]{2,1,0:T(8,128)(2,1)S(1)}, u32[]{:S(2)}, u32[]{:S(2)}) collective-permute-start(bf16[4,256,256]{2,1,0:T(8,128)(2,1)S(1)} %reshape.556), channel_id=1, source_target_pairs={{0,448},{1,449},{2,450},{3,451},{4,452},{5,453},{6,454},{7,455},{8... | collective-permute-start | bytes 1572872 | tf_op jit(solution)/shard_map/ppermute | solution.py:260
  58.5 10.4 %collective-permute-done.3 = bf16[4,256,256]{2,1,0:T(8,128)(2,1)S(1)} collective-permute-done((bf16[4,256,256]{2,1,0:T(8,128)(2,1)S(1)}, bf16[4,256,256]{2,1,0:T(8,128)(2,1)S(1)}, u32[]{:S(2)}, u32[]{:S(2)}) %collective-permute-start.3) | collective-permute-done | bytes 524320 | tf_op jit(solution)/shard_map/ppermute | solution.py:260
  70.6 14.3 %collective-permute-done.5 = bf16[4,256,256]{2,1,0:T(8,128)(2,1)S(1)} collective-permute-done((bf16[4,256,256]{2,1,0:T(8,128)(2,1)S(1)}, bf16[4,256,256]{2,1,0:T(8,128)(2,1)S(1)}, u32[]{:S(2)}, u32[]{:S(2)}) %collective-permute-start.5) | collective-permute-done | bytes 524320 | tf_op jit(solution)/shard_map/ppermute | solution.py:260
  88.4 1.9 collective-permute-start.8
  90.4 9.2 %collective-permute-start.9 = (bf16[4,128,256]{2,1,0:T(8,128)(2,1)S(1)}, bf16[4,128,256]{2,1,0:T(8,128)(2,1)S(1)}, u32[]{:S(2)}, u32[]{:S(2)}) collective-permute-start(bf16[4,128,256]{2,1,0:T(8,128)(2,1)S(1)} %copy-done.5), channel_id=1, source_target_pairs={{0,16},{1,17},{2,18},{3,19},{4,20},{5,21},{6,22},{7,23},{8,24},{9,... | collective-permute-start | bytes 786440 | tf_op jit(solution)/shard_map/ppermute | solution.py:252
  108.0 1.5 mul.135
  109.5 1.5 broadcast_multiply_fusion
  111.0 13.2 %project.1 = (bf16[16,4,128,256]{3,2,1,0:T(8,128)(2,1)}, bf16[16,4,4,80,128]{4,3,2,1,0:T(8,128)(2,1)}) custom-call(bf16[16,4,128,256]{3,2,1,0:T(8,128)(2,1)} %bitcast.44, bf16[256,256]{1,0:T(8,128)(2,1)} %key_w_ref.1, bf16[256,256]{1,0:T(8,128)(2,1)} %bitcast.51), custom_call_target="tpu_custom_call" | custom-call | tf_op jit(solution)/shard_map/project/pallas_call | solution.py:68
  124.2 2.2 copy-done.1
  126.4 11.7 %attend.3 = (bf16[4,256,128]{2,1,0:T(8,128)(2,1)S(1)}, f32[4,4,2,128]{3,2,1,0:T(2,128)S(1)}) custom-call(s32[4,16]{1,0:T(4,128)S(1)} %add_add_fusion.1.table_ref, bf16[16,4,128,256]{3,2,1,0:T(8,128)(2,1)S(1)} %copy-done.1, bf16[16,4,4,80,128]{4,3,2,1,0:T(8,128)(2,1)} %get-tuple-element.12.value_ref, ...), custom_call_target="tpu_custom_call" | custom-call | tf_op jit(solution)/shard_map/attend/pallas_call | solution.py:152
  138.2 29.3 %collective-permute-start.10 = (bf16[4,256,128]{2,1,0:T(8,128)(2,1)S(1)}, bf16[4,256,128]{2,1,0:T(8,128)(2,1)S(1)}, u32[]{:S(2)}, u32[]{:S(2)}) collective-permute-start(bf16[4,256,128]{2,1,0:T(8,128)(2,1)S(1)} %get-tuple-element.15), channel_id=1, source_target_pairs={{0,16},{1,17},{2,18},{3,19},{4,20},{5,21},{6,22},{7,23},{8,24},{9,... | collective-permute-start | bytes 786440 | tf_op jit(solution)/shard_map/ppermute | solution.py:297
  168.2 1.9 collective-permute-start.11
  171.8 2.2 copy-done.2
  174.0 37.4 %attend.2 = (f32[4,256,128]{2,1,0:T(8,128)S(1)}, f32[4,4,2,128]{3,2,1,0:T(2,128)S(1)}) custom-call(s32[4,16]{1,0:T(4,128)S(1)} %add_add_fusion.table_ref, bf16[16,4,128,256]{3,2,1,0:T(8,128)(2,1)S(1)} %copy-done.2, bf16[16,4,4,80,128]{4,3,2,1,0:T(8,128)(2,1)} %get-tuple-element.12.value_ref, bf16[4,4,128,256]{3,2,1,0:T(8,128)(2,1)S(1)} %get-tuple-element.24.query_ref, ...), custom_call_target="tpu_custom_call" | custom-call | tf_op jit(solution)/shard_map/attend/pallas_call | solution.py:152
  213.5 4.3 %finish.1 = bf16[4,128,256]{2,1,0:T(8,128)(2,1)} custom-call(f32[4,256,128]{2,1,0:T(8,128)} %copy-done.3, f32[4,8,128]{2,1,0:T(8,128)} %bitcast.43, bf16[4,256,128]{2,1,0:T(8,128)(2,1)} %copy-done.6, f32[4,8,128]{2,1,0:T(8,128)} %bitcast.55, bf16[4,128,256]{2,1,0:T(8,128)(2,1)} %fusion.7.rows_ref, bf16[256,256]{1,0:T(8,128)(2,1)} %bitcast.52, ...), custom_call_target="tpu_custom_call" | custom-call | tf_op jit(solution)/shard_map/finish/pallas_call | solution.py:209
  (84 shorter events, 24.4 us)
Async XLA Ops:
  6.5 94.4 %copy-start = (bf16[256,256]{1,0:T(8,128)(2,1)S(1)}, bf16[256,256]{1,0:T(8,128)(2,1)}, u32[]{:S(2)}) copy-start(bf16[256,256]{1,0:T(8,128)(2,1)} %param.18) | copy-start | bytes 393220
  6.5 104.5 %all-gather.3.cloned.1.call-start = ((), (), s32[]{:S(2)}) async-start(), calls=%async_computation | async-start | bytes 4456448 | tf_op jit(solution)/shard_map/all_gather | solution.py:251
  12.5 77.9 %copy-start.5 = (bf16[4,128,256]{2,1,0:T(8,128)(2,1)S(1)}, bf16[4,128,256]{2,1,0:T(8,128)(2,1)}, u32[]{:S(2)}) copy-start(bf16[4,128,256]{2,1,0:T(8,128)(2,1)} %fusion.7.rows_ref) | copy-start | bytes 786436
  12.5 87.2 %copy-start.11 = (s32[32,32]{1,0:T(8,128)S(1)}, s32[32,32]{1,0:T(8,128)}, u32[]{:S(2)}) copy-start(s32[32,32]{1,0:T(8,128)} %param.15) | copy-start | bytes 12292
  12.5 20.5 %collective-permute-start = (bf16[4,256,256]{2,1,0:T(8,128)(2,1)S(1)}, bf16[4,256,256]{2,1,0:T(8,128)(2,1)S(1)}, u32[]{:S(2)}, u32[]{:S(2)}) collective-permute-start(bf16[4,256,256]{2,1,0:T(8,128)(2,1)S(1)} %reshape.556), channel_id=1, source_target_pairs={{0,0},{1,1},{2,2},{3,3},{4,4},{5,5},{6,6},{7,7},{8,8},{9,9},{10,10... | collective-permute-start | bytes 1572872 | tf_op jit(solution)/shard_map/ppermute | solution.py:260
  16.1 35.9 %collective-permute-start.1 = (bf16[4,256,256]{2,1,0:T(8,128)(2,1)S(1)}, bf16[4,256,256]{2,1,0:T(8,128)(2,1)S(1)}, u32[]{:S(2)}, u32[]{:S(2)}) collective-permute-start(bf16[4,256,256]{2,1,0:T(8,128)(2,1)S(1)} %reshape.556), channel_id=1, source_target_pairs={{0,64},{1,65},{2,66},{3,67},{4,68},{5,69},{6,70},{7,71},{8,72},{9,... | collective-permute-start | bytes 1572872 | tf_op jit(solution)/shard_map/ppermute | solution.py:260
  20.0 34.8 %collective-permute-start.2 = (bf16[4,256,256]{2,1,0:T(8,128)(2,1)S(1)}, bf16[4,256,256]{2,1,0:T(8,128)(2,1)S(1)}, u32[]{:S(2)}, u32[]{:S(2)}) collective-permute-start(bf16[4,256,256]{2,1,0:T(8,128)(2,1)S(1)} %reshape.556), channel_id=1, source_target_pairs={{0,128},{1,129},{2,130},{3,131},{4,132},{5,133},{6,134},{7,135},{8... | collective-permute-start | bytes 1572872 | tf_op jit(solution)/shard_map/ppermute | solution.py:260
  26.0 42.9 %collective-permute-start.3 = (bf16[4,256,256]{2,1,0:T(8,128)(2,1)S(1)}, bf16[4,256,256]{2,1,0:T(8,128)(2,1)S(1)}, u32[]{:S(2)}, u32[]{:S(2)}) collective-permute-start(bf16[4,256,256]{2,1,0:T(8,128)(2,1)S(1)} %reshape.556), channel_id=1, source_target_pairs={{0,192},{1,193},{2,194},{3,195},{4,196},{5,197},{6,198},{7,199},{8... | collective-permute-start | bytes 1572872 | tf_op jit(solution)/shard_map/ppermute | solution.py:260
  28.9 40.9 %collective-permute-start.4 = (bf16[4,256,256]{2,1,0:T(8,128)(2,1)S(1)}, bf16[4,256,256]{2,1,0:T(8,128)(2,1)S(1)}, u32[]{:S(2)}, u32[]{:S(2)}) collective-permute-start(bf16[4,256,256]{2,1,0:T(8,128)(2,1)S(1)} %reshape.556), channel_id=1, source_target_pairs={{0,256},{1,257},{2,258},{3,259},{4,260},{5,261},{6,262},{7,263},{8... | collective-permute-start | bytes 1572872 | tf_op jit(solution)/shard_map/ppermute | solution.py:260
  33.0 51.9 %collective-permute-start.5 = (bf16[4,256,256]{2,1,0:T(8,128)(2,1)S(1)}, bf16[4,256,256]{2,1,0:T(8,128)(2,1)S(1)}, u32[]{:S(2)}, u32[]{:S(2)}) collective-permute-start(bf16[4,256,256]{2,1,0:T(8,128)(2,1)S(1)} %reshape.556), channel_id=1, source_target_pairs={{0,320},{1,321},{2,322},{3,323},{4,324},{5,325},{6,326},{7,327},{8... | collective-permute-start | bytes 1572872 | tf_op jit(solution)/shard_map/ppermute | solution.py:260
  37.2 64.1 %copy-start.8 = (bf16[256,256]{1,0:T(8,128)(2,1)S(1)}, bf16[256,256]{1,0:T(8,128)(2,1)}, u32[]{:S(2)}) copy-start(bf16[256,256]{1,0:T(8,128)(2,1)} %param.20) | copy-start | bytes 393220
  37.2 64.9 %copy-start.7 = (bf16[4,128,2]{2,1,0:T(8,128)(2,1)S(1)}, bf16[4,128,2]{2,1,0:T(8,128)(2,1)}, u32[]{:S(2)}) copy-start(bf16[4,128,2]{2,1,0:T(8,128)(2,1)} %constant.168.clone) | copy-start | bytes 6148
  52.0 33.7 %collective-permute-start.6 = (bf16[4,256,256]{2,1,0:T(8,128)(2,1)S(1)}, bf16[4,256,256]{2,1,0:T(8,128)(2,1)S(1)}, u32[]{:S(2)}, u32[]{:S(2)}) collective-permute-start(bf16[4,256,256]{2,1,0:T(8,128)(2,1)S(1)} %reshape.556), channel_id=1, source_target_pairs={{0,384},{1,385},{2,386},{3,387},{4,388},{5,389},{6,390},{7,391},{8... | collective-permute-start | bytes 1572872 | tf_op jit(solution)/shard_map/ppermute | solution.py:260
  54.8 32.8 %collective-permute-start.7 = (bf16[4,256,256]{2,1,0:T(8,128)(2,1)S(1)}, bf16[4,256,256]{2,1,0:T(8,128)(2,1)S(1)}, u32[]{:S(2)}, u32[]{:S(2)}) collective-permute-start(bf16[4,256,256]{2,1,0:T(8,128)(2,1)S(1)} %reshape.556), channel_id=1, source_target_pairs={{0,448},{1,449},{2,450},{3,451},{4,452},{5,453},{6,454},{7,455},{8... | collective-permute-start | bytes 1572872 | tf_op jit(solution)/shard_map/ppermute | solution.py:260
  88.4 35.8 %collective-permute-start.8 = (bf16[8,4,256,256]{3,2,1,0:T(8,128)(2,1)}, bf16[8,4,256,256]{3,2,1,0:T(8,128)(2,1)}, u32[]{:S(2)}, u32[]{:S(2)}) collective-permute-start(bf16[8,4,256,256]{3,2,1,0:T(8,128)(2,1)} %bitcast_dynamic-update-slice_fusion.near_ref), channel_id=1, source_target_pairs={{0,32},{32,0},{64,96},{96,64},{128,160},{160,128},{192,224},{224,1... | collective-permute-start | bytes 12582920 | tf_op jit(solution)/shard_map/ppermute | solution.py:262
  90.4 16.2 %collective-permute-start.9 = (bf16[4,128,256]{2,1,0:T(8,128)(2,1)S(1)}, bf16[4,128,256]{2,1,0:T(8,128)(2,1)S(1)}, u32[]{:S(2)}, u32[]{:S(2)}) collective-permute-start(bf16[4,128,256]{2,1,0:T(8,128)(2,1)S(1)} %copy-done.5), channel_id=1, source_target_pairs={{0,16},{1,17},{2,18},{3,19},{4,20},{5,21},{6,22},{7,23},{8,24},{9,... | collective-permute-start | bytes 786440 | tf_op jit(solution)/shard_map/ppermute | solution.py:252
  124.2 2.2 copy-start.1
  126.4 43.8 %copy-start.9 = (bf16[256,256]{1,0:T(8,128)(2,1)S(1)}, bf16[256,256]{1,0:T(8,128)(2,1)}, u32[]{:S(2)}) copy-start(bf16[256,256]{1,0:T(8,128)(2,1)} %param.21) | copy-start | bytes 393220
  126.4 44.5 %copy-start.12 = (f32[256]{0:T(256)S(1)}, f32[256]{0:T(256)}, u32[]{:S(2)}) copy-start(f32[256]{0:T(256)} %param.22) | copy-start | bytes 3076
  138.2 74.6 %collective-permute-start.10 = (bf16[4,256,128]{2,1,0:T(8,128)(2,1)S(1)}, bf16[4,256,128]{2,1,0:T(8,128)(2,1)S(1)}, u32[]{:S(2)}, u32[]{:S(2)}) collective-permute-start(bf16[4,256,128]{2,1,0:T(8,128)(2,1)S(1)} %get-tuple-element.15), channel_id=1, source_target_pairs={{0,16},{1,17},{2,18},{3,19},{4,20},{5,21},{6,22},{7,23},{8,24},{9,... | collective-permute-start | bytes 786440 | tf_op jit(solution)/shard_map/ppermute | solution.py:297
  168.2 44.6 %collective-permute-start.11 = (f32[4,4,2,128]{3,2,1,0:T(2,128)S(1)}, f32[4,4,2,128]{3,2,1,0:T(2,128)S(1)}, u32[]{:S(2)}, u32[]{:S(2)}) collective-permute-start(f32[4,4,2,128]{3,2,1,0:T(2,128)S(1)} %get-tuple-element.16), channel_id=1, source_target_pairs={{0,16},{1,17},{2,18},{3,19},{4,20},{5,21},{6,22},{7,23},{8,24},{9,... | collective-permute-start | bytes 49160 | tf_op jit(solution)/shard_map/ppermute | solution.py:298
  171.8 2.2 copy-start.2
  211.4 0.8 copy-start.3
  212.8 0.7 copy-start.6
  (2 other events, 1.2 us)
Sparse Core Ops, SparseCore 0:
  10.9 75.4 all-gather.2

commit v2 on v0

v2 whole, which is shorter than its diff:
```python
import jax
import jax.numpy as jnp
import numpy as np
from jax import lax
from jax.experimental import pallas as pl
from jax.experimental.pallas import tpu as pltpu
from jax.sharding import PartitionSpec as P

H = 8
DH = 32
BLOCK = 128
HALF = 128
GROUP = 4
TILE = 4
EXTRA = 16
SAFE_LOW = 2.0**-60
SAFE_HIGH = 2.0**90
LOG2E = 1.4426950408889634
LOW = -1e30

SEQ, RES, NZ = 16, 32, 16
Z_GROUPS = [[yl * NZ + z for z in range(NZ)] for yl in range(2)]
YL_PAIRS = [(r, (r + NZ) % RES) for r in range(RES)]
C_PAIRS = [(s, s ^ 1) for s in range(SEQ)]


def bias_pairs(u, v):
    pairs = []
    for x in range(4):
        for yh in range(2):
            for c in range(2):
                for yl in range(2):
                    for z in range(NZ):
                        to_x, to_yh, to_yl = (x + 2 * yl + u) % 4, yh ^ v, x // 2
                        source = (x * 4 + yh * 2 + c) * RES + yl * NZ + z
                        target = (to_x * 4 + to_yh * 2 + c) * RES + to_yl * NZ + z
                        pairs.append((source, target))
    return pairs


def standardize_features(source, scale, offset):
    values_f = source.astype(jnp.float32)
    center = jnp.mean(values_f, axis=-1, keepdims=True)
    spread = jnp.mean((values_f - center) ** 2, axis=-1, keepdims=True)
    return (values_f - center) * lax.rsqrt(spread + 1e-05) * scale + offset


def normalize_kernel(features_ref, scale_ref, offset_ref, out_ref):
    for s in range(features_ref.shape[0]):
        out_ref[s] = standardize_features(
            features_ref[s], scale_ref[...], offset_ref[...]
        ).astype(jnp.bfloat16)


def normalize(features, scale, offset):
    return pl.pallas_call(
        normalize_kernel,
        out_shape=jax.ShapeDtypeStruct(features.shape, jnp.bfloat16),
        name="normalize",
    )(features, scale, offset)


def prepare_kernel(
    normed_ref, partner_ref, scale_ref, offset_ref, query_w_ref, gate_w_ref, gate_off_ref,
    query_ref, gate_ref,
):
    for s in range(normed_ref.shape[0]):
        own = normed_ref[s]
        other = standardize_features(partner_ref[s], scale_ref[...], offset_ref[...]).astype(
            jnp.bfloat16
        )
        for r, rows in enumerate((other, own)):
            query = jnp.dot(rows, query_w_ref[...], preferred_element_type=jnp.float32)
            query_ref[r, s] = (query * (LOG2E / DH**0.5)).astype(jnp.bfloat16)
        gate_ref[s] = jax.nn.sigmoid(
            jnp.dot(own, gate_w_ref[...], preferred_element_type=jnp.float32) + gate_off_ref[...]
        )


def prepare(normed, partner, scale, offset, query_w, gate_w, gate_off):
    depth, span, width = normed.shape
    return pl.pallas_call(
        prepare_kernel,
        out_shape=[
            jax.ShapeDtypeStruct((2, depth, span, width), jnp.bfloat16),
            jax.ShapeDtypeStruct((depth, span, width), jnp.float32),
        ],
        name="prepare",
    )(normed, partner, scale, offset, query_w, gate_w, gate_off)


def attend_kernel(
    mask_ref, rows_ref, key_w_ref, value_w_ref, query_ref, near0_ref, near1_ref, far0_ref, far1_ref,
    sent_ref, own_ref,
    table_ref, key_ref, value_ref, spread_ref, bias_ref, acc_ref, top_ref, shift_ref,
):
    blocks, depth, span, width = rows_ref.shape
    g, r = pl.program_id(0), pl.program_id(1)
    seq, res = lax.axis_index("seq"), lax.axis_index("res")
    x, yh, c = seq // 4, lax.rem(seq // 2, 2), lax.rem(seq, 2)
    half, z_own = res // NZ, lax.rem(res, NZ)
    yl = jnp.where(r == 0, 1 - half, half)

    @pl.when((r == 0) & (g == 0))
    def _():
        key_wt = key_w_ref[...].astype(jnp.float32).T.astype(jnp.bfloat16)

        def fill(t, carry):
            rows = rows_ref[pl.ds(2 * t, 2)].reshape(2 * depth * span, width)
            keys = lax.dot_general(
                key_wt, rows, (((1,), (1,)), ((), ())), preferred_element_type=jnp.float32
            ).astype(jnp.bfloat16)
            values = jnp.dot(rows, value_w_ref[...], preferred_element_type=jnp.float32).astype(
                jnp.bfloat16
            )
            for i in range(2):
                for s in range(depth):
                    part = slice((i * depth + s) * span, (i * depth + s + 1) * span)
                    for e in range(2):
                        lanes = slice(e * HALF, (e + 1) * HALF)
                        key_ref[e, s, 2 * t + i] = keys[lanes, part]
                        value_ref[e, s, 2 * t + i, :, :HALF] = values[part, lanes]
                        value_ref[e, s, 2 * t + i, :, HALF:] = jnp.ones((span, HALF), jnp.bfloat16)
            return carry

        lax.fori_loop(0, blocks // 2, fill, 0)

    def clear(i, carry):
        for row in range(3):
            table_ref[row, i] = 0
        return carry

    def place(z, count):
        slot = z // 8 + 2 * yl
        table_ref[0, count] = z
        table_ref[1, count] = lax.rem(z // 2, 2) ^ c
        table_ref[2, count] = 2 * lax.rem(x - 2 * half - slot + 8, 4) + (lax.rem(z // 4, 2) ^ yh)
        return count + jnp.where(mask_ref[yl * NZ + z_own, half * NZ + z] > 0, 1, 0)

    lax.fori_loop(0, blocks, clear, 0)
    live = lax.fori_loop(0, blocks, place, 0)

    head_of_lane = lax.broadcasted_iota(jnp.int32, (span, HALF), 1) // DH
    for s in range(depth):
        query = query_ref[0, s].astype(jnp.float32)
        for h in range(GROUP):
            spread_ref[s, h * span : (h + 1) * span] = jnp.where(
                head_of_lane == h, query, 0.0
            ).astype(jnp.bfloat16)

    def bias_of(i):
        is_far, turn = table_ref[1, i], table_ref[2, i]
        lanes = pl.ds(pl.multiple_of(lax.rem(table_ref[0, i], 2) * BLOCK, BLOCK), BLOCK)
        inner = lax.rem(turn, 4)
        near = jnp.where(turn < 4, near0_ref[inner, :, :, lanes], near1_ref[inner, :, :, lanes])
        far = jnp.where(turn < 4, far0_ref[inner, :, :, lanes], far1_ref[inner, :, :, lanes])
        bias = jnp.where(is_far > 0, far, near).astype(jnp.float32)
        return (bias * LOG2E).reshape(GROUP * span, BLOCK)

    acc_ref[...] = jnp.zeros_like(acc_ref)

    def fast(t, carry):
        spots = [TILE * t + i for i in range(TILE)]
        z = [table_ref[0, i] for i in spots]
        for i in range(TILE):
            absent = jnp.where(spots[i] < live, 0.0, LOW)
            bias_ref[:, i * BLOCK : (i + 1) * BLOCK] = bias_of(spots[i]) + absent

        def weigh(s):
            keys = jnp.concatenate([key_ref[g, s, i] for i in z], axis=1)
            score = jnp.dot(spread_ref[s], keys, preferred_element_type=jnp.float32)
            return jnp.exp2(score + bias_ref[...]).astype(jnp.bfloat16)

        def add(s, weight):
            value = jnp.concatenate([value_ref[g, s, i] for i in z], axis=0)
            acc_ref[s] += jnp.dot(weight, value, preferred_element_type=jnp.float32)

        weight = weigh(0)
        for s in range(1, depth):
            later = weigh(s)
            add(s - 1, weight)
            weight = later
        add(depth - 1, weight)
        return carry

    lax.fori_loop(0, (live + TILE - 1) // TILE, fast, 0)
    totals = acc_ref[:, :, HALF:]
    bad = (live > 0) & ((jnp.max(totals) > SAFE_HIGH) | (jnp.min(totals) < SAFE_LOW))
    shift_ref[...] = jnp.zeros_like(shift_ref)

    @pl.when(bad)
    def _():
        top_ref[...] = jnp.full_like(top_ref, LOW)
        acc_ref[...] = jnp.zeros_like(acc_ref)

        def careful(t, carry):
            z = table_ref[0, t]
            bias_ref[:, :BLOCK] = bias_of(t)

            def one(s, inner):
                score = (
                    jnp.dot(spread_ref[s], key_ref[g, s, z], preferred_element_type=jnp.float32)
                    + bias_ref[:, :BLOCK]
                )
                old = top_ref[s]
                top = jnp.maximum(old, jnp.max(score, axis=1, keepdims=True))
                top_ref[s] = top
                weight = jnp.exp2(score - top).astype(jnp.bfloat16)
                acc_ref[s] = acc_ref[s] * jnp.exp2(old - top) + jnp.dot(
                    weight, value_ref[g, s, z], preferred_element_type=jnp.float32
                )
                return inner

            return lax.fori_loop(0, depth, one, carry)

        lax.fori_loop(0, live, careful, 0)
        for s in range(depth):
            shift = jnp.zeros((span, HALF), jnp.float32)
            for h in range(GROUP):
                shift = jnp.where(head_of_lane == h, top_ref[s, h * span : (h + 1) * span], shift)
            shift_ref[s] = shift

    for s in range(depth):
        total = jnp.zeros((span, HALF), jnp.float32)
        summed = jnp.zeros((span, HALF), jnp.float32)
        for h in range(GROUP):
            part = slice(h * span, (h + 1) * span)
            mine = head_of_lane == h
            summed = jnp.where(mine, acc_ref[s, part, :HALF], summed)
            total = jnp.where(mine, acc_ref[s, part, HALF:], total)
        some = total > 0.0
        safe = jnp.where(some, total, 1.0)
        mean = summed / safe
        wide = jnp.where(some, shift_ref[s] + jnp.log2(safe), LOW).T
        lse = jnp.concatenate([wide[h * DH : h * DH + 1] for h in range(GROUP)], axis=0)

        @pl.when(r == 0)
        def _():
            first = lse.astype(jnp.bfloat16).astype(jnp.float32)
            second = (lse - first).astype(jnp.bfloat16).astype(jnp.float32)
            third = lse - first - second
            sent_ref[s, :span] = mean.astype(jnp.bfloat16)
            sent_ref[s, span:] = jnp.concatenate(
                [first, second, third, jnp.zeros_like(lse)], axis=0
            ).astype(jnp.bfloat16)

        @pl.when(r == 1)
        def _():
            own_ref[s, :span] = mean
            own_ref[s, span:] = jnp.concatenate([lse, jnp.zeros_like(lse)], axis=0)


def attend(mask, rows, key_w, value_w, queries, near0, near1, far0, far1):
    blocks, depth, span, width = rows.shape
    turns = near0.shape[0]
    whole = lambda *shape: pl.BlockSpec(
        shape, lambda g, r: (0,) * len(shape), pipeline_mode=pl.Buffered(1)
    )
    bias = pl.BlockSpec((turns, GROUP, span, 2 * BLOCK), lambda g, r: (0, g, 0, 0))
    by_group = lambda g, r: (0, 0, g)
    return pl.pallas_call(
        attend_kernel,
        grid=(2, 2),
        in_specs=[
            pl.BlockSpec(memory_space=pltpu.SMEM),
            whole(blocks, depth, span, width),
            whole(width, width),
            whole(width, width),
            pl.BlockSpec((1, depth, span, HALF), lambda g, r: (r, 0, 0, g)),
            bias,
            bias,
            bias,
            bias,
        ],
        out_specs=[
            pl.BlockSpec((depth, span + EXTRA, HALF), by_group),
            pl.BlockSpec((depth, span + 8, HALF), by_group),
        ],
        out_shape=[
            jax.ShapeDtypeStruct((depth, span + EXTRA, width), jnp.bfloat16),
            jax.ShapeDtypeStruct((depth, span + 8, width), jnp.float32),
        ],
        scratch_shapes=[
            pltpu.SMEM((3, blocks), jnp.int32),
            pltpu.VMEM((2, depth, blocks, HALF, span), jnp.bfloat16),
            pltpu.VMEM((2, depth, blocks, span, 2 * HALF), jnp.bfloat16),
            pltpu.VMEM((depth, GROUP * span, HALF), jnp.bfloat16),
            pltpu.VMEM((GROUP * span, TILE * BLOCK), jnp.float32),
            pltpu.VMEM((depth, GROUP * span, 2 * HALF), jnp.float32),
            pltpu.VMEM((depth, GROUP * span, 1), jnp.float32),
            pltpu.VMEM((depth, span, HALF), jnp.float32),
        ],
        compiler_params=pltpu.CompilerParams(vmem_limit_bytes=56 * 1024 * 1024),
        name="attend",
    )(mask, rows, key_w, value_w, queries, near0, near1, far0, far1)


def finish_kernel(own_ref, got_ref, gate_ref, out_w_ref, out_off_ref, out_ref):
    depth, span, width = gate_ref.shape

    def widen(part):
        return jnp.broadcast_to(part[:, None, :], (GROUP, DH, span)).reshape(HALF, span).T

    for s in range(depth):
        gated = []
        for g in range(2):
            lanes = slice(g * HALF, (g + 1) * HALF)
            own_lse = own_ref[s, span : span + GROUP, lanes]
            pieces = got_ref[s, span:, lanes].astype(jnp.float32)
            got_lse = pieces[:GROUP] + pieces[GROUP : 2 * GROUP] + pieces[2 * GROUP : 3 * GROUP]
            own_part = widen(1.0 / (1.0 + jnp.exp2(got_lse - own_lse)))
            got_part = widen(1.0 / (1.0 + jnp.exp2(own_lse - got_lse)))
            attended = (
                own_ref[s, :span, lanes] * own_part
                + got_ref[s, :span, lanes].astype(jnp.float32) * got_part
            )
            gated.append((gate_ref[s, :, lanes] * attended).astype(jnp.bfloat16))
        result = jnp.dot(
            jnp.concatenate(gated, axis=1), out_w_ref[...], preferred_element_type=jnp.float32
        )
        out_ref[s] = (result + out_off_ref[...]).astype(jnp.bfloat16)


def finish(own, got, gate, out_w, out_off):
    return pl.pallas_call(
        finish_kernel,
        out_shape=jax.ShapeDtypeStruct(gate.shape, jnp.bfloat16),
        name="finish",
    )(own, got, gate, out_w, out_off)


def on_device(
    alignment_features,
    coupling_logit_offset,
    contact_tile_filter,
    standard_scale_array,
    standard_offset_array,
    probe_projection,
    lookup_projection,
    content_projection,
    sigmoid_projection,
    sigmoid_offset_array,
    result_projection,
    result_offset,
):
    scale, offset = standard_scale_array[None, :], standard_offset_array[None, :]
    partner = lax.ppermute(alignment_features, "res", YL_PAIRS)
    normed = normalize(alignment_features, scale, offset)
    gathered = lax.all_gather(normed, "res", axis_index_groups=Z_GROUPS)
    rounds = [
        lax.ppermute(coupling_logit_offset, ("seq", "res"), bias_pairs(u, v))
        for u in range(4)
        for v in range(2)
    ]
    near0, near1 = jnp.stack(rounds[:4]), jnp.stack(rounds[4:])
    far0 = lax.ppermute(near0, "seq", C_PAIRS)
    far1 = lax.ppermute(near1, "seq", C_PAIRS)
    queries, gate = prepare(
        normed, partner, scale, offset, probe_projection, sigmoid_projection,
        sigmoid_offset_array[None, :],
    )
    sent, own = attend(
        contact_tile_filter, gathered, lookup_projection, content_projection, queries,
        near0, near1, far0, far1,
    )
    got = lax.ppermute(sent, "res", YL_PAIRS)
    return finish(own, got, gate, result_projection, result_offset[None, :])


def solution(mesh):
    return jax.shard_map(
        on_device,
        mesh=mesh,
        in_specs=(
            P("seq", "res", None),
            P(None, "res", "seq"),
            P(),
            P(),
            P(),
            P(),
            P(),
            P(),
            P(),
            P(),
            P(),
            P(),
        ),
        out_specs=P("seq", "res", None),
        check_vma=False,
    )
```

time: 533 us -> 234 us (0.44)
  the two profiles are of different devices: /device:TPU:8 before, /device:TPU:184 now
where the time goes in v2:
time: 234 us
  Pallas kernels  117 us (50%)
  waiting for transfers between devices  63.9 us (27%)
  starting transfers between devices  36.2 us (15%)
  between operations  13.6 us (6%)
    pallas_call x1, Pallas kernels, attend(): pl.pallas_call(attend_kernel, grid=(2, 2), in_specs=[pl.BlockSpec(memory_...  110 us
    ppermute x8, waiting for transfers between devices, on_device(): lax.ppermute(coupling_logit_offset, ('seq', 'res'), bias_pairs(u, v))  46.4 us
    ppermute x8, starting transfers between devices, on_device(): lax.ppermute(coupling_logit_offset, ('seq', 'res'), bias_pairs(u, v))  28.5 us
    ppermute x1, waiting for transfers between devices, on_device(): got = lax.ppermute(sent, 'res', YL_PAIRS)  8.81 us
    ppermute x1, waiting for transfers between devices, on_device(): partner = lax.ppermute(alignment_features, 'res', YL_PAIRS)  8.67 us
  transfers between devices with their start and end apart: 13, of which 7 were waited for; matrix products, arithmetic and copies ran while one was open for 1% of the time, Pallas kernels for 1%

profile of v2, /device:TPU:184, one launch (start us, length us, event | category | flops | bytes accessed | tf_op | source)
XLA Modules:
  0.0 233.9 jit_solution(18324184369867029257)
XLA Ops:
  6.5 1.9 normalize.1.normed_ref
  8.5 2.1 collective-permute-start.6
  10.6 5.2 %collective-permute-start.5 = (bf16[8,128,256]{2,1,0:T(8,128)(2,1)}, bf16[8,128,256]{2,1,0:T(8,128)(2,1)S(1)}, u32[]{:S(2)}, u32[]{:S(2)}) collective-permute-start(bf16[8,128,256]{2,1,0:T(8,128)(2,1)} %param.13), channel_id=1, source_target_pairs={{0,256},{1,257},{2,258},{3,259},{4,260},{5,261},{6,262},{7,263},{8... | collective-permute-start | bytes 1572872 | tf_op jit(solution)/shard_map/ppermute | solution.py:351
  15.9 5.5 %collective-permute-start.8 = (bf16[8,128,256]{2,1,0:T(8,128)(2,1)}, bf16[8,128,256]{2,1,0:T(8,128)(2,1)S(1)}, u32[]{:S(2)}, u32[]{:S(2)}) collective-permute-start(bf16[8,128,256]{2,1,0:T(8,128)(2,1)} %param.13), channel_id=1, source_target_pairs={{0,448},{1,449},{2,450},{3,451},{4,452},{5,453},{6,454},{7,455},{8... | collective-permute-start | bytes 1572872 | tf_op jit(solution)/shard_map/ppermute | solution.py:351
  21.4 2.7 %collective-permute-start.7 = (bf16[8,128,256]{2,1,0:T(8,128)(2,1)}, bf16[8,128,256]{2,1,0:T(8,128)(2,1)S(1)}, u32[]{:S(2)}, u32[]{:S(2)}) collective-permute-start(bf16[8,128,256]{2,1,0:T(8,128)(2,1)} %param.13), channel_id=1, source_target_pairs={{0,384},{1,385},{2,386},{3,387},{4,388},{5,389},{6,390},{7,391},{8... | collective-permute-start | bytes 1572872 | tf_op jit(solution)/shard_map/ppermute | solution.py:351
  24.1 2.1 collective-permute-start.4
  26.3 5.8 %collective-permute-done.6 = bf16[8,128,256]{2,1,0:T(8,128)(2,1)S(1)} collective-permute-done((bf16[8,128,256]{2,1,0:T(8,128)(2,1)}, bf16[8,128,256]{2,1,0:T(8,128)(2,1)S(1)}, u32[]{:S(2)}, u32[]{:S(2)}) %collective-permute-start.6) | collective-permute-done | bytes 524320 | tf_op jit(solution)/shard_map/ppermute | solution.py:351
  32.1 3.1 %collective-permute-start.3 = (bf16[8,128,256]{2,1,0:T(8,128)(2,1)}, bf16[8,128,256]{2,1,0:T(8,128)(2,1)S(1)}, u32[]{:S(2)}, u32[]{:S(2)}) collective-permute-start(bf16[8,128,256]{2,1,0:T(8,128)(2,1)} %param.13), channel_id=1, source_target_pairs={{0,128},{1,129},{2,130},{3,131},{4,132},{5,133},{6,134},{7,135},{8... | collective-permute-start | bytes 1572872 | tf_op jit(solution)/shard_map/ppermute | solution.py:351
  35.2 12.8 %collective-permute-done.5 = bf16[8,128,256]{2,1,0:T(8,128)(2,1)S(1)} collective-permute-done((bf16[8,128,256]{2,1,0:T(8,128)(2,1)}, bf16[8,128,256]{2,1,0:T(8,128)(2,1)S(1)}, u32[]{:S(2)}, u32[]{:S(2)}) %collective-permute-start.5) | collective-permute-done | bytes 524320 | tf_op jit(solution)/shard_map/ppermute | solution.py:351
  48.0 2.5 %collective-permute-start.2 = (bf16[8,128,256]{2,1,0:T(8,128)(2,1)}, bf16[8,128,256]{2,1,0:T(8,128)(2,1)S(1)}, u32[]{:S(2)}, u32[]{:S(2)}) collective-permute-start(bf16[8,128,256]{2,1,0:T(8,128)(2,1)} %param.13), channel_id=1, source_target_pairs={{0,64},{1,65},{2,66},{3,67},{4,68},{5,69},{6,70},{7,71},{8,72},{9,... | collective-permute-start | bytes 1572872 | tf_op jit(solution)/shard_map/ppermute | solution.py:351
  50.5 5.2 %collective-permute-start.1 = (bf16[8,128,256]{2,1,0:T(8,128)(2,1)}, bf16[8,128,256]{2,1,0:T(8,128)(2,1)S(1)}, u32[]{:S(2)}, u32[]{:S(2)}) collective-permute-start(bf16[8,128,256]{2,1,0:T(8,128)(2,1)} %param.13), channel_id=1, source_target_pairs={{0,0},{1,1},{2,2},{3,3},{4,4},{5,5},{6,6},{7,7},{8,8},{9,9},{10,10... | collective-permute-start | bytes 1572872 | tf_op jit(solution)/shard_map/ppermute | solution.py:351
  56.0 1.9 collective-permute-start.10
  58.0 3.0 %collective-permute-done.3 = bf16[8,128,256]{2,1,0:T(8,128)(2,1)S(1)} collective-permute-done((bf16[8,128,256]{2,1,0:T(8,128)(2,1)}, bf16[8,128,256]{2,1,0:T(8,128)(2,1)S(1)}, u32[]{:S(2)}, u32[]{:S(2)}) %collective-permute-start.3) | collective-permute-done | bytes 524320 | tf_op jit(solution)/shard_map/ppermute | solution.py:351
  61.0 2.4 %collective-permute-done.2 = bf16[8,128,256]{2,1,0:T(8,128)(2,1)S(1)} collective-permute-done((bf16[8,128,256]{2,1,0:T(8,128)(2,1)}, bf16[8,128,256]{2,1,0:T(8,128)(2,1)S(1)}, u32[]{:S(2)}, u32[]{:S(2)}) %collective-permute-start.2) | collective-permute-done | bytes 524320 | tf_op jit(solution)/shard_map/ppermute | solution.py:351
  63.3 22.3 %collective-permute-done.1 = bf16[8,128,256]{2,1,0:T(8,128)(2,1)S(1)} collective-permute-done((bf16[8,128,256]{2,1,0:T(8,128)(2,1)}, bf16[8,128,256]{2,1,0:T(8,128)(2,1)S(1)}, u32[]{:S(2)}, u32[]{:S(2)}) %collective-permute-start.1) | collective-permute-done | bytes 524320 | tf_op jit(solution)/shard_map/ppermute | solution.py:351
  85.7 1.6 pad_maximum_fusion.near0_ref
  87.3 1.9 collective-permute-start.9
  89.2 1.9 collective-permute-start
  91.2 8.7 %collective-permute-done.partner_ref = bf16[4,128,256]{2,1,0:T(8,128)(2,1)S(1)} collective-permute-done((bf16[4,128,256]{2,1,0:T(8,128)(2,1)S(1)}, bf16[4,128,256]{2,1,0:T(8,128)(2,1)S(1)}, u32[]{:S(2)}, u32[]{:S(2)}) %collective-permute-start) | collective-permute-done | bytes 262176 | tf_op jit(solution)/shard_map/ppermute | solution.py:347
  100.6 2.7 %prepare.1 = (bf16[2,4,128,256]{3,2,1,0:T(8,128)(2,1)}, f32[4,128,256]{2,1,0:T(8,128)}) custom-call(bf16[4,128,256]{2,1,0:T(8,128)(2,1)} %normalize.1.normed_ref, bf16[4,128,256]{2,1,0:T(8,128)(2,1)} %copy-done.3, f32[1,256]{1,0:T(1,128)} %bitcast.23, f32[1,256]{1,0:T(1,128)} %bitcast.25, bf16[256,256]{1,0:T(8,128)(2,1)} %query_w_ref.1, ...), custom_call_target="tpu_custom_call" | custom-call | tf_op jit(solution)/shard_map/prepare/pallas_call | solution.py:82
  103.3 109.7 %attend.1 = (bf16[4,144,256]{2,1,0:T(8,128)(2,1)}, f32[4,136,256]{2,1,0:T(8,128)}) custom-call(s32[32,32]{1,0:T(8,128)} %mask_ref.1, bf16[16,4,128,256]{3,2,1,0:T(8,128)(2,1)} %bitcast.13, bf16[256,256]{1,0:T(8,128)(2,1)} %key_w_ref.1, bf16[256,256]{1,0:T(8,128)(2,1)} %value_w_ref.1, bf16[2,4,128,256]{3,2,1,0:T(8,128)(2,1)} %get-tuple-element.9.query_ref, ...), custom_call_target="tpu_custom_call" | custom-call | tf_op jit(solution)/shard_map/attend/pallas_call | solution.py:261
  213.0 1.9 collective-permute-start.11
  215.0 8.8 %collective-permute-done.11.got_ref = bf16[4,144,256]{2,1,0:T(8,128)(2,1)S(1)} collective-permute-done((bf16[4,144,256]{2,1,0:T(8,128)(2,1)}, bf16[4,144,256]{2,1,0:T(8,128)(2,1)S(1)}, u32[]{:S(2)}, u32[]{:S(2)}) %collective-permute-start.11) | collective-permute-done | bytes 294944 | tf_op jit(solution)/shard_map/ppermute | solution.py:366
  224.5 2.6 %finish.1 = bf16[4,128,256]{2,1,0:T(8,128)(2,1)} custom-call(f32[4,136,256]{2,1,0:T(8,128)} %get-tuple-element.10.own_ref, bf16[4,144,256]{2,1,0:T(8,128)(2,1)} %copy-done.1, f32[4,128,256]{2,1,0:T(8,128)} %get-tuple-element.12.gate_ref, bf16[256,256]{1,0:T(8,128)(2,1)} %out_w_ref.1, f32[1,256]{1,0:T(1,128)} %bitcast.27), custom_call_target="tpu_custom_call" | custom-call | tf_op jit(solution)/shard_map/finish/pallas_call | solution.py:325
  (17 shorter events, 1.8 us)
Async XLA Ops:
  6.5 96.8 %all-gather.3.cloned.1.call-start = ((), (), s32[]{:S(2)}) async-start(), calls=%async_computation | async-start | bytes 4456448 | tf_op jit(solution)/shard_map/all_gather | solution.py:349
  8.5 23.6 %collective-permute-start.6 = (bf16[8,128,256]{2,1,0:T(8,128)(2,1)}, bf16[8,128,256]{2,1,0:T(8,128)(2,1)S(1)}, u32[]{:S(2)}, u32[]{:S(2)}) collective-permute-start(bf16[8,128,256]{2,1,0:T(8,128)(2,1)} %param.13), channel_id=1, source_target_pairs={{0,320},{1,321},{2,322},{3,323},{4,324},{5,325},{6,326},{7,327},{8... | collective-permute-start | bytes 1572872 | tf_op jit(solution)/shard_map/ppermute | solution.py:351
  10.6 37.4 %collective-permute-start.5 = (bf16[8,128,256]{2,1,0:T(8,128)(2,1)}, bf16[8,128,256]{2,1,0:T(8,128)(2,1)S(1)}, u32[]{:S(2)}, u32[]{:S(2)}) collective-permute-start(bf16[8,128,256]{2,1,0:T(8,128)(2,1)} %param.13), channel_id=1, source_target_pairs={{0,256},{1,257},{2,258},{3,259},{4,260},{5,261},{6,262},{7,263},{8... | collective-permute-start | bytes 1572872 | tf_op jit(solution)/shard_map/ppermute | solution.py:351
  15.9 34.7 %collective-permute-start.8 = (bf16[8,128,256]{2,1,0:T(8,128)(2,1)}, bf16[8,128,256]{2,1,0:T(8,128)(2,1)S(1)}, u32[]{:S(2)}, u32[]{:S(2)}) collective-permute-start(bf16[8,128,256]{2,1,0:T(8,128)(2,1)} %param.13), channel_id=1, source_target_pairs={{0,448},{1,449},{2,450},{3,451},{4,452},{5,453},{6,454},{7,455},{8... | collective-permute-start | bytes 1572872 | tf_op jit(solution)/shard_map/ppermute | solution.py:351
  21.4 34.4 %collective-permute-start.7 = (bf16[8,128,256]{2,1,0:T(8,128)(2,1)}, bf16[8,128,256]{2,1,0:T(8,128)(2,1)S(1)}, u32[]{:S(2)}, u32[]{:S(2)}) collective-permute-start(bf16[8,128,256]{2,1,0:T(8,128)(2,1)} %param.13), channel_id=1, source_target_pairs={{0,384},{1,385},{2,386},{3,387},{4,388},{5,389},{6,390},{7,391},{8... | collective-permute-start | bytes 1572872 | tf_op jit(solution)/shard_map/ppermute | solution.py:351
  24.1 33.8 %collective-permute-start.4 = (bf16[8,128,256]{2,1,0:T(8,128)(2,1)}, bf16[8,128,256]{2,1,0:T(8,128)(2,1)S(1)}, u32[]{:S(2)}, u32[]{:S(2)}) collective-permute-start(bf16[8,128,256]{2,1,0:T(8,128)(2,1)} %param.13), channel_id=1, source_target_pairs={{0,192},{1,193},{2,194},{3,195},{4,196},{5,197},{6,198},{7,199},{8... | collective-permute-start | bytes 1572872 | tf_op jit(solution)/shard_map/ppermute | solution.py:351
  32.1 28.9 %collective-permute-start.3 = (bf16[8,128,256]{2,1,0:T(8,128)(2,1)}, bf16[8,128,256]{2,1,0:T(8,128)(2,1)S(1)}, u32[]{:S(2)}, u32[]{:S(2)}) collective-permute-start(bf16[8,128,256]{2,1,0:T(8,128)(2,1)} %param.13), channel_id=1, source_target_pairs={{0,128},{1,129},{2,130},{3,131},{4,132},{5,133},{6,134},{7,135},{8... | collective-permute-start | bytes 1572872 | tf_op jit(solution)/shard_map/ppermute | solution.py:351
  48.0 15.3 %collective-permute-start.2 = (bf16[8,128,256]{2,1,0:T(8,128)(2,1)}, bf16[8,128,256]{2,1,0:T(8,128)(2,1)S(1)}, u32[]{:S(2)}, u32[]{:S(2)}) collective-permute-start(bf16[8,128,256]{2,1,0:T(8,128)(2,1)} %param.13), channel_id=1, source_target_pairs={{0,64},{1,65},{2,66},{3,67},{4,68},{5,69},{6,70},{7,71},{8,72},{9,... | collective-permute-start | bytes 1572872 | tf_op jit(solution)/shard_map/ppermute | solution.py:351
  50.5 35.2 %collective-permute-start.1 = (bf16[8,128,256]{2,1,0:T(8,128)(2,1)}, bf16[8,128,256]{2,1,0:T(8,128)(2,1)S(1)}, u32[]{:S(2)}, u32[]{:S(2)}) collective-permute-start(bf16[8,128,256]{2,1,0:T(8,128)(2,1)} %param.13), channel_id=1, source_target_pairs={{0,0},{1,1},{2,2},{3,3},{4,4},{5,5},{6,6},{7,7},{8,8},{9,9},{10,10... | collective-permute-start | bytes 1572872 | tf_op jit(solution)/shard_map/ppermute | solution.py:351
  56.0 31.3 %copy-start = (bf16[4,8,128,256]{3,2,1,0:T(8,128)(2,1)}, bf16[4,8,128,256]{3,2,1,0:T(8,128)(2,1)S(1)}, u32[]{:S(2)}) copy-start(bf16[4,8,128,256]{3,2,1,0:T(8,128)(2,1)S(1)} %pad_maximum_fusion.1.near1_ref) | copy-start | bytes 6291460
  56.0 47.3 %collective-permute-start.10 = (bf16[4,8,128,256]{3,2,1,0:T(8,128)(2,1)S(1)}, bf16[4,8,128,256]{3,2,1,0:T(8,128)(2,1)}, u32[]{:S(2)}, u32[]{:S(2)}) collective-permute-start(bf16[4,8,128,256]{3,2,1,0:T(8,128)(2,1)S(1)} %pad_maximum_fusion.1.near1_ref), channel_id=1, source_target_pairs={{0,32},{32,0},{64,96},{96,64},{128,160},{160,128},{192,224},{224,1... | collective-permute-start | bytes 6291464 | tf_op jit(solution)/shard_map/ppermute | solution.py:357
  85.7 3.5 %copy-start.2 = (bf16[4,128,256]{2,1,0:T(8,128)(2,1)S(1)}, bf16[4,128,256]{2,1,0:T(8,128)(2,1)}, u32[]{:S(2)}) copy-start(bf16[4,128,256]{2,1,0:T(8,128)(2,1)} %features_ref.1) | copy-start | bytes 786436
  87.3 16.0 %collective-permute-start.9 = (bf16[4,8,128,256]{3,2,1,0:T(8,128)(2,1)}, bf16[4,8,128,256]{3,2,1,0:T(8,128)(2,1)}, u32[]{:S(2)}, u32[]{:S(2)}) collective-permute-start(bf16[4,8,128,256]{3,2,1,0:T(8,128)(2,1)} %pad_maximum_fusion.near0_ref), channel_id=1, source_target_pairs={{0,32},{32,0},{64,96},{96,64},{128,160},{160,128},{192,224},{224,1... | collective-permute-start | bytes 6291464 | tf_op jit(solution)/shard_map/ppermute | solution.py:356
  89.2 10.6 %collective-permute-start = (bf16[4,128,256]{2,1,0:T(8,128)(2,1)S(1)}, bf16[4,128,256]{2,1,0:T(8,128)(2,1)S(1)}, u32[]{:S(2)}, u32[]{:S(2)}) collective-permute-start(bf16[4,128,256]{2,1,0:T(8,128)(2,1)S(1)} %copy-done.2), channel_id=1, source_target_pairs={{0,16},{1,17},{2,18},{3,19},{4,20},{5,21},{6,22},{7,23},{8,24},{9,... | collective-permute-start | bytes 786440 | tf_op jit(solution)/shard_map/ppermute | solution.py:347
  99.8 0.7 copy-start.3
  213.0 10.7 %collective-permute-start.11 = (bf16[4,144,256]{2,1,0:T(8,128)(2,1)}, bf16[4,144,256]{2,1,0:T(8,128)(2,1)S(1)}, u32[]{:S(2)}, u32[]{:S(2)}) collective-permute-start(bf16[4,144,256]{2,1,0:T(8,128)(2,1)} %get-tuple-element.11), channel_id=1, source_target_pairs={{0,16},{1,17},{2,18},{3,19},{4,20},{5,21},{6,22},{7,23},{8,24},{9,... | collective-permute-start | bytes 884744 | tf_op jit(solution)/shard_map/ppermute | solution.py:366
  223.8 0.7 copy-start.1
Sparse Core Ops, SparseCore 0:
  9.4 78.0 all-gather.2

commit v3 on v2

v3 whole, which is shorter than its diff:
```python
import jax
import jax.numpy as jnp
import numpy as np
from jax import lax
from jax.experimental import pallas as pl
from jax.experimental.pallas import tpu as pltpu
from jax.sharding import PartitionSpec as P

H = 8
DH = 32
BLOCK = 128
HALF = 128
GROUP = 4
TILE = 4
EXTRA = 16
SAFE_LOW = 2.0**-60
SAFE_HIGH = 2.0**90
LOG2E = 1.4426950408889634
LOW = -1e30

SEQ, RES, NZ = 16, 32, 16
Z_GROUPS = [[yl * NZ + z for z in range(NZ)] for yl in range(2)]
YL_PAIRS = [(r, (r + NZ) % RES) for r in range(RES)]
C_PAIRS = [(s, s ^ 1) for s in range(SEQ)]


def bias_pairs(u, v):
    pairs = []
    for x in range(4):
        for yh in range(2):
            for c in range(2):
                for yl in range(2):
                    for z in range(NZ):
                        to_x, to_yh, to_yl = (x + 2 * yl + u) % 4, yh ^ v, x // 2
                        source = (x * 4 + yh * 2 + c) * RES + yl * NZ + z
                        target = (to_x * 4 + to_yh * 2 + c) * RES + to_yl * NZ + z
                        pairs.append((source, target))
    return pairs


def standardize_features(source, scale, offset):
    values_f = source.astype(jnp.float32)
    center = jnp.mean(values_f, axis=-1, keepdims=True)
    spread = jnp.mean((values_f - center) ** 2, axis=-1, keepdims=True)
    return (values_f - center) * lax.rsqrt(spread + 1e-05) * scale + offset


def normalize_kernel(features_ref, scale_ref, offset_ref, out_ref):
    for s in range(features_ref.shape[0]):
        out_ref[s] = standardize_features(
            features_ref[s], scale_ref[...], offset_ref[...]
        ).astype(jnp.bfloat16)


def normalize(features, scale, offset):
    return pl.pallas_call(
        normalize_kernel,
        out_shape=jax.ShapeDtypeStruct(features.shape, jnp.bfloat16),
        name="normalize",
    )(features, scale, offset)


def prepare_kernel(
    normed_ref, partner_ref, scale_ref, offset_ref, query_w_ref, key_w_ref, gate_w_ref, gate_off_ref,
    query_ref, gate_ref,
):
    depth, span, width = normed_ref.shape
    key_wt = key_w_ref[...].astype(jnp.float32).T.astype(jnp.bfloat16)
    head_of_lane = lax.broadcasted_iota(jnp.int32, (span, HALF), 1) // DH
    for s in range(depth):
        own = normed_ref[s]
        other = standardize_features(partner_ref[s], scale_ref[...], offset_ref[...]).astype(
            jnp.bfloat16
        )
        for r, rows in enumerate((other, own)):
            query = jnp.dot(rows, query_w_ref[...], preferred_element_type=jnp.float32)
            query = query * (LOG2E / DH**0.5)
            for g in range(2):
                lanes = slice(g * HALF, (g + 1) * HALF)
                spread = jnp.concatenate(
                    [jnp.where(head_of_lane == h, query[:, lanes], 0.0) for h in range(GROUP)],
                    axis=0,
                ).astype(jnp.bfloat16)
                query_ref[r, g, s] = jnp.dot(
                    spread, key_wt[lanes], preferred_element_type=jnp.float32
                ).astype(jnp.bfloat16)
        gate_ref[s] = jax.nn.sigmoid(
            jnp.dot(own, gate_w_ref[...], preferred_element_type=jnp.float32) + gate_off_ref[...]
        )


def prepare(normed, partner, scale, offset, query_w, key_w, gate_w, gate_off):
    depth, span, width = normed.shape
    return pl.pallas_call(
        prepare_kernel,
        out_shape=[
            jax.ShapeDtypeStruct((2, 2, depth, GROUP * span, width), jnp.bfloat16),
            jax.ShapeDtypeStruct((depth, span, width), jnp.float32),
        ],
        compiler_params=pltpu.CompilerParams(vmem_limit_bytes=24 * 1024 * 1024),
        name="prepare",
    )(normed, partner, scale, offset, query_w, key_w, gate_w, gate_off)


def attend_kernel(
    mask_ref, rows_ref, value_w_ref, query_ref, near0_ref, near1_ref, far0_ref, far1_ref,
    sent_ref, own_ref,
    table_ref, bias_ref, acc_ref, sum_ref, top_ref,
):
    blocks, depth, span, width = rows_ref.shape
    g, r = pl.program_id(0), pl.program_id(1)
    seq, res = lax.axis_index("seq"), lax.axis_index("res")
    x, yh, c = seq // 4, lax.rem(seq // 2, 2), lax.rem(seq, 2)
    half, z_own = res // NZ, lax.rem(res, NZ)
    yl = jnp.where(r == 0, 1 - half, half)

    def clear(i, carry):
        for row in range(3):
            table_ref[row, i] = 0
        return carry

    def place(z, count):
        slot = z // 8 + 2 * yl
        table_ref[0, count] = z
        table_ref[1, count] = lax.rem(z // 2, 2) ^ c
        table_ref[2, count] = 2 * lax.rem(x - 2 * half - slot + 8, 4) + (lax.rem(z // 4, 2) ^ yh)
        return count + jnp.where(mask_ref[yl * NZ + z_own, half * NZ + z] > 0, 1, 0)

    lax.fori_loop(0, blocks, clear, 0)
    live = lax.fori_loop(0, blocks, place, 0)

    def bias_of(i):
        is_far, turn = table_ref[1, i], table_ref[2, i]
        lanes = pl.ds(pl.multiple_of(lax.rem(table_ref[0, i], 2) * BLOCK, BLOCK), BLOCK)
        inner = lax.rem(turn, 4)
        near = jnp.where(turn < 4, near0_ref[inner, :, :, lanes], near1_ref[inner, :, :, lanes])
        far = jnp.where(turn < 4, far0_ref[inner, :, :, lanes], far1_ref[inner, :, :, lanes])
        bias = jnp.where(is_far > 0, far, near).astype(jnp.float32)
        return (bias * LOG2E).reshape(GROUP * span, BLOCK)

    acc_ref[...] = jnp.zeros_like(acc_ref)
    sum_ref[...] = jnp.zeros_like(sum_ref)

    def scores(s, rows):
        return lax.dot_general(
            query_ref[0, 0, s], rows, (((1,), (1,)), ((), ())), preferred_element_type=jnp.float32
        )

    def tile(start, size, partial):
        spots = [start + i for i in range(size)]
        z = [table_ref[0, i] for i in spots]
        for i in range(size):
            bias = bias_of(spots[i])
            if partial:
                bias = bias + jnp.where(spots[i] < live, 0.0, LOW)
            bias_ref[:, i * BLOCK : (i + 1) * BLOCK] = bias

        def weigh(s):
            rows = jnp.concatenate([rows_ref[i, s] for i in z], axis=0)
            weight = jnp.exp2(scores(s, rows) + bias_ref[:, : size * BLOCK])
            part = weight[:, :BLOCK]
            for i in range(1, size):
                part = part + weight[:, i * BLOCK : (i + 1) * BLOCK]
            sum_ref[s] += part
            return weight.astype(jnp.bfloat16)

        def add(s, weight):
            rows = jnp.concatenate([rows_ref[i, s] for i in z], axis=0)
            acc_ref[s] += jnp.dot(weight, rows, preferred_element_type=jnp.float32)

        weight = weigh(0)
        for s in range(1, depth):
            later = weigh(s)
            add(s - 1, weight)
            weight = later
        add(depth - 1, weight)

    def full(t, carry):
        tile(TILE * t, TILE, False)
        return carry

    rest = lax.rem(live, TILE)
    lax.fori_loop(0, live // TILE, full, 0)

    @pl.when(rest > 2)
    def _():
        tile(live - rest, TILE, True)

    @pl.when((rest > 0) & (rest <= 2))
    def _():
        tile(live - rest, 2, True)

    largest, least = 0.0, SAFE_HIGH
    for s in range(depth):
        total = jnp.sum(sum_ref[s], axis=1, keepdims=True)
        sum_ref[s] = jnp.broadcast_to(total, (GROUP * span, BLOCK))
        largest = jnp.maximum(largest, jnp.max(total))
        least = jnp.minimum(least, jnp.min(total))
        top_ref[s] = jnp.zeros_like(total)
    bad = (live > 0) & ((largest > SAFE_HIGH) | (least < SAFE_LOW))

    @pl.when(bad)
    def _():
        top_ref[...] = jnp.full_like(top_ref, LOW)
        acc_ref[...] = jnp.zeros_like(acc_ref)
        sum_ref[...] = jnp.zeros_like(sum_ref)

        def careful(t, carry):
            z = table_ref[0, t]
            bias_ref[:, :BLOCK] = bias_of(t)

            def one(s, inner):
                score = scores(s, rows_ref[z, s]) + bias_ref[:, :BLOCK]
                old = top_ref[s]
                top = jnp.maximum(old, jnp.max(score, axis=1, keepdims=True))
                top_ref[s] = top
                weight = jnp.exp2(score - top)
                shrink = jnp.exp2(old - top)
                sum_ref[s] = sum_ref[s] * shrink + jnp.sum(weight, axis=1, keepdims=True)
                acc_ref[s] = acc_ref[s] * shrink + jnp.dot(
                    weight.astype(jnp.bfloat16), rows_ref[z, s], preferred_element_type=jnp.float32
                )
                return inner

            return lax.fori_loop(0, depth, one, carry)

        lax.fori_loop(0, live, careful, 0)

    head_of_lane = lax.broadcasted_iota(jnp.int32, (span, HALF), 1) // DH
    for s in range(depth):
        total = sum_ref[s]
        some = total > 0.0
        safe = jnp.where(some, total, 1.0)
        lse = jnp.where(some, top_ref[s] + jnp.log2(safe), LOW)
        inverse = 1.0 / safe
        mixed = (acc_ref[s] * jnp.concatenate([inverse, inverse], axis=1)).astype(jnp.bfloat16)
        values = jnp.dot(mixed, value_w_ref[...], preferred_element_type=jnp.float32)
        mean = values[:span]
        wide = lse[:span]
        for h in range(1, GROUP):
            part = slice(h * span, (h + 1) * span)
            mean = jnp.where(head_of_lane == h, values[part], mean)
            wide = jnp.where(head_of_lane == h, lse[part], wide)
        wide = wide.T
        lse = jnp.concatenate([wide[h * DH : h * DH + 1] for h in range(GROUP)], axis=0)

        @pl.when(r == 0)
        def _():
            first = lse.astype(jnp.bfloat16).astype(jnp.float32)
            second = (lse - first).astype(jnp.bfloat16).astype(jnp.float32)
            third = lse - first - second
            sent_ref[s, :span] = mean.astype(jnp.bfloat16)
            sent_ref[s, span:] = jnp.concatenate(
                [first, second, third, jnp.zeros_like(lse)], axis=0
            ).astype(jnp.bfloat16)

        @pl.when(r == 1)
        def _():
            own_ref[s, :span] = mean
            own_ref[s, span:] = jnp.concatenate([lse, jnp.zeros_like(lse)], axis=0)


def attend(mask, rows, value_w, queries, near0, near1, far0, far1):
    blocks, depth, span, width = rows.shape
    turns = near0.shape[0]
    bias = pl.BlockSpec((turns, GROUP, span, 2 * BLOCK), lambda g, r: (0, g, 0, 0))
    by_group = lambda g, r: (0, 0, g)
    return pl.pallas_call(
        attend_kernel,
        grid=(2, 2),
        in_specs=[
            pl.BlockSpec(memory_space=pltpu.SMEM),
            pl.BlockSpec(
                (blocks, depth, span, width),
                lambda g, r: (0, 0, 0, 0),
                pipeline_mode=pl.Buffered(1),
            ),
            pl.BlockSpec((width, HALF), lambda g, r: (0, g)),
            pl.BlockSpec((1, 1, depth, GROUP * span, width), lambda g, r: (r, g, 0, 0, 0)),
            bias,
            bias,
            bias,
            bias,
        ],
        out_specs=[
            pl.BlockSpec((depth, span + EXTRA, HALF), by_group),
            pl.BlockSpec((depth, span + 8, HALF), by_group),
        ],
        out_shape=[
            jax.ShapeDtypeStruct((depth, span + EXTRA, width), jnp.bfloat16),
            jax.ShapeDtypeStruct((depth, span + 8, width), jnp.float32),
        ],
        scratch_shapes=[
            pltpu.SMEM((3, blocks), jnp.int32),
            pltpu.VMEM((GROUP * span, TILE * BLOCK), jnp.float32),
            pltpu.VMEM((depth, GROUP * span, width), jnp.float32),
            pltpu.VMEM((depth, GROUP * span, BLOCK), jnp.float32),
            pltpu.VMEM((depth, GROUP * span, 1), jnp.float32),
        ],
        compiler_params=pltpu.CompilerParams(vmem_limit_bytes=32 * 1024 * 1024),
        name="attend",
    )(mask, rows, value_w, queries, near0, near1, far0, far1)


def finish_kernel(own_ref, got_ref, gate_ref, out_w_ref, out_off_ref, out_ref):
    depth, span, width = gate_ref.shape

    def widen(part):
        return jnp.broadcast_to(part[:, None, :], (GROUP, DH, span)).reshape(HALF, span).T

    for s in range(depth):
        gated = []
        for g in range(2):
            lanes = slice(g * HALF, (g + 1) * HALF)
            own_lse = own_ref[s, span : span + GROUP, lanes]
            pieces = got_ref[s, span:, lanes].astype(jnp.float32)
            got_lse = pieces[:GROUP] + pieces[GROUP : 2 * GROUP] + pieces[2 * GROUP : 3 * GROUP]
            own_part = widen(1.0 / (1.0 + jnp.exp2(got_lse - own_lse)))
            got_part = widen(1.0 / (1.0 + jnp.exp2(own_lse - got_lse)))
            attended = (
                own_ref[s, :span, lanes] * own_part
                + got_ref[s, :span, lanes].astype(jnp.float32) * got_part
            )
            gated.append((gate_ref[s, :, lanes] * attended).astype(jnp.bfloat16))
        result = jnp.dot(
            jnp.concatenate(gated, axis=1), out_w_ref[...], preferred_element_type=jnp.float32
        )
        out_ref[s] = (result + out_off_ref[...]).astype(jnp.bfloat16)


def finish(own, got, gate, out_w, out_off):
    return pl.pallas_call(
        finish_kernel,
        out_shape=jax.ShapeDtypeStruct(gate.shape, jnp.bfloat16),
        name="finish",
    )(own, got, gate, out_w, out_off)


def on_device(
    alignment_features,
    coupling_logit_offset,
    contact_tile_filter,
    standard_scale_array,
    standard_offset_array,
    probe_projection,
    lookup_projection,
    content_projection,
    sigmoid_projection,
    sigmoid_offset_array,
    result_projection,
    result_offset,
):
    scale, offset = standard_scale_array[None, :], standard_offset_array[None, :]
    partner = lax.ppermute(alignment_features, "res", YL_PAIRS)
    normed = normalize(alignment_features, scale, offset)
    gathered = lax.all_gather(normed, "res", axis_index_groups=Z_GROUPS)

    def rounds(bias, turns):
        return jnp.stack(
            [
                lax.ppermute(bias, ("seq", "res"), bias_pairs(u, v))
                for u in turns
                for v in range(2)
            ]
        )

    near0 = rounds(coupling_logit_offset, (0, 1))
    far0 = lax.ppermute(near0, "seq", C_PAIRS)
    later_bias, partner = lax.optimization_barrier((coupling_logit_offset, partner))
    near1 = rounds(later_bias, (2, 3))
    queries, gate = prepare(
        normed, partner, scale, offset, probe_projection, lookup_projection, sigmoid_projection,
        sigmoid_offset_array[None, :],
    )
    near1, queries, gate = lax.optimization_barrier((near1, queries, gate))
    far1 = lax.ppermute(near1, "seq", C_PAIRS)
    sent, own = attend(
        contact_tile_filter, gathered, content_projection, queries, near0, near1, far0, far1
    )
    got = lax.ppermute(sent, "res", YL_PAIRS)
    return finish(own, got, gate, result_projection, result_offset[None, :])


def solution(mesh):
    return jax.shard_map(
        on_device,
        mesh=mesh,
        in_specs=(
            P("seq", "res", None),
            P(None, "res", "seq"),
            P(),
            P(),
            P(),
            P(),
            P(),
            P(),
            P(),
            P(),
            P(),
            P(),
        ),
        out_specs=P("seq", "res", None),
        check_vma=False,
    )
```

time: 234 us -> 326 us (1.39)
  the two profiles are of different devices: /device:TPU:184 before, /device:TPU:390 now
where the time goes in v3:
time: 326 us; the launch traced here: 325 us
  Pallas kernels  191 us (59%)
  waiting for transfers between devices  58.8 us (18%)
  starting transfers between devices  38.6 us (12%)
  local copies, waits for them, and re-layouts  22.6 us (7%)
  between operations  13.6 us (4%)
    pallas_call x1, Pallas kernels, attend(): pl.pallas_call(attend_kernel, grid=(2, 2), in_specs=[pl.BlockSpec(memory_...  184 us
    ppermute x8, starting transfers between devices, rounds(): lax.ppermute(bias, ('seq', 'res'), bias_pairs(u, v))  30.2 us
    ppermute x8, waiting for transfers between devices, rounds(): lax.ppermute(bias, ('seq', 'res'), bias_pairs(u, v))  29.9 us
    unnamed x42, local copies, waits for them, and re-layouts  22.6 us
    ppermute x1, waiting for transfers between devices, on_device(): partner = lax.ppermute(alignment_features, 'res', YL_PAIRS)  18.4 us
    ppermute x1, waiting for transfers between devices, on_device(): got = lax.ppermute(sent, 'res', YL_PAIRS)  9.01 us
  transfers between devices with their start and end apart: 13, of which 7 were waited for; matrix products, arithmetic and copies ran while one was open for 0% of the time, Pallas kernels for 1%

profile of v3, /device:TPU:390, one launch (start us, length us, event | category | flops | bytes accessed | tf_op | source)
XLA Modules:
  0.0 325.3 jit_solution(5513952949204326837)
XLA Ops:
  6.5 1.9 normalize.1.normed_ref
  8.5 4.9 %collective-permute-start.6 = (bf16[8,128,256]{2,1,0:T(8,128)(2,1)}, bf16[8,128,256]{2,1,0:T(8,128)(2,1)S(1)}, u32[]{:S(2)}, u32[]{:S(2)}) collective-permute-start(bf16[8,128,256]{2,1,0:T(8,128)(2,1)} %param.13), channel_id=1, source_target_pairs={{0,64},{1,65},{2,66},{3,67},{4,68},{5,69},{6,70},{7,71},{8,72},{9,... | collective-permute-start | bytes 1572872 | tf_op jit(solution)/shard_map/ppermute | solution.py:361
  13.4 3.6 %collective-permute-start.5 = (bf16[8,128,256]{2,1,0:T(8,128)(2,1)}, bf16[8,128,256]{2,1,0:T(8,128)(2,1)S(1)}, u32[]{:S(2)}, u32[]{:S(2)}) collective-permute-start(bf16[8,128,256]{2,1,0:T(8,128)(2,1)} %param.13), channel_id=1, source_target_pairs={{0,0},{1,1},{2,2},{3,3},{4,4},{5,5},{6,6},{7,7},{8,8},{9,9},{10,10... | collective-permute-start | bytes 1572872 | tf_op jit(solution)/shard_map/ppermute | solution.py:361
  17.0 3.8 %collective-permute-start.8 = (bf16[8,128,256]{2,1,0:T(8,128)(2,1)}, bf16[8,128,256]{2,1,0:T(8,128)(2,1)S(1)}, u32[]{:S(2)}, u32[]{:S(2)}) collective-permute-start(bf16[8,128,256]{2,1,0:T(8,128)(2,1)} %param.13), channel_id=1, source_target_pairs={{0,192},{1,193},{2,194},{3,195},{4,196},{5,197},{6,198},{7,199},{8... | collective-permute-start | bytes 1572872 | tf_op jit(solution)/shard_map/ppermute | solution.py:361
  20.8 2.7 collective-permute-start
  23.5 3.2 collective-permute-start.7
  26.7 18.4 %collective-permute-done.partner_ref = bf16[4,128,256]{2,1,0:T(8,128)(2,1)S(1)} collective-permute-done((bf16[4,128,256]{2,1,0:T(8,128)(2,1)}, bf16[4,128,256]{2,1,0:T(8,128)(2,1)S(1)}, u32[]{:S(2)}, u32[]{:S(2)}) %collective-permute-start) | collective-permute-done | bytes 262176 | tf_op jit(solution)/shard_map/ppermute | solution.py:354
  45.1 4.0 %collective-permute-start.4 = (bf16[8,128,256]{2,1,0:T(8,128)(2,1)}, bf16[8,128,256]{2,1,0:T(8,128)(2,1)S(1)}, u32[]{:S(2)}, u32[]{:S(2)}) collective-permute-start(bf16[8,128,256]{2,1,0:T(8,128)(2,1)} %param.13), channel_id=1, source_target_pairs={{0,448},{1,449},{2,450},{3,451},{4,452},{5,453},{6,454},{7,455},{8... | collective-permute-start | bytes 1572872 | tf_op jit(solution)/shard_map/ppermute | solution.py:361
  49.1 5.6 %collective-permute-start.3 = (bf16[8,128,256]{2,1,0:T(8,128)(2,1)}, bf16[8,128,256]{2,1,0:T(8,128)(2,1)S(1)}, u32[]{:S(2)}, u32[]{:S(2)}) collective-permute-start(bf16[8,128,256]{2,1,0:T(8,128)(2,1)} %param.13), channel_id=1, source_target_pairs={{0,384},{1,385},{2,386},{3,387},{4,388},{5,389},{6,390},{7,391},{8... | collective-permute-start | bytes 1572872 | tf_op jit(solution)/shard_map/ppermute | solution.py:361
  54.8 1.9 collective-permute-start.2
  56.7 3.1 collective-permute-start.1
  65.6 2.5 prepare.1
  70.9 1.9 collective-permute-start.9
  72.9 8.8 %collective-permute-done.3 = bf16[8,128,256]{2,1,0:T(8,128)(2,1)S(1)} collective-permute-done((bf16[8,128,256]{2,1,0:T(8,128)(2,1)}, bf16[8,128,256]{2,1,0:T(8,128)(2,1)S(1)}, u32[]{:S(2)}, u32[]{:S(2)}) %collective-permute-start.3) | collective-permute-done | bytes 524320 | tf_op jit(solution)/shard_map/ppermute | solution.py:361
  81.6 11.2 %collective-permute-done.2 = bf16[8,128,256]{2,1,0:T(8,128)(2,1)S(1)} collective-permute-done((bf16[8,128,256]{2,1,0:T(8,128)(2,1)}, bf16[8,128,256]{2,1,0:T(8,128)(2,1)S(1)}, u32[]{:S(2)}, u32[]{:S(2)}) %collective-permute-start.2) | collective-permute-done | bytes 524320 | tf_op jit(solution)/shard_map/ppermute | solution.py:361
  92.8 9.6 %collective-permute-done.1 = bf16[8,128,256]{2,1,0:T(8,128)(2,1)S(1)} collective-permute-done((bf16[8,128,256]{2,1,0:T(8,128)(2,1)}, bf16[8,128,256]{2,1,0:T(8,128)(2,1)S(1)}, u32[]{:S(2)}, u32[]{:S(2)}) %collective-permute-start.1) | collective-permute-done | bytes 524320 | tf_op jit(solution)/shard_map/ppermute | solution.py:361
  102.7 1.9 collective-permute-start.10
  111.7 2.2 copy-done.2
  113.9 2.2 copy-done.4
  116.1 1.6 copy-done.7
  119.3 184.1 %attend.1 = (bf16[4,144,256]{2,1,0:T(8,128)(2,1)S(1)}, f32[4,136,256]{2,1,0:T(8,128)S(1)}) custom-call(s32[32,32]{1,0:T(8,128)S(1)} %copy-done.16, bf16[16,4,128,256]{3,2,1,0:T(8,128)(2,1)S(1)} %bitcast.13, bf16[256,256]{1,0:T(8,128)(2,1)S(1)} %copy-done.12, bf16[2,2,4,512,256]{4,3,2,1,0:T(8,128)(2,1)S(1)} %copy-done.4, ...), custom_call_target="tpu_custom_call" | custom-call | tf_op jit(solution)/shard_map/attend/pallas_call | solution.py:268
  304.2 1.9 collective-permute-start.11
  306.1 9.0 %collective-permute-done.11.got_ref = bf16[4,144,256]{2,1,0:T(8,128)(2,1)S(1)} collective-permute-done((bf16[4,144,256]{2,1,0:T(8,128)(2,1)S(1)}, bf16[4,144,256]{2,1,0:T(8,128)(2,1)S(1)}, u32[]{:S(2)}, u32[]{:S(2)}) %collective-permute-start.11) | collective-permute-done | bytes 294944 | tf_op jit(solution)/shard_map/ppermute | solution.py:380
  315.8 2.6 finish.1
  (51 shorter events, 19.0 us)
Async XLA Ops:
  6.5 103.6 %all-gather.3.cloned.1.call-start = ((), (), s32[]{:S(2)}) async-start(), calls=%async_computation | async-start | bytes 4456448 | tf_op jit(solution)/shard_map/all_gather | solution.py:356
  8.5 40.6 %collective-permute-start.6 = (bf16[8,128,256]{2,1,0:T(8,128)(2,1)}, bf16[8,128,256]{2,1,0:T(8,128)(2,1)S(1)}, u32[]{:S(2)}, u32[]{:S(2)}) collective-permute-start(bf16[8,128,256]{2,1,0:T(8,128)(2,1)} %param.13), channel_id=1, source_target_pairs={{0,64},{1,65},{2,66},{3,67},{4,68},{5,69},{6,70},{7,71},{8,72},{9,... | collective-permute-start | bytes 1572872 | tf_op jit(solution)/shard_map/ppermute | solution.py:361
  13.4 41.3 %collective-permute-start.5 = (bf16[8,128,256]{2,1,0:T(8,128)(2,1)}, bf16[8,128,256]{2,1,0:T(8,128)(2,1)S(1)}, u32[]{:S(2)}, u32[]{:S(2)}) collective-permute-start(bf16[8,128,256]{2,1,0:T(8,128)(2,1)} %param.13), channel_id=1, source_target_pairs={{0,0},{1,1},{2,2},{3,3},{4,4},{5,5},{6,6},{7,7},{8,8},{9,9},{10,10... | collective-permute-start | bytes 1572872 | tf_op jit(solution)/shard_map/ppermute | solution.py:361
  17.0 39.7 %collective-permute-start.8 = (bf16[8,128,256]{2,1,0:T(8,128)(2,1)}, bf16[8,128,256]{2,1,0:T(8,128)(2,1)S(1)}, u32[]{:S(2)}, u32[]{:S(2)}) collective-permute-start(bf16[8,128,256]{2,1,0:T(8,128)(2,1)} %param.13), channel_id=1, source_target_pairs={{0,192},{1,193},{2,194},{3,195},{4,196},{5,197},{6,198},{7,199},{8... | collective-permute-start | bytes 1572872 | tf_op jit(solution)/shard_map/ppermute | solution.py:361
  20.8 24.3 %collective-permute-start = (bf16[4,128,256]{2,1,0:T(8,128)(2,1)}, bf16[4,128,256]{2,1,0:T(8,128)(2,1)S(1)}, u32[]{:S(2)}, u32[]{:S(2)}) collective-permute-start(bf16[4,128,256]{2,1,0:T(8,128)(2,1)} %features_ref.1), channel_id=1, source_target_pairs={{0,16},{1,17},{2,18},{3,19},{4,20},{5,21},{6,22},{7,23},{8,24},{9,... | collective-permute-start | bytes 786440 | tf_op jit(solution)/shard_map/ppermute | solution.py:354
  23.5 45.8 %collective-permute-start.7 = (bf16[8,128,256]{2,1,0:T(8,128)(2,1)}, bf16[8,128,256]{2,1,0:T(8,128)(2,1)S(1)}, u32[]{:S(2)}, u32[]{:S(2)}) collective-permute-start(bf16[8,128,256]{2,1,0:T(8,128)(2,1)} %param.13), channel_id=1, source_target_pairs={{0,128},{1,129},{2,130},{3,131},{4,132},{5,133},{6,134},{7,135},{8... | collective-permute-start | bytes 1572872 | tf_op jit(solution)/shard_map/ppermute | solution.py:361
  45.1 27.8 %collective-permute-start.4 = (bf16[8,128,256]{2,1,0:T(8,128)(2,1)}, bf16[8,128,256]{2,1,0:T(8,128)(2,1)S(1)}, u32[]{:S(2)}, u32[]{:S(2)}) collective-permute-start(bf16[8,128,256]{2,1,0:T(8,128)(2,1)} %param.13), channel_id=1, source_target_pairs={{0,448},{1,449},{2,450},{3,451},{4,452},{5,453},{6,454},{7,455},{8... | collective-permute-start | bytes 1572872 | tf_op jit(solution)/shard_map/ppermute | solution.py:361
  49.1 32.5 %collective-permute-start.3 = (bf16[8,128,256]{2,1,0:T(8,128)(2,1)}, bf16[8,128,256]{2,1,0:T(8,128)(2,1)S(1)}, u32[]{:S(2)}, u32[]{:S(2)}) collective-permute-start(bf16[8,128,256]{2,1,0:T(8,128)(2,1)} %param.13), channel_id=1, source_target_pairs={{0,384},{1,385},{2,386},{3,387},{4,388},{5,389},{6,390},{7,391},{8... | collective-permute-start | bytes 1572872 | tf_op jit(solution)/shard_map/ppermute | solution.py:361
  54.8 38.1 %collective-permute-start.2 = (bf16[8,128,256]{2,1,0:T(8,128)(2,1)}, bf16[8,128,256]{2,1,0:T(8,128)(2,1)S(1)}, u32[]{:S(2)}, u32[]{:S(2)}) collective-permute-start(bf16[8,128,256]{2,1,0:T(8,128)(2,1)} %param.13), channel_id=1, source_target_pairs={{0,320},{1,321},{2,322},{3,323},{4,324},{5,325},{6,326},{7,327},{8... | collective-permute-start | bytes 1572872 | tf_op jit(solution)/shard_map/ppermute | solution.py:361
  56.7 45.7 %collective-permute-start.1 = (bf16[8,128,256]{2,1,0:T(8,128)(2,1)}, bf16[8,128,256]{2,1,0:T(8,128)(2,1)S(1)}, u32[]{:S(2)}, u32[]{:S(2)}) collective-permute-start(bf16[8,128,256]{2,1,0:T(8,128)(2,1)} %param.13), channel_id=1, source_target_pairs={{0,256},{1,257},{2,258},{3,259},{4,260},{5,261},{6,262},{7,263},{8... | collective-permute-start | bytes 1572872 | tf_op jit(solution)/shard_map/ppermute | solution.py:361
  68.9 2.0 copy-start.3
  70.9 35.0 %collective-permute-start.9 = (bf16[4,8,128,256]{3,2,1,0:T(8,128)(2,1)S(1)}, bf16[4,8,128,256]{3,2,1,0:T(8,128)(2,1)S(1)}, u32[]{:S(2)}, u32[]{:S(2)}) collective-permute-start(bf16[4,8,128,256]{3,2,1,0:T(8,128)(2,1)S(1)} %pad_maximum_fusion.1.near0_ref), channel_id=1, source_target_pairs={{0,32},{32,0},{64,96},{96,64},{128,160},{160,128},{192,224},{224,1... | collective-permute-start | bytes 6291464 | tf_op jit(solution)/shard_map/ppermute | solution.py:368
  102.4 7.7 %copy-start.12 = (bf16[256,256]{1,0:T(8,128)(2,1)S(1)}, bf16[256,256]{1,0:T(8,128)(2,1)}, u32[]{:S(2)}) copy-start(bf16[256,256]{1,0:T(8,128)(2,1)} %value_w_ref.1) | copy-start | bytes 393220
  102.4 7.7 %copy-start.16 = (s32[32,32]{1,0:T(8,128)S(1)}, s32[32,32]{1,0:T(8,128)}, u32[]{:S(2)}) copy-start(s32[32,32]{1,0:T(8,128)} %mask_ref.1) | copy-start | bytes 12292
  102.7 6.1 %collective-permute-start.10 = (bf16[4,8,128,256]{3,2,1,0:T(8,128)(2,1)S(1)}, bf16[4,8,128,256]{3,2,1,0:T(8,128)(2,1)S(1)}, u32[]{:S(2)}, u32[]{:S(2)}) collective-permute-start(bf16[4,8,128,256]{3,2,1,0:T(8,128)(2,1)S(1)} %pad_maximum_fusion.near1_ref), channel_id=1, source_target_pairs={{0,32},{32,0},{64,96},{96,64},{128,160},{160,128},{192,224},{224,1... | collective-permute-start | bytes 6291464 | tf_op jit(solution)/shard_map/ppermute | solution.py:376
  104.6 1.3 copy-start
  105.9 1.4 copy-start.6
  108.7 1.4 copy-start.8
  110.1 1.6 copy-start.1
  111.7 2.2 copy-start.2
  113.9 2.2 copy-start.4
  116.1 1.6 copy-start.7
  117.7 1.6 copy-start.9
  304.2 10.9 %collective-permute-start.11 = (bf16[4,144,256]{2,1,0:T(8,128)(2,1)S(1)}, bf16[4,144,256]{2,1,0:T(8,128)(2,1)S(1)}, u32[]{:S(2)}, u32[]{:S(2)}) collective-permute-start(bf16[4,144,256]{2,1,0:T(8,128)(2,1)S(1)} %get-tuple-element.21), channel_id=1, source_target_pairs={{0,16},{1,17},{2,18},{3,19},{4,20},{5,21},{6,22},{7,23},{8,24},{9,... | collective-permute-start | bytes 884744 | tf_op jit(solution)/shard_map/ppermute | solution.py:380
  (10 other events, 8.1 us)
Sparse Core Ops, SparseCore 0:
  9.4 75.4 all-gather.2

commit v4 on v3

--- a/solution.py
+++ b/solution.py
@@ -22,19 +22,19 @@
 Z_GROUPS = [[yl * NZ + z for z in range(NZ)] for yl in range(2)]
 YL_PAIRS = [(r, (r + NZ) % RES) for r in range(RES)]
 C_PAIRS = [(s, s ^ 1) for s in range(SEQ)]
-
-
-def bias_pairs(u, v):
+PLANE_GROUPS = [[2 * k + c for k in range(SEQ // 2)] for c in range(2)]
+
+
+def swap_pairs():
     pairs = []
     for x in range(4):
-        for yh in range(2):
-            for c in range(2):
-                for yl in range(2):
-                    for z in range(NZ):
-                        to_x, to_yh, to_yl = (x + 2 * yl + u) % 4, yh ^ v, x // 2
-                        source = (x * 4 + yh * 2 + c) * RES + yl * NZ + z
-                        target = (to_x * 4 + to_yh * 2 + c) * RES + to_yl * NZ + z
-                        pairs.append((source, target))
+        for other in range(4):
+            for yl in range(2):
+                for z in range(NZ):
+                    to_x, to_yl = (x, yl) if yl == x // 2 else ((x + 2) % 4, 1 - yl)
+                    source = (x * 4 + other) * RES + yl * NZ + z
+                    target = (to_x * 4 + other) * RES + to_yl * NZ + z
+                    pairs.append((source, target))
     return pairs
 
 
@@ -56,6 +56,7 @@
     return pl.pallas_call(
         normalize_kernel,
         out_shape=jax.ShapeDtypeStruct(features.shape, jnp.bfloat16),
+        cost_estimate=pl.CostEstimate(flops=1000, bytes_accessed=1000, transcendentals=0),
         name="normalize",
     )(features, scale, offset)
 
@@ -98,20 +99,20 @@
             jax.ShapeDtypeStruct((depth, span, width), jnp.float32),
         ],
         compiler_params=pltpu.CompilerParams(vmem_limit_bytes=24 * 1024 * 1024),
+        cost_estimate=pl.CostEstimate(flops=1000, bytes_accessed=1000, transcendentals=0),
         name="prepare",
     )(normed, partner, scale, offset, query_w, key_w, gate_w, gate_off)
 
 
 def attend_kernel(
-    mask_ref, rows_ref, value_w_ref, query_ref, near0_ref, near1_ref, far0_ref, far1_ref,
+    mask_ref, rows_ref, value_w_ref, query_ref, near_ref, far_ref,
     sent_ref, own_ref,
     table_ref, bias_ref, acc_ref, sum_ref, top_ref,
 ):
     blocks, depth, span, width = rows_ref.shape
     g, r = pl.program_id(0), pl.program_id(1)
     seq, res = lax.axis_index("seq"), lax.axis_index("res")
-    x, yh, c = seq // 4, lax.rem(seq // 2, 2), lax.rem(seq, 2)
-    half, z_own = res // NZ, lax.rem(res, NZ)
+    c, half, z_own = lax.rem(seq, 2), res // NZ, lax.rem(res, NZ)
     yl = jnp.where(r == 0, 1 - half, half)
 
     def clear(i, carry):
@@ -120,10 +121,10 @@
         return carry
 
     def place(z, count):
-        slot = z // 8 + 2 * yl
+        holder = lax.rem(2 * half + z // 8 + jnp.where(r == 0, 2, 0), 4)
         table_ref[0, count] = z
         table_ref[1, count] = lax.rem(z // 2, 2) ^ c
-        table_ref[2, count] = 2 * lax.rem(x - 2 * half - slot + 8, 4) + (lax.rem(z // 4, 2) ^ yh)
+        table_ref[2, count] = 2 * holder + lax.rem(z // 4, 2)
         return count + jnp.where(mask_ref[yl * NZ + z_own, half * NZ + z] > 0, 1, 0)
 
     lax.fori_loop(0, blocks, clear, 0)
@@ -132,10 +133,9 @@
     def bias_of(i):
         is_far, turn = table_ref[1, i], table_ref[2, i]
         lanes = pl.ds(pl.multiple_of(lax.rem(table_ref[0, i], 2) * BLOCK, BLOCK), BLOCK)
-        inner = lax.rem(turn, 4)
-        near = jnp.where(turn < 4, near0_ref[inner, :, :, lanes], near1_ref[inner, :, :, lanes])
-        far = jnp.where(turn < 4, far0_ref[inner, :, :, lanes], far1_ref[inner, :, :, lanes])
-        bias = jnp.where(is_far > 0, far, near).astype(jnp.float32)
+        bias = jnp.where(
+            is_far > 0, far_ref[turn, :, :, lanes], near_ref[turn, :, :, lanes]
+        ).astype(jnp.float32)
         return (bias * LOG2E).reshape(GROUP * span, BLOCK)
 
     acc_ref[...] = jnp.zeros_like(acc_ref)
@@ -260,9 +260,9 @@
             own_ref[s, span:] = jnp.concatenate([lse, jnp.zeros_like(lse)], axis=0)
 
 
-def attend(mask, rows, value_w, queries, near0, near1, far0, far1):
+def attend(mask, rows, value_w, queries, near, far):
     blocks, depth, span, width = rows.shape
-    turns = near0.shape[0]
+    turns = near.shape[0]
     bias = pl.BlockSpec((turns, GROUP, span, 2 * BLOCK), lambda g, r: (0, g, 0, 0))
     by_group = lambda g, r: (0, 0, g)
     return pl.pallas_call(
@@ -279,8 +279,6 @@
             pl.BlockSpec((1, 1, depth, GROUP * span, width), lambda g, r: (r, g, 0, 0, 0)),
             bias,
             bias,
-            bias,
-            bias,
         ],
         out_specs=[
             pl.BlockSpec((depth, span + EXTRA, HALF), by_group),
@@ -297,9 +295,9 @@
             pltpu.VMEM((depth, GROUP * span, BLOCK), jnp.float32),
             pltpu.VMEM((depth, GROUP * span, 1), jnp.float32),
         ],
-        compiler_params=pltpu.CompilerParams(vmem_limit_bytes=32 * 1024 * 1024),
+        compiler_params=pltpu.CompilerParams(vmem_limit_bytes=56 * 1024 * 1024),
         name="attend",
-    )(mask, rows, value_w, queries, near0, near1, far0, far1)
+    )(mask, rows, value_w, queries, near, far)
 
 
 def finish_kernel(own_ref, got_ref, gate_ref, out_w_ref, out_off_ref, out_ref):
@@ -355,28 +353,16 @@
     normed = normalize(alignment_features, scale, offset)
     gathered = lax.all_gather(normed, "res", axis_index_groups=Z_GROUPS)
 
-    def rounds(bias, turns):
-        return jnp.stack(
-            [
-                lax.ppermute(bias, ("seq", "res"), bias_pairs(u, v))
-                for u in turns
-                for v in range(2)
-            ]
-        )
-
-    near0 = rounds(coupling_logit_offset, (0, 1))
-    far0 = lax.ppermute(near0, "seq", C_PAIRS)
-    later_bias, partner = lax.optimization_barrier((coupling_logit_offset, partner))
-    near1 = rounds(later_bias, (2, 3))
+    swapped = lax.ppermute(coupling_logit_offset, ("seq", "res"), swap_pairs())
     queries, gate = prepare(
         normed, partner, scale, offset, probe_projection, lookup_projection, sigmoid_projection,
         sigmoid_offset_array[None, :],
     )
-    near1, queries, gate = lax.optimization_barrier((near1, queries, gate))
-    far1 = lax.ppermute(near1, "seq", C_PAIRS)
-    sent, own = attend(
-        contact_tile_filter, gathered, content_projection, queries, near0, near1, far0, far1
-    )
+    swapped, queries, gate = lax.optimization_barrier((swapped, queries, gate))
+    copies = jnp.broadcast_to(swapped[None], (SEQ // 2,) + swapped.shape)
+    near = lax.all_to_all(copies, "seq", 0, 0, axis_index_groups=PLANE_GROUPS, tiled=True)
+    far = lax.ppermute(near, "seq", C_PAIRS)
+    sent, own = attend(contact_tile_filter, gathered, content_projection, queries, near, far)
     got = lax.ppermute(sent, "res", YL_PAIRS)
     return finish(own, got, gate, result_projection, result_offset[None, :])
 

time: 326 us -> 315 us (0.966)
  the two profiles are of different devices: /device:TPU:390 before, /device:TPU:1 now
where the time goes in v4:
time: 315 us; the launch traced here: 314 us
  Pallas kernels  191 us (61%)
  blocking collectives  56.7 us (18%)
  waiting for transfers between devices  28.9 us (9%)
  starting transfers between devices  14.8 us (5%)
  between operations  13.5 us (4%)
  local copies, waits for them, and re-layouts  8.89 us (3%)
    pallas_call x1, Pallas kernels, attend(): pl.pallas_call(attend_kernel, grid=(2, 2), in_specs=[pl.BlockSpec(memory_...  184 us
    all_to_all x1, blocking collectives, on_device(): lax.all_to_all(copies, 'seq', 0, 0, axis_index_groups=PLANE_GROUPS, tiled...  56.7 us
    ppermute x1, waiting for transfers between devices, on_device(): partner = lax.ppermute(alignment_features, 'res', YL_PAIRS)  13.4 us
    ppermute x1, waiting for transfers between devices, on_device(): got = lax.ppermute(sent, 'res', YL_PAIRS)  8.39 us
    unnamed x20, local copies, waits for them, and re-layouts  8.39 us
    ppermute x1, waiting for transfers between devices, on_device(): far = lax.ppermute(near, 'seq', C_PAIRS)  7.08 us
    ppermute x1, starting transfers between devices, on_device(): partner = lax.ppermute(alignment_features, 'res', YL_PAIRS)  6.88 us
  transfers between devices with their start and end apart: 5, of which 3 were waited for; matrix products, arithmetic and copies ran while one was open for 0% of the time, Pallas kernels for 1%

profile of v4, /device:TPU:1, one launch (start us, length us, event | category | flops | bytes accessed | tf_op | source)
XLA Modules:
  0.0 314.1 jit_solution(17197879229086474619)
XLA Ops:
  6.5 1.7 collective-permute-start
  8.2 6.9 %collective-permute-start.1 = (bf16[4,128,256]{2,1,0:T(8,128)(2,1)}, bf16[4,128,256]{2,1,0:T(8,128)(2,1)S(1)}, u32[]{:S(2)}, u32[]{:S(2)}) collective-permute-start(bf16[4,128,256]{2,1,0:T(8,128)(2,1)} %features_ref.1), channel_id=1, source_target_pairs={{0,16},{1,17},{2,18},{3,19},{4,20},{5,21},{6,22},{7,23},{8,24},{9,... | collective-permute-start | bytes 786440 | tf_op jit(solution)/shard_map/ppermute | solution.py:352
  15.1 2.0 normalize.1.normed_ref
  17.1 0.0 all-gather.3.cloned.1.call-update
  17.1 13.4 %collective-permute-done.1.partner_ref = bf16[4,128,256]{2,1,0:T(8,128)(2,1)S(1)} collective-permute-done((bf16[4,128,256]{2,1,0:T(8,128)(2,1)}, bf16[4,128,256]{2,1,0:T(8,128)(2,1)S(1)}, u32[]{:S(2)}, u32[]{:S(2)}) %collective-permute-start.1) | collective-permute-done | bytes 262176 | tf_op jit(solution)/shard_map/ppermute | solution.py:352
  30.5 0.9 copy-done.1
  31.5 0.9 copy-done.3
  32.4 0.9 copy-done.4
  33.3 0.9 copy-done.5
  34.2 0.7 copy-done.6
  34.9 0.7 copy-done.7
  35.6 0.7 copy-done.8
  36.2 2.5 prepare.1
  38.8 2.0 copy-done
  40.7 0.5 broadcast_in_dim.21
  41.3 56.7 %all_to_all.5.near_ref = bf16[8,8,128,256]{3,2,1,0:T(8,128)(2,1)} all-to-all(bf16[8,8,128,256]{3,2,1,0:T(8,128)(2,1)S(1)} %broadcast_in_dim.21), channel_id=1, replica_groups={{0,64,128,192,256,320,384,448},{32,96,160,224,288,352,416,480},{1,65,12..., dimensions={0} | all-to-all | bytes 8388608 | tf_op jit(solution)/shard_map/all_to_all | solution.py:363
  98.0 4.3 %collective-permute-start.2 = (bf16[8,8,128,256]{3,2,1,0:T(8,128)(2,1)}, bf16[8,8,128,256]{3,2,1,0:T(8,128)(2,1)}, u32[]{:S(2)}, u32[]{:S(2)}) collective-permute-start(bf16[8,8,128,256]{3,2,1,0:T(8,128)(2,1)} %all_to_all.5.near_ref), channel_id=1, source_target_pairs={{0,32},{32,0},{64,96},{96,64},{128,160},{160,128},{192,224},{224,1... | collective-permute-start | bytes 12582920 | tf_op jit(solution)/shard_map/ppermute | solution.py:364
  102.2 0.0 all-gather.3.cloned.1.call-done
  102.3 7.1 %collective-permute-done.2.far_ref = bf16[8,8,128,256]{3,2,1,0:T(8,128)(2,1)} collective-permute-done((bf16[8,8,128,256]{3,2,1,0:T(8,128)(2,1)}, bf16[8,8,128,256]{3,2,1,0:T(8,128)(2,1)}, u32[]{:S(2)}, u32[]{:S(2)}) %collective-permute-start.2) | collective-permute-done | bytes 4194336 | tf_op jit(solution)/shard_map/ppermute | solution.py:364
  109.4 184.3 %attend.1 = (bf16[4,144,256]{2,1,0:T(8,128)(2,1)}, f32[4,136,256]{2,1,0:T(8,128)}) custom-call(s32[32,32]{1,0:T(8,128)} %mask_ref.1, bf16[16,4,128,256]{3,2,1,0:T(8,128)(2,1)} %bitcast.10, bf16[256,256]{1,0:T(8,128)(2,1)} %value_w_ref.1, bf16[2,2,4,512,256]{4,3,2,1,0:T(8,128)(2,1)} %copy-done, bf16[8,8,128,256]{3,2,1,0:T(8,128)(2,1)} %all_to_all.5.near_ref, ...), custom_call_target="tpu_custom_call" | custom-call | tf_op jit(solution)/shard_map/attend/pallas_call | solution.py:268
  293.7 1.9 collective-permute-start.3
  295.6 8.4 %collective-permute-done.3.got_ref = bf16[4,144,256]{2,1,0:T(8,128)(2,1)S(1)} collective-permute-done((bf16[4,144,256]{2,1,0:T(8,128)(2,1)}, bf16[4,144,256]{2,1,0:T(8,128)(2,1)S(1)}, u32[]{:S(2)}, u32[]{:S(2)}) %collective-permute-start.3) | collective-permute-done | bytes 294944 | tf_op jit(solution)/shard_map/ppermute | solution.py:366
  304.0 0.7 copy-done.9
  304.7 2.6 finish.1
  (13 shorter events, 0.0 us)
Async XLA Ops:
  6.5 95.7 %all-gather.3.cloned.1.call-start = ((), (), s32[]{:S(2)}) async-start(), calls=%async_computation.1 | async-start | bytes 4456448 | tf_op jit(solution)/shard_map/all_gather | solution.py:354
  6.5 34.2 %collective-permute-start = (bf16[8,128,256]{2,1,0:T(8,128)(2,1)}, bf16[8,128,256]{2,1,0:T(8,128)(2,1)S(1)}, u32[]{:S(2)}, u32[]{:S(2)}) collective-permute-start(bf16[8,128,256]{2,1,0:T(8,128)(2,1)} %param.13), channel_id=1, source_target_pairs={{0,0},{1,1},{2,2},{3,3},{4,4},{5,5},{6,6},{7,7},{8,8},{9,9},{10,10... | collective-permute-start | bytes 1572872 | tf_op jit(solution)/shard_map/ppermute | solution.py:356
  8.2 22.3 %collective-permute-start.1 = (bf16[4,128,256]{2,1,0:T(8,128)(2,1)}, bf16[4,128,256]{2,1,0:T(8,128)(2,1)S(1)}, u32[]{:S(2)}, u32[]{:S(2)}) collective-permute-start(bf16[4,128,256]{2,1,0:T(8,128)(2,1)} %features_ref.1), channel_id=1, source_target_pairs={{0,16},{1,17},{2,18},{3,19},{4,20},{5,21},{6,22},{7,23},{8,24},{9,... | collective-permute-start | bytes 786440 | tf_op jit(solution)/shard_map/ppermute | solution.py:352
  30.5 0.9 copy-start.1
  31.5 0.9 copy-start.3
  32.4 0.9 copy-start.4
  33.3 0.9 copy-start.5
  34.2 0.7 copy-start.6
  34.9 0.7 copy-start.7
  35.6 0.7 copy-start.8
  38.8 2.0 copy-start
  40.7 57.2 %copy-start.2 = (f32[4,128,256]{2,1,0:T(8,128)}, f32[4,128,256]{2,1,0:T(8,128)S(1)}, u32[]{:S(2)}) copy-start(f32[4,128,256]{2,1,0:T(8,128)S(1)} %get-tuple-element.18.gate_ref) | copy-start | bytes 1572868
  98.0 11.4 %collective-permute-start.2 = (bf16[8,8,128,256]{3,2,1,0:T(8,128)(2,1)}, bf16[8,8,128,256]{3,2,1,0:T(8,128)(2,1)}, u32[]{:S(2)}, u32[]{:S(2)}) collective-permute-start(bf16[8,8,128,256]{3,2,1,0:T(8,128)(2,1)} %all_to_all.5.near_ref), channel_id=1, source_target_pairs={{0,32},{32,0},{64,96},{96,64},{128,160},{160,128},{192,224},{224,1... | collective-permute-start | bytes 12582920 | tf_op jit(solution)/shard_map/ppermute | solution.py:364
  293.7 10.3 %collective-permute-start.3 = (bf16[4,144,256]{2,1,0:T(8,128)(2,1)}, bf16[4,144,256]{2,1,0:T(8,128)(2,1)S(1)}, u32[]{:S(2)}, u32[]{:S(2)}) collective-permute-start(bf16[4,144,256]{2,1,0:T(8,128)(2,1)} %get-tuple-element.17), channel_id=1, source_target_pairs={{0,16},{1,17},{2,18},{3,19},{4,20},{5,21},{6,22},{7,23},{8,24},{9,... | collective-permute-start | bytes 884744 | tf_op jit(solution)/shard_map/ppermute | solution.py:366
  304.0 0.7 copy-start.9
Sparse Core Ops, SparseCore 0:
  17.2 73.5 all-gather.2

commit v5 on v4

--- a/solution.py
+++ b/solution.py
@@ -105,38 +105,87 @@
 
 
 def attend_kernel(
-    mask_ref, rows_ref, value_w_ref, query_ref, near_ref, far_ref,
+    mask_ref, rows_hbm, value_w_ref, query_ref, near_hbm, far_hbm,
     sent_ref, own_ref,
-    table_ref, bias_ref, acc_ref, sum_ref, top_ref,
+    table_ref, live_ref, rows_ref, packed_ref, bias_ref, acc_ref, sum_ref, top_ref, row_sem, bias_sem,
 ):
     blocks, depth, span, width = rows_ref.shape
     g, r = pl.program_id(0), pl.program_id(1)
     seq, res = lax.axis_index("seq"), lax.axis_index("res")
     c, half, z_own = lax.rem(seq, 2), res // NZ, lax.rem(res, NZ)
-    yl = jnp.where(r == 0, 1 - half, half)
-
-    def clear(i, carry):
-        for row in range(3):
-            table_ref[row, i] = 0
-        return carry
-
-    def place(z, count):
-        holder = lax.rem(2 * half + z // 8 + jnp.where(r == 0, 2, 0), 4)
-        table_ref[0, count] = z
-        table_ref[1, count] = lax.rem(z // 2, 2) ^ c
-        table_ref[2, count] = 2 * holder + lax.rem(z // 4, 2)
-        return count + jnp.where(mask_ref[yl * NZ + z_own, half * NZ + z] > 0, 1, 0)
-
-    lax.fori_loop(0, blocks, clear, 0)
-    live = lax.fori_loop(0, blocks, place, 0)
-
-    def bias_of(i):
-        is_far, turn = table_ref[1, i], table_ref[2, i]
-        lanes = pl.ds(pl.multiple_of(lax.rem(table_ref[0, i], 2) * BLOCK, BLOCK), BLOCK)
-        bias = jnp.where(
-            is_far > 0, far_ref[turn, :, :, lanes], near_ref[turn, :, :, lanes]
-        ).astype(jnp.float32)
-        return (bias * LOG2E).reshape(GROUP * span, BLOCK)
+
+    def is_live(line, z):
+        yl = 1 - half if line == 0 else half
+        return mask_ref[yl * NZ + z_own, half * NZ + z] > 0
+
+    def row_copy(z):
+        return pltpu.make_async_copy(rows_hbm.at[z], rows_ref.at[z], row_sem.at[z])
+
+    def bias_copy(source, line, group, i, slot, spot):
+        lanes = pl.ds(pl.multiple_of(lax.rem(table_ref[line, 0, i], 2) * BLOCK, BLOCK), BLOCK)
+        heads = pl.ds(group * GROUP, GROUP)
+        return pltpu.make_async_copy(
+            source.at[table_ref[line, 2, i], heads, :, lanes],
+            packed_ref.at[slot, spot],
+            bias_sem.at[slot, spot],
+        )
+
+    def start_bias(line, group, i, slot, spot):
+        @pl.when(table_ref[line, 1, i] > 0)
+        def _():
+            bias_copy(far_hbm, line, group, i, slot, spot).start()
+
+        @pl.when(table_ref[line, 1, i] == 0)
+        def _():
+            bias_copy(near_hbm, line, group, i, slot, spot).start()
+
+    def start_tile(line, group, t):
+        for spot in range(TILE):
+            start_bias(line, group, TILE * t + spot, lax.rem(t, 2), spot)
+
+    @pl.when((g == 0) & (r == 0))
+    def _():
+        for line in range(2):
+
+            def place(z, count):
+                table_ref[line, 0, count] = z
+                table_ref[line, 1, count] = lax.rem(z // 2, 2) ^ c
+                holder = lax.rem(2 * half + z // 8 + (2 if line == 0 else 0), 4)
+                table_ref[line, 2, count] = 2 * holder + lax.rem(z // 4, 2)
+                return count + jnp.where(is_live(line, z), 1, 0)
+
+            live = lax.fori_loop(0, blocks, place, 0)
+            live_ref[line] = live
+
+            def repeat(i, carry):
+                for row in range(3):
+                    table_ref[line, row, i] = table_ref[line, row, 0]
+                return carry
+
+            lax.fori_loop(live, blocks, repeat, 0)
+
+        def needed(i, carry):
+            row_copy(table_ref[0, 0, i]).start()
+            return carry
+
+        def other(z, carry):
+            @pl.when(jnp.logical_not(is_live(0, z)))
+            def _():
+                row_copy(z).start()
+
+            return carry
+
+        first = jnp.minimum(live_ref[0], TILE)
+        lax.fori_loop(0, first, needed, 0)
+
+        @pl.when(live_ref[0] > 0)
+        def _():
+            start_tile(0, 0, 0)
+
+        lax.fori_loop(first, live_ref[0], needed, 0)
+        lax.fori_loop(0, blocks, other, 0)
+
+    live = live_ref[r]
 
     acc_ref[...] = jnp.zeros_like(acc_ref)
     sum_ref[...] = jnp.zeros_like(sum_ref)
@@ -146,11 +195,32 @@
             query_ref[0, 0, s], rows, (((1,), (1,)), ((), ())), preferred_element_type=jnp.float32
         )
 
-    def tile(start, size, partial):
-        spots = [start + i for i in range(size)]
-        z = [table_ref[0, i] for i in spots]
+    tiles = (live + TILE - 1) // TILE
+
+    def unpacked(slot, spot):
+        return (packed_ref[slot, spot].astype(jnp.float32) * LOG2E).reshape(GROUP * span, BLOCK)
+
+    def tile(t, size, partial):
+        @pl.when(t + 1 < tiles)
+        def _():
+            start_tile(r, g, t + 1)
+
+        slot = lax.rem(t, 2)
+        spots = [TILE * t + i for i in range(size)]
+        z = [table_ref[r, 0, i] for i in spots]
+
+        @pl.when((g == 0) & (r == 0))
+        def _():
+            for i in range(size):
+
+                @pl.when(spots[i] < live)
+                def _():
+                    row_copy(z[i]).wait()
+
+        for i in range(TILE):
+            bias_copy(near_hbm, r, g, TILE * t + i, slot, i).wait()
         for i in range(size):
-            bias = bias_of(spots[i])
+            bias = unpacked(slot, i)
             if partial:
                 bias = bias + jnp.where(spots[i] < live, 0.0, LOW)
             bias_ref[:, i * BLOCK : (i + 1) * BLOCK] = bias
@@ -176,7 +246,7 @@
         add(depth - 1, weight)
 
     def full(t, carry):
-        tile(TILE * t, TILE, False)
+        tile(t, TILE, False)
         return carry
 
     rest = lax.rem(live, TILE)
@@ -184,11 +254,11 @@
 
     @pl.when(rest > 2)
     def _():
-        tile(live - rest, TILE, True)
+        tile(tiles - 1, TILE, True)
 
     @pl.when((rest > 0) & (rest <= 2))
     def _():
-        tile(live - rest, 2, True)
+        tile(tiles - 1, 2, True)
 
     largest, least = 0.0, SAFE_HIGH
     for s in range(depth):
@@ -206,8 +276,10 @@
         sum_ref[...] = jnp.zeros_like(sum_ref)
 
         def careful(t, carry):
-            z = table_ref[0, t]
-            bias_ref[:, :BLOCK] = bias_of(t)
+            z = table_ref[r, 0, t]
+            start_bias(r, g, t, 0, 0)
+            bias_copy(near_hbm, r, g, t, 0, 0).wait()
+            bias_ref[:, :BLOCK] = unpacked(0, 0)
 
             def one(s, inner):
                 score = scores(s, rows_ref[z, s]) + bias_ref[:, :BLOCK]
@@ -225,6 +297,23 @@
             return lax.fori_loop(0, depth, one, carry)
 
         lax.fori_loop(0, live, careful, 0)
+
+    follower = jnp.where(r == 0, 1, 0)
+
+    @pl.when(((g == 0) | (r == 0)) & (live_ref[follower] > 0))
+    def _():
+        start_tile(follower, g + r, 0)
+
+    @pl.when((g == 0) & (r == 0))
+    def _():
+        def arrived(z, carry):
+            @pl.when(jnp.logical_not(is_live(0, z)))
+            def _():
+                row_copy(z).wait()
+
+            return carry
+
+        lax.fori_loop(0, blocks, arrived, 0)
 
     head_of_lane = lax.broadcasted_iota(jnp.int32, (span, HALF), 1) // DH
     for s in range(depth):
@@ -262,23 +351,17 @@
 
 def attend(mask, rows, value_w, queries, near, far):
     blocks, depth, span, width = rows.shape
-    turns = near.shape[0]
-    bias = pl.BlockSpec((turns, GROUP, span, 2 * BLOCK), lambda g, r: (0, g, 0, 0))
     by_group = lambda g, r: (0, 0, g)
     return pl.pallas_call(
         attend_kernel,
         grid=(2, 2),
         in_specs=[
             pl.BlockSpec(memory_space=pltpu.SMEM),
-            pl.BlockSpec(
-                (blocks, depth, span, width),
-                lambda g, r: (0, 0, 0, 0),
-                pipeline_mode=pl.Buffered(1),
-            ),
+            pl.BlockSpec(memory_space=pl.ANY),
             pl.BlockSpec((width, HALF), lambda g, r: (0, g)),
             pl.BlockSpec((1, 1, depth, GROUP * span, width), lambda g, r: (r, g, 0, 0, 0)),
-            bias,
-            bias,
+            pl.BlockSpec(memory_space=pl.ANY),
+            pl.BlockSpec(memory_space=pl.ANY),
         ],
         out_specs=[
             pl.BlockSpec((depth, span + EXTRA, HALF), by_group),
@@ -289,11 +372,16 @@
             jax.ShapeDtypeStruct((depth, span + 8, width), jnp.float32),
         ],
         scratch_shapes=[
-            pltpu.SMEM((3, blocks), jnp.int32),
+            pltpu.SMEM((2, 3, blocks), jnp.int32),
+            pltpu.SMEM((2,), jnp.int32),
+            pltpu.VMEM((blocks, depth, span, width), jnp.bfloat16),
+            pltpu.VMEM((2, TILE, GROUP, span, BLOCK), jnp.bfloat16),
             pltpu.VMEM((GROUP * span, TILE * BLOCK), jnp.float32),
             pltpu.VMEM((depth, GROUP * span, width), jnp.float32),
             pltpu.VMEM((depth, GROUP * span, BLOCK), jnp.float32),
             pltpu.VMEM((depth, GROUP * span, 1), jnp.float32),
+            pltpu.SemaphoreType.DMA((blocks,)),
+            pltpu.SemaphoreType.DMA((2, TILE)),
         ],
         compiler_params=pltpu.CompilerParams(vmem_limit_bytes=56 * 1024 * 1024),
         name="attend",
@@ -352,16 +440,15 @@
     partner = lax.ppermute(alignment_features, "res", YL_PAIRS)
     normed = normalize(alignment_features, scale, offset)
     gathered = lax.all_gather(normed, "res", axis_index_groups=Z_GROUPS)
-
     swapped = lax.ppermute(coupling_logit_offset, ("seq", "res"), swap_pairs())
+    swapped, partner, normed = lax.optimization_barrier((swapped, partner, normed))
+    copies = jnp.broadcast_to(swapped[None], (SEQ // 2,) + swapped.shape)
+    near = lax.all_to_all(copies, "seq", 0, 0, axis_index_groups=PLANE_GROUPS, tiled=True)
+    far = lax.ppermute(near, "seq", C_PAIRS)
     queries, gate = prepare(
         normed, partner, scale, offset, probe_projection, lookup_projection, sigmoid_projection,
         sigmoid_offset_array[None, :],
     )
-    swapped, queries, gate = lax.optimization_barrier((swapped, queries, gate))
-    copies = jnp.broadcast_to(swapped[None], (SEQ // 2,) + swapped.shape)
-    near = lax.all_to_all(copies, "seq", 0, 0, axis_index_groups=PLANE_GROUPS, tiled=True)
-    far = lax.ppermute(near, "seq", C_PAIRS)
     sent, own = attend(contact_tile_filter, gathered, content_projection, queries, near, far)
     got = lax.ppermute(sent, "res", YL_PAIRS)
     return finish(own, got, gate, result_projection, result_offset[None, :])

time: 315 us -> 331 us (1.051)
  the two profiles are of different devices: /device:TPU:1 before, /device:TPU:360 now
where the time goes in v5:
time: 331 us; the launch traced here: 330 us
  Pallas kernels  220 us (66%)
  blocking collectives  55.5 us (17%)
  waiting for transfers between devices  26.4 us (8%)
  between operations  13.6 us (4%)
  starting transfers between devices  10.6 us (3%)
  local copies, waits for them, and re-layouts  4.02 us (1%)
    pallas_call x1, Pallas kernels, attend(): pl.pallas_call(attend_kernel, grid=(2, 2), in_specs=[pl.BlockSpec(memory_...  213 us
    all_to_all x1, blocking collectives, on_device(): lax.all_to_all(copies, 'seq', 0, 0, axis_index_groups=PLANE_GROUPS, tiled...  55.5 us
    ppermute x1, waiting for transfers between devices, on_device(): partner = lax.ppermute(alignment_features, 'res', YL_PAIRS)  15.1 us
    ppermute x1, waiting for transfers between devices, on_device(): got = lax.ppermute(sent, 'res', YL_PAIRS)  9.21 us
  transfers between devices with their start and end apart: 5, of which 3 were waited for; matrix products, arithmetic and copies ran while one was open for 0% of the time, Pallas kernels for 1%

profile of v5, /device:TPU:360, one launch (start us, length us, event | category | flops | bytes accessed | tf_op | source)
XLA Modules:
  0.0 330.1 jit_solution(4316310181018955273)
XLA Ops:
  6.5 4.8 %collective-permute-start = (bf16[8,128,256]{2,1,0:T(8,128)(2,1)}, bf16[8,128,256]{2,1,0:T(8,128)(2,1)S(1)}, u32[]{:S(2)}, u32[]{:S(2)}) collective-permute-start(bf16[8,128,256]{2,1,0:T(8,128)(2,1)} %param.13), channel_id=1, source_target_pairs={{0,0},{1,1},{2,2},{3,3},{4,4},{5,5},{6,6},{7,7},{8,8},{9,9},{10,10... | collective-permute-start | bytes 1572872 | tf_op jit(solution)/shard_map/ppermute | solution.py:443
  11.4 1.9 collective-permute-start.1
  13.3 2.0 normalize.1.normed_ref
  15.2 0.0 all-gather.3.cloned.1.call-update
  15.3 15.1 %collective-permute-done.1.partner_ref = bf16[4,128,256]{2,1,0:T(8,128)(2,1)S(1)} collective-permute-done((bf16[4,128,256]{2,1,0:T(8,128)(2,1)}, bf16[4,128,256]{2,1,0:T(8,128)(2,1)S(1)}, u32[]{:S(2)}, u32[]{:S(2)}) %collective-permute-start.1) | collective-permute-done | bytes 262176 | tf_op jit(solution)/shard_map/ppermute | solution.py:440
  30.3 0.5 broadcast_in_dim.21
  30.8 0.0 copy-start.1
  30.8 0.0 copy-start.3
  30.8 0.0 copy-start.4
  30.9 0.0 copy-start.5
  30.9 0.0 copy-start.6
  30.9 0.0 copy-start.7
  30.9 0.0 copy-start.8
  30.9 55.5 %all_to_all.5.near_hbm = bf16[8,8,128,256]{3,2,1,0:T(8,128)(2,1)} all-to-all(bf16[8,8,128,256]{3,2,1,0:T(8,128)(2,1)S(1)} %broadcast_in_dim.21), channel_id=1, replica_groups={{0,64,128,192,256,320,384,448},{32,96,160,224,288,352,416,480},{1,65,12..., dimensions={0} | all-to-all | bytes 8388608 | tf_op jit(solution)/shard_map/all_to_all | solution.py:446
  86.4 1.9 collective-permute-start.2
  88.4 2.5 prepare.1
  90.9 2.0 copy-done
  92.9 0.8 copy-done.2
  93.7 2.1 collective-permute-done.2.far_hbm
  95.8 213.1 %attend.1 = (bf16[4,144,256]{2,1,0:T(8,128)(2,1)}, f32[4,136,256]{2,1,0:T(8,128)}) custom-call(s32[32,32]{1,0:T(8,128)} %mask_ref.1, bf16[16,4,128,256]{3,2,1,0:T(8,128)(2,1)} %bitcast.10, bf16[256,256]{1,0:T(8,128)(2,1)} %value_w_ref.1, bf16[2,2,4,512,256]{4,3,2,1,0:T(8,128)(2,1)} %copy-done, bf16[8,8,128,256]{3,2,1,0:T(8,128)(2,1)} %all_to_all.5.near_hbm, ...), custom_call_target="tpu_custom_call" | custom-call | tf_op jit(solution)/shard_map/attend/pallas_call | solution.py:355
  308.9 1.9 collective-permute-start.3
  310.8 9.2 %collective-permute-done.3.got_ref = bf16[4,144,256]{2,1,0:T(8,128)(2,1)S(1)} collective-permute-done((bf16[4,144,256]{2,1,0:T(8,128)(2,1)}, bf16[4,144,256]{2,1,0:T(8,128)(2,1)S(1)}, u32[]{:S(2)}, u32[]{:S(2)}) %collective-permute-start.3) | collective-permute-done | bytes 294944 | tf_op jit(solution)/shard_map/ppermute | solution.py:453
  320.0 0.7 copy-done.9
  320.7 2.6 finish.1
  (13 shorter events, 0.0 us)
Async XLA Ops:
  6.5 87.1 %all-gather.3.cloned.1.call-start = ((), (), s32[]{:S(2)}) async-start(), calls=%async_computation.1 | async-start | bytes 4456448 | tf_op jit(solution)/shard_map/all_gather | solution.py:442
  6.5 23.8 %collective-permute-start = (bf16[8,128,256]{2,1,0:T(8,128)(2,1)}, bf16[8,128,256]{2,1,0:T(8,128)(2,1)S(1)}, u32[]{:S(2)}, u32[]{:S(2)}) collective-permute-start(bf16[8,128,256]{2,1,0:T(8,128)(2,1)} %param.13), channel_id=1, source_target_pairs={{0,0},{1,1},{2,2},{3,3},{4,4},{5,5},{6,6},{7,7},{8,8},{9,9},{10,10... | collective-permute-start | bytes 1572872 | tf_op jit(solution)/shard_map/ppermute | solution.py:443
  11.4 19.0 %collective-permute-start.1 = (bf16[4,128,256]{2,1,0:T(8,128)(2,1)}, bf16[4,128,256]{2,1,0:T(8,128)(2,1)S(1)}, u32[]{:S(2)}, u32[]{:S(2)}) collective-permute-start(bf16[4,128,256]{2,1,0:T(8,128)(2,1)} %features_ref.1), channel_id=1, source_target_pairs={{0,16},{1,17},{2,18},{3,19},{4,20},{5,21},{6,22},{7,23},{8,24},{9,... | collective-permute-start | bytes 786440 | tf_op jit(solution)/shard_map/ppermute | solution.py:440
  30.8 57.5 %copy-start.1 = (bf16[4,128,256]{2,1,0:T(8,128)(2,1)S(1)}, bf16[4,128,256]{2,1,0:T(8,128)(2,1)}, u32[]{:S(2)}) copy-start(bf16[4,128,256]{2,1,0:T(8,128)(2,1)} %normalize.1.normed_ref) | copy-start | bytes 786436
  30.8 57.5 %copy-start.3 = (bf16[256,256]{1,0:T(8,128)(2,1)S(1)}, bf16[256,256]{1,0:T(8,128)(2,1)}, u32[]{:S(2)}) copy-start(bf16[256,256]{1,0:T(8,128)(2,1)} %query_w_ref.1) | copy-start | bytes 393220
  30.8 57.5 %copy-start.4 = (bf16[256,256]{1,0:T(8,128)(2,1)S(1)}, bf16[256,256]{1,0:T(8,128)(2,1)}, u32[]{:S(2)}) copy-start(bf16[256,256]{1,0:T(8,128)(2,1)} %key_w_ref.1) | copy-start | bytes 393220
  30.9 57.5 %copy-start.5 = (bf16[256,256]{1,0:T(8,128)(2,1)S(1)}, bf16[256,256]{1,0:T(8,128)(2,1)}, u32[]{:S(2)}) copy-start(bf16[256,256]{1,0:T(8,128)(2,1)} %gate_w_ref.1) | copy-start | bytes 393220
  30.9 57.5 %copy-start.6 = (f32[256]{0:T(256)S(1)}, f32[256]{0:T(256)}, u32[]{:S(2)}) copy-start(f32[256]{0:T(256)} %param.15) | copy-start | bytes 3076
  30.9 57.5 %copy-start.7 = (f32[256]{0:T(256)S(1)}, f32[256]{0:T(256)}, u32[]{:S(2)}) copy-start(f32[256]{0:T(256)} %param.16) | copy-start | bytes 3076
  30.9 57.5 %copy-start.8 = (f32[256]{0:T(256)S(1)}, f32[256]{0:T(256)}, u32[]{:S(2)}) copy-start(f32[256]{0:T(256)} %param.21) | copy-start | bytes 3076
  86.4 9.4 %collective-permute-start.2 = (bf16[8,8,128,256]{3,2,1,0:T(8,128)(2,1)}, bf16[8,8,128,256]{3,2,1,0:T(8,128)(2,1)}, u32[]{:S(2)}, u32[]{:S(2)}) collective-permute-start(bf16[8,8,128,256]{3,2,1,0:T(8,128)(2,1)} %all_to_all.5.near_hbm), channel_id=1, source_target_pairs={{0,32},{32,0},{64,96},{96,64},{128,160},{160,128},{192,224},{224,1... | collective-permute-start | bytes 12582920 | tf_op jit(solution)/shard_map/ppermute | solution.py:447
  90.9 2.0 copy-start
  92.9 0.8 copy-start.2
  308.9 11.1 %collective-permute-start.3 = (bf16[4,144,256]{2,1,0:T(8,128)(2,1)}, bf16[4,144,256]{2,1,0:T(8,128)(2,1)S(1)}, u32[]{:S(2)}, u32[]{:S(2)}) collective-permute-start(bf16[4,144,256]{2,1,0:T(8,128)(2,1)} %get-tuple-element.17), channel_id=1, source_target_pairs={{0,16},{1,17},{2,18},{3,19},{4,20},{5,21},{6,22},{7,23},{8,24},{9,... | collective-permute-start | bytes 884744 | tf_op jit(solution)/shard_map/ppermute | solution.py:453
  320.0 0.7 copy-start.9
Sparse Core Ops, SparseCore 0:
  15.4 74.6 all-gather.2

commit v6 on v5

--- a/solution.py
+++ b/solution.py
@@ -1,3 +1,5 @@
+import functools
+
 import jax
 import jax.numpy as jnp
 import numpy as np
@@ -105,87 +107,78 @@
 
 
 def attend_kernel(
-    mask_ref, rows_hbm, value_w_ref, query_ref, near_hbm, far_hbm,
-    sent_ref, own_ref,
-    table_ref, live_ref, rows_ref, packed_ref, bias_ref, acc_ref, sum_ref, top_ref, row_sem, bias_sem,
+    own_line, mask_ref, rows_hbm, value_w_ref, query_ref, near_hbm, far_hbm,
+    out_ref,
+    table_ref, live_ref, rows_ref, packed_ref, bias_ref, acc_ref, sum_ref, top_ref, shift_ref, row_sem, bias_sem,
 ):
     blocks, depth, span, width = rows_ref.shape
-    g, r = pl.program_id(0), pl.program_id(1)
+    g = pl.program_id(0)
     seq, res = lax.axis_index("seq"), lax.axis_index("res")
     c, half, z_own = lax.rem(seq, 2), res // NZ, lax.rem(res, NZ)
 
-    def is_live(line, z):
-        yl = 1 - half if line == 0 else half
-        return mask_ref[yl * NZ + z_own, half * NZ + z] > 0
+    line = (half if own_line else 1 - half) * NZ + z_own
+
+    def is_live(z):
+        return mask_ref[line, half * NZ + z] > 0
 
     def row_copy(z):
         return pltpu.make_async_copy(rows_hbm.at[z], rows_ref.at[z], row_sem.at[z])
 
-    def bias_copy(source, line, group, i, slot, spot):
-        lanes = pl.ds(pl.multiple_of(lax.rem(table_ref[line, 0, i], 2) * BLOCK, BLOCK), BLOCK)
+    def bias_copy(source, group, i, slot, spot):
+        lanes = pl.ds(pl.multiple_of(lax.rem(table_ref[0, i], 2) * BLOCK, BLOCK), BLOCK)
         heads = pl.ds(group * GROUP, GROUP)
         return pltpu.make_async_copy(
-            source.at[table_ref[line, 2, i], heads, :, lanes],
+            source.at[table_ref[2, i], heads, :, lanes],
             packed_ref.at[slot, spot],
             bias_sem.at[slot, spot],
         )
 
-    def start_bias(line, group, i, slot, spot):
-        @pl.when(table_ref[line, 1, i] > 0)
+    def start_bias(group, i, slot, spot):
+        @pl.when(table_ref[1, i] > 0)
         def _():
-            bias_copy(far_hbm, line, group, i, slot, spot).start()
-
-        @pl.when(table_ref[line, 1, i] == 0)
+            bias_copy(far_hbm, group, i, slot, spot).start()
+
+        @pl.when(table_ref[1, i] == 0)
         def _():
-            bias_copy(near_hbm, line, group, i, slot, spot).start()
-
-    def start_tile(line, group, t):
+            bias_copy(near_hbm, group, i, slot, spot).start()
+
+    def start_tile(group, t):
         for spot in range(TILE):
-            start_bias(line, group, TILE * t + spot, lax.rem(t, 2), spot)
-
-    @pl.when((g == 0) & (r == 0))
+            start_bias(group, TILE * t + spot, lax.rem(t, 2), spot)
+
+    @pl.when(g == 0)
     def _():
-        for line in range(2):
-
-            def place(z, count):
-                table_ref[line, 0, count] = z
-                table_ref[line, 1, count] = lax.rem(z // 2, 2) ^ c
-                holder = lax.rem(2 * half + z // 8 + (2 if line == 0 else 0), 4)
-                table_ref[line, 2, count] = 2 * holder + lax.rem(z // 4, 2)
-                return count + jnp.where(is_live(line, z), 1, 0)
-
-            live = lax.fori_loop(0, blocks, place, 0)
-            live_ref[line] = live
-
-            def repeat(i, carry):
-                for row in range(3):
-                    table_ref[line, row, i] = table_ref[line, row, 0]
-                return carry
-
-            lax.fori_loop(live, blocks, repeat, 0)
+        def place(z, count):
+            table_ref[0, count] = z
+            table_ref[1, count] = lax.rem(z // 2, 2) ^ c
+            holder = lax.rem(2 * half + z // 8 + (0 if own_line else 2), 4)
+            table_ref[2, count] = 2 * holder + lax.rem(z // 4, 2)
+            return count + jnp.where(is_live(z), 1, 0)
+
+        count = lax.fori_loop(0, blocks, place, 0)
+        live_ref[0] = count
+
+        def repeat(i, carry):
+            for row in range(3):
+                table_ref[row, i] = table_ref[row, 0]
+            return carry
+
+        lax.fori_loop(count, blocks, repeat, 0)
 
         def needed(i, carry):
-            row_copy(table_ref[0, 0, i]).start()
+            row_copy(table_ref[0, i]).start()
             return carry
 
-        def other(z, carry):
-            @pl.when(jnp.logical_not(is_live(0, z)))
-            def _():
-                row_copy(z).start()
-
-            return carry
-
-        first = jnp.minimum(live_ref[0], TILE)
+        first = jnp.minimum(count, TILE)
         lax.fori_loop(0, first, needed, 0)
 
-        @pl.when(live_ref[0] > 0)
+        @pl.when(count > 0)
         def _():
-            start_tile(0, 0, 0)
-
-        lax.fori_loop(first, live_ref[0], needed, 0)
-        lax.fori_loop(0, blocks, other, 0)
-
-    live = live_ref[r]
+            start_tile(0, 0)
+
+        lax.fori_loop(first, count, needed, 0)
+
+    live = live_ref[0]
 
     acc_ref[...] = jnp.zeros_like(acc_ref)
     sum_ref[...] = jnp.zeros_like(sum_ref)
@@ -203,13 +196,13 @@
     def tile(t, size, partial):
         @pl.when(t + 1 < tiles)
         def _():
-            start_tile(r, g, t + 1)
+            start_tile(g, t + 1)
 
         slot = lax.rem(t, 2)
         spots = [TILE * t + i for i in range(size)]
-        z = [table_ref[r, 0, i] for i in spots]
-
-        @pl.when((g == 0) & (r == 0))
+        z = [table_ref[0, i] for i in spots]
+
+        @pl.when(g == 0)
         def _():
             for i in range(size):
 
@@ -218,7 +211,7 @@
                     row_copy(z[i]).wait()
 
         for i in range(TILE):
-            bias_copy(near_hbm, r, g, TILE * t + i, slot, i).wait()
+            bias_copy(near_hbm, g, TILE * t + i, slot, i).wait()
         for i in range(size):
             bias = unpacked(slot, i)
             if partial:
@@ -260,13 +253,14 @@
     def _():
         tile(tiles - 1, 2, True)
 
-    largest, least = 0.0, SAFE_HIGH
+    head_of_lane = lax.broadcasted_iota(jnp.int32, (span, HALF), 1) // DH
+    shift_ref[...] = jnp.zeros_like(shift_ref)
+    totals = []
     for s in range(depth):
-        total = jnp.sum(sum_ref[s], axis=1, keepdims=True)
-        sum_ref[s] = jnp.broadcast_to(total, (GROUP * span, BLOCK))
-        largest = jnp.maximum(largest, jnp.max(total))
-        least = jnp.minimum(least, jnp.min(total))
-        top_ref[s] = jnp.zeros_like(total)
+        totals.append(jnp.sum(sum_ref[s], axis=1, keepdims=True))
+        sum_ref[s] = jnp.broadcast_to(totals[s], (GROUP * span, BLOCK))
+    largest = jnp.max(jnp.maximum(*map(lambda p: jnp.maximum(*p), (totals[:2], totals[2:]))))
+    least = jnp.min(jnp.minimum(*map(lambda p: jnp.minimum(*p), (totals[:2], totals[2:]))))
     bad = (live > 0) & ((largest > SAFE_HIGH) | (least < SAFE_LOW))
 
     @pl.when(bad)
@@ -276,9 +270,9 @@
         sum_ref[...] = jnp.zeros_like(sum_ref)
 
         def careful(t, carry):
-            z = table_ref[r, 0, t]
-            start_bias(r, g, t, 0, 0)
-            bias_copy(near_hbm, r, g, t, 0, 0).wait()
+            z = table_ref[0, t]
+            start_bias(g, t, 0, 0)
+            bias_copy(near_hbm, g, t, 0, 0).wait()
             bias_ref[:, :BLOCK] = unpacked(0, 0)
 
             def one(s, inner):
@@ -297,93 +291,77 @@
             return lax.fori_loop(0, depth, one, carry)
 
         lax.fori_loop(0, live, careful, 0)
-
-    follower = jnp.where(r == 0, 1, 0)
-
-    @pl.when(((g == 0) | (r == 0)) & (live_ref[follower] > 0))
+        for s in range(depth):
+            for h in range(GROUP):
+                top = top_ref[s, h * span : (h + 1) * span]
+                shift_ref[s] = jnp.where(head_of_lane == h, top, shift_ref[s])
+
+    @pl.when((g == 0) & (live > 0))
     def _():
-        start_tile(follower, g + r, 0)
-
-    @pl.when((g == 0) & (r == 0))
-    def _():
-        def arrived(z, carry):
-            @pl.when(jnp.logical_not(is_live(0, z)))
-            def _():
-                row_copy(z).wait()
-
-            return carry
-
-        lax.fori_loop(0, blocks, arrived, 0)
-
-    head_of_lane = lax.broadcasted_iota(jnp.int32, (span, HALF), 1) // DH
+        start_tile(1, 0)
+
     for s in range(depth):
-        total = sum_ref[s]
-        some = total > 0.0
-        safe = jnp.where(some, total, 1.0)
-        lse = jnp.where(some, top_ref[s] + jnp.log2(safe), LOW)
-        inverse = 1.0 / safe
-        mixed = (acc_ref[s] * jnp.concatenate([inverse, inverse], axis=1)).astype(jnp.bfloat16)
-        values = jnp.dot(mixed, value_w_ref[...], preferred_element_type=jnp.float32)
-        mean = values[:span]
-        wide = lse[:span]
+        values = jnp.dot(
+            acc_ref[s].astype(jnp.bfloat16), value_w_ref[...], preferred_element_type=jnp.float32
+        )
+        mean, total = values[:span], sum_ref[s, :span]
         for h in range(1, GROUP):
             part = slice(h * span, (h + 1) * span)
             mean = jnp.where(head_of_lane == h, values[part], mean)
-            wide = jnp.where(head_of_lane == h, lse[part], wide)
-        wide = wide.T
+            total = jnp.where(head_of_lane == h, sum_ref[s, part], total)
+        some = total > 0.0
+        safe = jnp.where(some, total, 1.0)
+        mean = mean / safe
+        wide = jnp.where(some, shift_ref[s] + jnp.log2(safe), LOW).T
         lse = jnp.concatenate([wide[h * DH : h * DH + 1] for h in range(GROUP)], axis=0)
 
-        @pl.when(r == 0)
-        def _():
+        if own_line:
+            out_ref[s, :span] = mean
+            out_ref[s, span:] = jnp.concatenate([lse, jnp.zeros_like(lse)], axis=0)
+        else:
             first = lse.astype(jnp.bfloat16).astype(jnp.float32)
             second = (lse - first).astype(jnp.bfloat16).astype(jnp.float32)
             third = lse - first - second
-            sent_ref[s, :span] = mean.astype(jnp.bfloat16)
-            sent_ref[s, span:] = jnp.concatenate(
+            out_ref[s, :span] = mean.astype(jnp.bfloat16)
+            out_ref[s, span:] = jnp.concatenate(
                 [first, second, third, jnp.zeros_like(lse)], axis=0
             ).astype(jnp.bfloat16)
 
-        @pl.when(r == 1)
-        def _():
-            own_ref[s, :span] = mean
-            own_ref[s, span:] = jnp.concatenate([lse, jnp.zeros_like(lse)], axis=0)
-
-
-def attend(mask, rows, value_w, queries, near, far):
+
+def attend(own_line, mask, rows, value_w, queries, near, far):
     blocks, depth, span, width = rows.shape
-    by_group = lambda g, r: (0, 0, g)
+    r = int(own_line)
+    out_rows, out_type = (span + 8, jnp.float32) if own_line else (span + EXTRA, jnp.bfloat16)
     return pl.pallas_call(
-        attend_kernel,
-        grid=(2, 2),
+        functools.partial(attend_kernel, own_line),
+        grid=(2,),
         in_specs=[
             pl.BlockSpec(memory_space=pltpu.SMEM),
             pl.BlockSpec(memory_space=pl.ANY),
-            pl.BlockSpec((width, HALF), lambda g, r: (0, g)),
-            pl.BlockSpec((1, 1, depth, GROUP * span, width), lambda g, r: (r, g, 0, 0, 0)),
+            pl.BlockSpec((width, HALF), lambda g: (0, g)),
+            pl.BlockSpec((1, 1, depth, GROUP * span, width), lambda g: (r, g, 0, 0, 0)),
             pl.BlockSpec(memory_space=pl.ANY),
             pl.BlockSpec(memory_space=pl.ANY),
         ],
-        out_specs=[
-            pl.BlockSpec((depth, span + EXTRA, HALF), by_group),
-            pl.BlockSpec((depth, span + 8, HALF), by_group),
-        ],
-        out_shape=[
-            jax.ShapeDtypeStruct((depth, span + EXTRA, width), jnp.bfloat16),
-            jax.ShapeDtypeStruct((depth, span + 8, width), jnp.float32),
-        ],
+        out_specs=pl.BlockSpec((depth, out_rows, HALF), lambda g: (0, 0, g)),
+        out_shape=jax.ShapeDtypeStruct((depth, out_rows, width), out_type),
         scratch_shapes=[
-            pltpu.SMEM((2, 3, blocks), jnp.int32),
-            pltpu.SMEM((2,), jnp.int32),
+            pltpu.SMEM((3, blocks), jnp.int32),
+            pltpu.SMEM((1,), jnp.int32),
             pltpu.VMEM((blocks, depth, span, width), jnp.bfloat16),
             pltpu.VMEM((2, TILE, GROUP, span, BLOCK), jnp.bfloat16),
             pltpu.VMEM((GROUP * span, TILE * BLOCK), jnp.float32),
             pltpu.VMEM((depth, GROUP * span, width), jnp.float32),
             pltpu.VMEM((depth, GROUP * span, BLOCK), jnp.float32),
             pltpu.VMEM((depth, GROUP * span, 1), jnp.float32),
+            pltpu.VMEM((depth, span, HALF), jnp.float32),
             pltpu.SemaphoreType.DMA((blocks,)),
             pltpu.SemaphoreType.DMA((2, TILE)),
         ],
         compiler_params=pltpu.CompilerParams(vmem_limit_bytes=56 * 1024 * 1024),
+        cost_estimate=pl.CostEstimate(
+            flops=8 * 10**9, bytes_accessed=10 * 2**20, transcendentals=2**23
+        ),
         name="attend",
     )(mask, rows, value_w, queries, near, far)
 
@@ -440,7 +418,8 @@
     partner = lax.ppermute(alignment_features, "res", YL_PAIRS)
     normed = normalize(alignment_features, scale, offset)
     gathered = lax.all_gather(normed, "res", axis_index_groups=Z_GROUPS)
-    swapped = lax.ppermute(coupling_logit_offset, ("seq", "res"), swap_pairs())
+    normed, bias = lax.optimization_barrier((normed, coupling_logit_offset))
+    swapped = lax.ppermute(bias, ("seq", "res"), swap_pairs())
     swapped, partner, normed = lax.optimization_barrier((swapped, partner, normed))
     copies = jnp.broadcast_to(swapped[None], (SEQ // 2,) + swapped.shape)
     near = lax.all_to_all(copies, "seq", 0, 0, axis_index_groups=PLANE_GROUPS, tiled=True)
@@ -449,8 +428,9 @@
         normed, partner, scale, offset, probe_projection, lookup_projection, sigmoid_projection,
         sigmoid_offset_array[None, :],
     )
-    sent, own = attend(contact_tile_filter, gathered, content_projection, queries, near, far)
-    got = lax.ppermute(sent, "res", YL_PAIRS)
+    inputs = (contact_tile_filter, gathered, content_projection, queries, near, far)
+    got = lax.ppermute(attend(False, *inputs), "res", YL_PAIRS)
+    own = attend(True, *inputs)
     return finish(own, got, gate, result_projection, result_offset[None, :])
 
 

time: 331 us -> 329 us (level)
  the two profiles are of different devices: /device:TPU:360 before, /device:TPU:105 now
where the time goes in v6:
time: 329 us; the launch traced here: 328 us
  Pallas kernels  221 us (67%)
  blocking collectives  53.6 us (16%)
  waiting for transfers between devices  19.3 us (6%)
  starting transfers between devices  16.6 us (5%)
  between operations  13.6 us (4%)
  local copies, waits for them, and re-layouts  3.96 us (1%)
    pallas_call x2, Pallas kernels, attend(): pl.pallas_call(functools.partial(attend_kernel, own_line), grid=(2,), in_...  214 us
    all_to_all x1, blocking collectives, on_device(): lax.all_to_all(copies, 'seq', 0, 0, axis_index_groups=PLANE_GROUPS, tiled...  53.6 us
    ppermute x1, waiting for transfers between devices, on_device(): partner = lax.ppermute(alignment_features, 'res', YL_PAIRS)  17.5 us
  transfers between devices with their start and end apart: 5, of which 2 were waited for; matrix products, arithmetic and copies ran while one was open for 0% of the time, Pallas kernels for 61%

profile of v6, /device:TPU:105, one launch (start us, length us, event | category | flops | bytes accessed | tf_op | source)
XLA Modules:
  0.0 327.7 jit_solution(2610689013296752562)
XLA Ops:
  6.5 1.9 normalize.1.normed_ref
  8.5 4.5 %collective-permute-start = (bf16[8,128,256]{2,1,0:T(8,128)(2,1)}, bf16[8,128,256]{2,1,0:T(8,128)(2,1)S(1)}, u32[]{:S(2)}, u32[]{:S(2)}) collective-permute-start(bf16[8,128,256]{2,1,0:T(8,128)(2,1)} %param.13), channel_id=1, source_target_pairs={{0,0},{1,1},{2,2},{3,3},{4,4},{5,5},{6,6},{7,7},{8,8},{9,9},{10,10... | collective-permute-start | bytes 1572872 | tf_op jit(solution)/shard_map/ppermute | solution.py:422
  13.0 1.9 collective-permute-start.1
  14.9 0.0 all-gather.3.cloned.1.call-update
  15.0 17.5 %collective-permute-done.1.partner_ref = bf16[4,128,256]{2,1,0:T(8,128)(2,1)S(1)} collective-permute-done((bf16[4,128,256]{2,1,0:T(8,128)(2,1)}, bf16[4,128,256]{2,1,0:T(8,128)(2,1)S(1)}, u32[]{:S(2)}, u32[]{:S(2)}) %collective-permute-start.1) | collective-permute-done | bytes 262176 | tf_op jit(solution)/shard_map/ppermute | solution.py:418
  32.4 0.5 broadcast_in_dim.21
  32.9 0.0 copy-start
  32.9 0.0 copy-start.2
  33.0 0.0 copy-start.3
  33.0 0.0 copy-start.4
  33.0 0.0 copy-start.5
  33.0 0.0 copy-start.6
  33.0 0.0 copy-start.7
  33.0 53.6 %all_to_all.5.near_hbm = bf16[8,8,128,256]{3,2,1,0:T(8,128)(2,1)} all-to-all(bf16[8,8,128,256]{3,2,1,0:T(8,128)(2,1)S(1)} %broadcast_in_dim.21), channel_id=1, replica_groups={{0,64,128,192,256,320,384,448},{32,96,160,224,288,352,416,480},{1,65,12..., dimensions={0} | all-to-all | bytes 8388608 | tf_op jit(solution)/shard_map/all_to_all | solution.py:425
  86.6 4.3 %collective-permute-start.2 = (bf16[8,8,128,256]{3,2,1,0:T(8,128)(2,1)}, bf16[8,8,128,256]{3,2,1,0:T(8,128)(2,1)}, u32[]{:S(2)}, u32[]{:S(2)}) collective-permute-start(bf16[8,8,128,256]{3,2,1,0:T(8,128)(2,1)} %all_to_all.5.near_hbm), channel_id=1, source_target_pairs={{0,32},{32,0},{64,96},{96,64},{128,160},{160,128},{192,224},{224,1... | collective-permute-start | bytes 12582920 | tf_op jit(solution)/shard_map/ppermute | solution.py:426
  91.0 2.5 prepare.1
  93.5 0.8 copy-done.1
  94.3 1.9 copy-done.8
  96.2 1.8 collective-permute-done.2.far_hbm
  98.0 16.4 %attend.3 = bf16[4,144,256]{2,1,0:T(8,128)(2,1)} custom-call(s32[32,32]{1,0:T(8,128)} %mask_ref.3, bf16[16,4,128,256]{3,2,1,0:T(8,128)(2,1)} %bitcast.11, bf16[256,256]{1,0:T(8,128)(2,1)} %value_w_ref.3, bf16[2,2,4,512,256]{4,3,2,1,0:T(8,128)(2,1)} %copy-done.8, bf16[8,8,128,256]{3,2,1,0:T(8,128)(2,1)} %all_to_all.5.near_hbm, ...), custom_call_target="tpu_custom_call" | custom-call | flops 8000000000 | bytes 10485760 | tf_op jit(solution)/shard_map/attend/pallas_call | solution.py:335
  114.4 5.9 %collective-permute-start.3 = (bf16[4,144,256]{2,1,0:T(8,128)(2,1)}, bf16[4,144,256]{2,1,0:T(8,128)(2,1)S(1)}, u32[]{:S(2)}, u32[]{:S(2)}) collective-permute-start(bf16[4,144,256]{2,1,0:T(8,128)(2,1)} %attend.3), channel_id=1, source_target_pairs={{0,16},{1,17},{2,18},{3,19},{4,20},{5,21},{6,22},{7,23},{8,24},{9,... | collective-permute-start | bytes 884744 | tf_op jit(solution)/shard_map/ppermute | solution.py:432
  120.3 197.2 %attend.2.own_ref = f32[4,136,256]{2,1,0:T(8,128)} custom-call(s32[32,32]{1,0:T(8,128)} %mask_ref.3, bf16[16,4,128,256]{3,2,1,0:T(8,128)(2,1)} %bitcast.12, bf16[256,256]{1,0:T(8,128)(2,1)} %value_w_ref.3, bf16[2,2,4,512,256]{4,3,2,1,0:T(8,128)(2,1)} %copy-done.8, bf16[8,8,128,256]{3,2,1,0:T(8,128)(2,1)} %all_to_all.5.near_hbm, ...), custom_call_target="tpu_custom_call" | custom-call | flops 8000000000 | bytes 10485760 | tf_op jit(solution)/shard_map/attend/pallas_call | solution.py:335
  317.6 0.7 copy-done.9
  318.3 2.6 finish.1
  (14 shorter events, 0.0 us)
Async XLA Ops:
  6.5 89.7 %all-gather.3.cloned.1.call-start = ((), (), s32[]{:S(2)}) async-start(), calls=%async_computation.1 | async-start | bytes 4456448 | tf_op jit(solution)/shard_map/all_gather | solution.py:420
  8.5 24.0 %collective-permute-start = (bf16[8,128,256]{2,1,0:T(8,128)(2,1)}, bf16[8,128,256]{2,1,0:T(8,128)(2,1)S(1)}, u32[]{:S(2)}, u32[]{:S(2)}) collective-permute-start(bf16[8,128,256]{2,1,0:T(8,128)(2,1)} %param.13), channel_id=1, source_target_pairs={{0,0},{1,1},{2,2},{3,3},{4,4},{5,5},{6,6},{7,7},{8,8},{9,9},{10,10... | collective-permute-start | bytes 1572872 | tf_op jit(solution)/shard_map/ppermute | solution.py:422
  13.0 19.4 %collective-permute-start.1 = (bf16[4,128,256]{2,1,0:T(8,128)(2,1)}, bf16[4,128,256]{2,1,0:T(8,128)(2,1)S(1)}, u32[]{:S(2)}, u32[]{:S(2)}) collective-permute-start(bf16[4,128,256]{2,1,0:T(8,128)(2,1)} %features_ref.1), channel_id=1, source_target_pairs={{0,16},{1,17},{2,18},{3,19},{4,20},{5,21},{6,22},{7,23},{8,24},{9,... | collective-permute-start | bytes 786440 | tf_op jit(solution)/shard_map/ppermute | solution.py:418
  32.9 58.0 %copy-start = (bf16[4,128,256]{2,1,0:T(8,128)(2,1)S(1)}, bf16[4,128,256]{2,1,0:T(8,128)(2,1)}, u32[]{:S(2)}) copy-start(bf16[4,128,256]{2,1,0:T(8,128)(2,1)} %normalize.1.normed_ref) | copy-start | bytes 786436
  32.9 58.0 %copy-start.2 = (bf16[256,256]{1,0:T(8,128)(2,1)S(1)}, bf16[256,256]{1,0:T(8,128)(2,1)}, u32[]{:S(2)}) copy-start(bf16[256,256]{1,0:T(8,128)(2,1)} %query_w_ref.1) | copy-start | bytes 393220
  33.0 58.0 %copy-start.3 = (bf16[256,256]{1,0:T(8,128)(2,1)S(1)}, bf16[256,256]{1,0:T(8,128)(2,1)}, u32[]{:S(2)}) copy-start(bf16[256,256]{1,0:T(8,128)(2,1)} %key_w_ref.1) | copy-start | bytes 393220
  33.0 58.0 %copy-start.4 = (bf16[256,256]{1,0:T(8,128)(2,1)S(1)}, bf16[256,256]{1,0:T(8,128)(2,1)}, u32[]{:S(2)}) copy-start(bf16[256,256]{1,0:T(8,128)(2,1)} %gate_w_ref.1) | copy-start | bytes 393220
  33.0 58.0 %copy-start.5 = (f32[256]{0:T(256)S(1)}, f32[256]{0:T(256)}, u32[]{:S(2)}) copy-start(f32[256]{0:T(256)} %param.15) | copy-start | bytes 3076
  33.0 58.0 %copy-start.6 = (f32[256]{0:T(256)S(1)}, f32[256]{0:T(256)}, u32[]{:S(2)}) copy-start(f32[256]{0:T(256)} %param.16) | copy-start | bytes 3076
  33.0 58.0 %copy-start.7 = (f32[256]{0:T(256)S(1)}, f32[256]{0:T(256)}, u32[]{:S(2)}) copy-start(f32[256]{0:T(256)} %param.21) | copy-start | bytes 3076
  86.6 11.4 %collective-permute-start.2 = (bf16[8,8,128,256]{3,2,1,0:T(8,128)(2,1)}, bf16[8,8,128,256]{3,2,1,0:T(8,128)(2,1)}, u32[]{:S(2)}, u32[]{:S(2)}) collective-permute-start(bf16[8,8,128,256]{3,2,1,0:T(8,128)(2,1)} %all_to_all.5.near_hbm), channel_id=1, source_target_pairs={{0,32},{32,0},{64,96},{96,64},{128,160},{160,128},{192,224},{224,1... | collective-permute-start | bytes 12582920 | tf_op jit(solution)/shard_map/ppermute | solution.py:426
  93.5 0.8 copy-start.1
  94.3 1.9 copy-start.8
  114.4 203.1 %collective-permute-start.3 = (bf16[4,144,256]{2,1,0:T(8,128)(2,1)}, bf16[4,144,256]{2,1,0:T(8,128)(2,1)S(1)}, u32[]{:S(2)}, u32[]{:S(2)}) collective-permute-start(bf16[4,144,256]{2,1,0:T(8,128)(2,1)} %attend.3), channel_id=1, source_target_pairs={{0,16},{1,17},{2,18},{3,19},{4,20},{5,21},{6,22},{7,23},{8,24},{9,... | collective-permute-start | bytes 884744 | tf_op jit(solution)/shard_map/ppermute | solution.py:432
  317.6 0.7 copy-start.9
Sparse Core Ops, SparseCore 0:
  15.1 72.5 all-gather.2

commit v7 on v6

--- a/solution.py
+++ b/solution.py
@@ -30,13 +30,15 @@
 def swap_pairs():
     pairs = []
     for x in range(4):
-        for other in range(4):
-            for yl in range(2):
-                for z in range(NZ):
-                    to_x, to_yl = (x, yl) if yl == x // 2 else ((x + 2) % 4, 1 - yl)
-                    source = (x * 4 + other) * RES + yl * NZ + z
-                    target = (to_x * 4 + other) * RES + to_yl * NZ + z
-                    pairs.append((source, target))
+        for yh in range(2):
+            for c in range(2):
+                for yl in range(2):
+                    for z in range(NZ):
+                        stays = yl == x // 2
+                        to = (x, yh, yl) if stays else ((x + 2) % 4, 1 - yh, 1 - yl)
+                        source = (x * 4 + yh * 2 + c) * RES + yl * NZ + z
+                        target = (to[0] * 4 + to[1] * 2 + c) * RES + to[2] * NZ + z
+                        pairs.append((source, target))
     return pairs
 
 
@@ -152,7 +154,7 @@
             table_ref[0, count] = z
             table_ref[1, count] = lax.rem(z // 2, 2) ^ c
             holder = lax.rem(2 * half + z // 8 + (0 if own_line else 2), 4)
-            table_ref[2, count] = 2 * holder + lax.rem(z // 4, 2)
+            table_ref[2, count] = 2 * holder + (lax.rem(z // 4, 2) ^ (0 if own_line else 1))
             return count + jnp.where(is_live(z), 1, 0)
 
         count = lax.fori_loop(0, blocks, place, 0)
@@ -418,8 +420,7 @@
     partner = lax.ppermute(alignment_features, "res", YL_PAIRS)
     normed = normalize(alignment_features, scale, offset)
     gathered = lax.all_gather(normed, "res", axis_index_groups=Z_GROUPS)
-    normed, bias = lax.optimization_barrier((normed, coupling_logit_offset))
-    swapped = lax.ppermute(bias, ("seq", "res"), swap_pairs())
+    swapped = lax.ppermute(coupling_logit_offset, ("seq", "res"), swap_pairs())
     swapped, partner, normed = lax.optimization_barrier((swapped, partner, normed))
     copies = jnp.broadcast_to(swapped[None], (SEQ // 2,) + swapped.shape)
     near = lax.all_to_all(copies, "seq", 0, 0, axis_index_groups=PLANE_GROUPS, tiled=True)

time: 329 us -> 327 us (level)
  the two profiles are of different devices: /device:TPU:105 before, /device:TPU:34 now
where the time goes in v7:
time: 327 us; the launch traced here: 326 us
  Pallas kernels  213 us (65%)
  blocking collectives  58.8 us (18%)
  starting transfers between devices  22.5 us (7%)
  waiting for transfers between devices  13.9 us (4%)
  between operations  13.6 us (4%)
  local copies, waits for them, and re-layouts  3.96 us (1%)
    pallas_call x2, Pallas kernels, attend(): pl.pallas_call(functools.partial(attend_kernel, own_line), grid=(2,), in_...  206 us
    all_to_all x1, blocking collectives, on_device(): lax.all_to_all(copies, 'seq', 0, 0, axis_index_groups=PLANE_GROUPS, tiled...  58.8 us
    ppermute x1, starting transfers between devices, on_device(): got = lax.ppermute(attend(False, *inputs), 'res', YL_PAIRS)  12 us
    all_gather x1, waiting for transfers between devices, on_device(): gathered = lax.all_gather(normed, 'res', axis_index_groups=Z_GROUPS)  9.65 us
    ppermute x1, starting transfers between devices, on_device(): partner = lax.ppermute(alignment_features, 'res', YL_PAIRS)  6.84 us
  transfers between devices with their start and end apart: 5, of which 2 were waited for; matrix products, arithmetic and copies ran while one was open for 0% of the time, Pallas kernels for 62%

profile of v7, /device:TPU:34, one launch (start us, length us, event | category | flops | bytes accessed | tf_op | source)
XLA Modules:
  0.0 326.2 jit_solution(4834163504417532490)
XLA Ops:
  6.5 1.7 collective-permute-start
  8.2 6.8 %collective-permute-start.1 = (bf16[4,128,256]{2,1,0:T(8,128)(2,1)}, bf16[4,128,256]{2,1,0:T(8,128)(2,1)S(1)}, u32[]{:S(2)}, u32[]{:S(2)}) collective-permute-start(bf16[4,128,256]{2,1,0:T(8,128)(2,1)} %features_ref.1), channel_id=1, source_target_pairs={{0,16},{1,17},{2,18},{3,19},{4,20},{5,21},{6,22},{7,23},{8,24},{9,... | collective-permute-start | bytes 786440 | tf_op jit(solution)/shard_map/ppermute | solution.py:420
  15.1 2.0 normalize.1.normed_ref
  17.0 0.0 all-gather.3.cloned.1.call-update
  17.1 4.2 %collective-permute-done.1.partner_ref = bf16[4,128,256]{2,1,0:T(8,128)(2,1)S(1)} collective-permute-done((bf16[4,128,256]{2,1,0:T(8,128)(2,1)}, bf16[4,128,256]{2,1,0:T(8,128)(2,1)S(1)}, u32[]{:S(2)}, u32[]{:S(2)}) %collective-permute-start.1) | collective-permute-done | bytes 262176 | tf_op jit(solution)/shard_map/ppermute | solution.py:420
  21.3 0.5 broadcast_in_dim.21
  21.8 0.0 copy-start
  21.8 0.0 copy-start.2
  21.8 0.0 copy-start.3
  21.8 0.0 copy-start.4
  21.8 0.0 copy-start.5
  21.9 0.0 copy-start.6
  21.9 0.0 copy-start.7
  21.9 58.8 %all_to_all.5.near_hbm = bf16[8,8,128,256]{3,2,1,0:T(8,128)(2,1)} all-to-all(bf16[8,8,128,256]{3,2,1,0:T(8,128)(2,1)S(1)} %broadcast_in_dim.21), channel_id=1, replica_groups={{0,64,128,192,256,320,384,448},{32,96,160,224,288,352,416,480},{1,65,12..., dimensions={0} | all-to-all | bytes 8388608 | tf_op jit(solution)/shard_map/all_to_all | solution.py:426
  80.7 1.9 collective-permute-start.2
  82.7 2.5 prepare.1
  85.2 0.8 copy-done.1
  86.0 1.9 copy-done.8
  87.9 9.7 %all-gather.3.cloned.1.call-done = bf16[64,128,256]{2,1,0:T(8,128)(2,1)} async-done(((bf16[4,128,256]{2,1,0:T(8,128)(2,1)}), bf16[64,128,256]{2,1,0:T(8,128)(2,1)}) %all-gather.3.cloned.1.call-update) | async-done | bytes 4194320 | tf_op jit(solution)/shard_map/all_gather | solution.py:422
  97.6 9.1 %attend.3 = bf16[4,144,256]{2,1,0:T(8,128)(2,1)} custom-call(s32[32,32]{1,0:T(8,128)} %mask_ref.3, bf16[16,4,128,256]{3,2,1,0:T(8,128)(2,1)} %bitcast.11, bf16[256,256]{1,0:T(8,128)(2,1)} %value_w_ref.3, bf16[2,2,4,512,256]{4,3,2,1,0:T(8,128)(2,1)} %copy-done.8, bf16[8,8,128,256]{3,2,1,0:T(8,128)(2,1)} %all_to_all.5.near_hbm, ...), custom_call_target="tpu_custom_call" | custom-call | flops 8000000000 | bytes 10485760 | tf_op jit(solution)/shard_map/attend/pallas_call | solution.py:337
  106.7 12.0 %collective-permute-start.3 = (bf16[4,144,256]{2,1,0:T(8,128)(2,1)}, bf16[4,144,256]{2,1,0:T(8,128)(2,1)S(1)}, u32[]{:S(2)}, u32[]{:S(2)}) collective-permute-start(bf16[4,144,256]{2,1,0:T(8,128)(2,1)} %attend.3), channel_id=1, source_target_pairs={{0,16},{1,17},{2,18},{3,19},{4,20},{5,21},{6,22},{7,23},{8,24},{9,... | collective-permute-start | bytes 884744 | tf_op jit(solution)/shard_map/ppermute | solution.py:433
  118.8 197.2 %attend.2.own_ref = f32[4,136,256]{2,1,0:T(8,128)} custom-call(s32[32,32]{1,0:T(8,128)} %mask_ref.3, bf16[16,4,128,256]{3,2,1,0:T(8,128)(2,1)} %bitcast.12, bf16[256,256]{1,0:T(8,128)(2,1)} %value_w_ref.3, bf16[2,2,4,512,256]{4,3,2,1,0:T(8,128)(2,1)} %copy-done.8, bf16[8,8,128,256]{3,2,1,0:T(8,128)(2,1)} %all_to_all.5.near_hbm, ...), custom_call_target="tpu_custom_call" | custom-call | flops 8000000000 | bytes 10485760 | tf_op jit(solution)/shard_map/attend/pallas_call | solution.py:337
  316.1 0.7 copy-done.9
  316.8 2.6 finish.1
  (14 shorter events, 0.0 us)
Async XLA Ops:
  6.5 91.1 %all-gather.3.cloned.1.call-start = ((), (), s32[]{:S(2)}) async-start(), calls=%async_computation.1 | async-start | bytes 4456448 | tf_op jit(solution)/shard_map/all_gather | solution.py:422
  6.5 14.8 %collective-permute-start = (bf16[8,128,256]{2,1,0:T(8,128)(2,1)}, bf16[8,128,256]{2,1,0:T(8,128)(2,1)S(1)}, u32[]{:S(2)}, u32[]{:S(2)}) collective-permute-start(bf16[8,128,256]{2,1,0:T(8,128)(2,1)} %param.13), channel_id=1, source_target_pairs={{0,0},{1,1},{2,2},{3,3},{4,4},{5,5},{6,6},{7,7},{8,8},{9,9},{10,10... | collective-permute-start | bytes 1572872 | tf_op jit(solution)/shard_map/ppermute | solution.py:423
  8.2 13.1 %collective-permute-start.1 = (bf16[4,128,256]{2,1,0:T(8,128)(2,1)}, bf16[4,128,256]{2,1,0:T(8,128)(2,1)S(1)}, u32[]{:S(2)}, u32[]{:S(2)}) collective-permute-start(bf16[4,128,256]{2,1,0:T(8,128)(2,1)} %features_ref.1), channel_id=1, source_target_pairs={{0,16},{1,17},{2,18},{3,19},{4,20},{5,21},{6,22},{7,23},{8,24},{9,... | collective-permute-start | bytes 786440 | tf_op jit(solution)/shard_map/ppermute | solution.py:420
  21.8 60.8 %copy-start = (bf16[4,128,256]{2,1,0:T(8,128)(2,1)S(1)}, bf16[4,128,256]{2,1,0:T(8,128)(2,1)}, u32[]{:S(2)}) copy-start(bf16[4,128,256]{2,1,0:T(8,128)(2,1)} %normalize.1.normed_ref) | copy-start | bytes 786436
  21.8 60.8 %copy-start.2 = (bf16[256,256]{1,0:T(8,128)(2,1)S(1)}, bf16[256,256]{1,0:T(8,128)(2,1)}, u32[]{:S(2)}) copy-start(bf16[256,256]{1,0:T(8,128)(2,1)} %query_w_ref.1) | copy-start | bytes 393220
  21.8 60.8 %copy-start.3 = (bf16[256,256]{1,0:T(8,128)(2,1)S(1)}, bf16[256,256]{1,0:T(8,128)(2,1)}, u32[]{:S(2)}) copy-start(bf16[256,256]{1,0:T(8,128)(2,1)} %key_w_ref.1) | copy-start | bytes 393220
  21.8 60.8 %copy-start.4 = (bf16[256,256]{1,0:T(8,128)(2,1)S(1)}, bf16[256,256]{1,0:T(8,128)(2,1)}, u32[]{:S(2)}) copy-start(bf16[256,256]{1,0:T(8,128)(2,1)} %gate_w_ref.1) | copy-start | bytes 393220
  21.8 60.8 %copy-start.5 = (f32[256]{0:T(256)S(1)}, f32[256]{0:T(256)}, u32[]{:S(2)}) copy-start(f32[256]{0:T(256)} %param.15) | copy-start | bytes 3076
  21.9 60.8 %copy-start.6 = (f32[256]{0:T(256)S(1)}, f32[256]{0:T(256)}, u32[]{:S(2)}) copy-start(f32[256]{0:T(256)} %param.16) | copy-start | bytes 3076
  21.9 60.8 %copy-start.7 = (f32[256]{0:T(256)S(1)}, f32[256]{0:T(256)}, u32[]{:S(2)}) copy-start(f32[256]{0:T(256)} %param.21) | copy-start | bytes 3076
  80.7 16.9 %collective-permute-start.2 = (bf16[8,8,128,256]{3,2,1,0:T(8,128)(2,1)}, bf16[8,8,128,256]{3,2,1,0:T(8,128)(2,1)}, u32[]{:S(2)}, u32[]{:S(2)}) collective-permute-start(bf16[8,8,128,256]{3,2,1,0:T(8,128)(2,1)} %all_to_all.5.near_hbm), channel_id=1, source_target_pairs={{0,32},{32,0},{64,96},{96,64},{128,160},{160,128},{192,224},{224,1... | collective-permute-start | bytes 12582920 | tf_op jit(solution)/shard_map/ppermute | solution.py:427
  85.2 0.8 copy-start.1
  86.0 1.9 copy-start.8
  106.7 209.3 %collective-permute-start.3 = (bf16[4,144,256]{2,1,0:T(8,128)(2,1)}, bf16[4,144,256]{2,1,0:T(8,128)(2,1)S(1)}, u32[]{:S(2)}, u32[]{:S(2)}) collective-permute-start(bf16[4,144,256]{2,1,0:T(8,128)(2,1)} %attend.3), channel_id=1, source_target_pairs={{0,16},{1,17},{2,18},{3,19},{4,20},{5,21},{6,22},{7,23},{8,24},{9,... | collective-permute-start | bytes 884744 | tf_op jit(solution)/shard_map/ppermute | solution.py:433
  316.1 0.7 copy-start.9
Sparse Core Ops, SparseCore 0:
  17.2 80.3 all-gather.2

commit v8 on v7

--- a/solution.py
+++ b/solution.py
@@ -417,10 +417,30 @@
     result_offset,
 ):
     scale, offset = standard_scale_array[None, :], standard_offset_array[None, :]
-    partner = lax.ppermute(alignment_features, "res", YL_PAIRS)
+    width = alignment_features.shape[-1]
     normed = normalize(alignment_features, scale, offset)
     gathered = lax.all_gather(normed, "res", axis_index_groups=Z_GROUPS)
-    swapped = lax.ppermute(coupling_logit_offset, ("seq", "res"), swap_pairs())
+
+    def travel(operands):
+        bias, features, _ = operands
+        return (
+            lax.ppermute(bias, ("seq", "res"), swap_pairs()),
+            lax.ppermute(features, "res", YL_PAIRS),
+        )
+
+    def travel_flat(operands):
+        bias, features, rows = operands
+        flat = lax.ppermute(bias.reshape(-1, bias.shape[-1]), ("seq", "res"), swap_pairs())
+        return flat.reshape(bias.shape), lax.ppermute(
+            features.reshape(-1, width), "res", YL_PAIRS
+        ).reshape(rows.shape)
+
+    swapped, partner = lax.cond(
+        contact_tile_filter[0, 0] > 0,
+        travel,
+        travel_flat,
+        (coupling_logit_offset, alignment_features, normed),
+    )
     swapped, partner, normed = lax.optimization_barrier((swapped, partner, normed))
     copies = jnp.broadcast_to(swapped[None], (SEQ // 2,) + swapped.shape)
     near = lax.all_to_all(copies, "seq", 0, 0, axis_index_groups=PLANE_GROUPS, tiled=True)

time: 327 us -> 325 us (level)
  the two profiles are of different devices: /device:TPU:34 before, /device:TPU:289 now
where the time goes in v8:
time: 325 us; the launch traced here: 324 us
  Pallas kernels  220 us (68%)
  blocking collectives  57.3 us (18%)
  starting transfers between devices  19.2 us (6%)
  between operations  14.3 us (4%)
  waiting for transfers between devices  6.87 us (2%)
  local copies, waits for them, and re-layouts  6.3 us (2%)
    pallas_call x2, Pallas kernels, attend(): pl.pallas_call(functools.partial(attend_kernel, own_line), grid=(2,), in_...  212 us
    all_to_all x1, blocking collectives, on_device(): lax.all_to_all(copies, 'seq', 0, 0, axis_index_groups=PLANE_GROUPS, tiled...  57.3 us
  transfers between devices with their start and end apart: 5, of which 2 were waited for; matrix products, arithmetic and copies ran while one was open for 1% of the time, Pallas kernels for 62%

profile of v8, /device:TPU:289, one launch (start us, length us, event | category | flops | bytes accessed | tf_op | source)
XLA Modules:
  0.0 323.9 jit_solution(9966429855793654260)
XLA Ops:
  6.5 1.9 normalize.1.normed_ref
  8.5 0.0 all-gather.3.cloned.1.call-update
  8.5 1.3 slice.3
  10.4 14.9 %conditional.1 = (bf16[8,128,256]{2,1,0:T(8,128)(2,1)}, bf16[4,128,256]{2,1,0:T(8,128)(2,1)}) conditional(s32[]{:T(128)} %bitcast.7, (bf16[8,128,256]{2,1,0:T(8,128)(2,1)}, bf16[4,128,256]{2,1,0:T(8,128)(2,1)}) %tuple.14, (bf16[8,128,256]{2,1,0:T(8,128)(2,1)}, bf16[4,128,256]{2,1,0:T(8,128)(2,1)}) %tuple.14), branch_computations={%region_0.0_spmd, %region_1.0_spmd} | conditional | bytes 3145824 | solution.py:438
  10.4 5.4 %collective-permute-start.2 = (bf16[8,128,256]{2,1,0:T(8,128)(2,1)}, bf16[8,128,256]{2,1,0:T(8,128)(2,1)}, u32[]{:S(2)}, u32[]{:S(2)}) collective-permute-start(bf16[8,128,256]{2,1,0:T(8,128)(2,1)} %get-tuple-element.15), channel_id=1, source_target_pairs={{0,0},{1,1},{2,2},{3,3},{4,4},{5,5},{6,6},{7,7},{8,8},{9,9},{10,10... | collective-permute-start | bytes 1572872 | tf_op jit(solution)/shard_map/cond/branch_1_fun/ppermute | solution.py:427
  15.8 3.5 %collective-permute-start.3 = (bf16[4,128,256]{2,1,0:T(8,128)(2,1)}, bf16[4,128,256]{2,1,0:T(8,128)(2,1)}, u32[]{:S(2)}, u32[]{:S(2)}) collective-permute-start(bf16[4,128,256]{2,1,0:T(8,128)(2,1)} %get-tuple-element.16), channel_id=1, source_target_pairs={{0,16},{1,17},{2,18},{3,19},{4,20},{5,21},{6,22},{7,23},{8,24},{9,... | collective-permute-start | bytes 786440 | tf_op jit(solution)/shard_map/cond/branch_1_fun/ppermute | solution.py:428
  19.3 6.0 %collective-permute-done.3 = bf16[4,128,256]{2,1,0:T(8,128)(2,1)} collective-permute-done((bf16[4,128,256]{2,1,0:T(8,128)(2,1)}, bf16[4,128,256]{2,1,0:T(8,128)(2,1)}, u32[]{:S(2)}, u32[]{:S(2)}) %collective-permute-start.3) | collective-permute-done | bytes 262176 | tf_op jit(solution)/shard_map/cond/branch_1_fun/ppermute | solution.py:428
  25.4 1.6 broadcast_in_dim.21
  26.9 0.0 copy-start
  26.9 0.0 copy-start.2
  26.9 0.0 copy-start.3
  27.0 0.0 copy-start.4
  27.0 0.0 copy-start.5
  27.0 57.3 %all_to_all.5.near_hbm = bf16[8,8,128,256]{3,2,1,0:T(8,128)(2,1)} all-to-all(bf16[8,8,128,256]{3,2,1,0:T(8,128)(2,1)S(1)} %broadcast_in_dim.21), channel_id=1, replica_groups={{0,64,128,192,256,320,384,448},{32,96,160,224,288,352,416,480},{1,65,12..., dimensions={0} | all-to-all | bytes 8388608 | tf_op jit(solution)/shard_map/all_to_all | solution.py:446
  84.3 5.3 %collective-permute-start.4 = (bf16[8,8,128,256]{3,2,1,0:T(8,128)(2,1)}, bf16[8,8,128,256]{3,2,1,0:T(8,128)(2,1)}, u32[]{:S(2)}, u32[]{:S(2)}) collective-permute-start(bf16[8,8,128,256]{3,2,1,0:T(8,128)(2,1)} %all_to_all.5.near_hbm), channel_id=1, source_target_pairs={{0,32},{32,0},{64,96},{96,64},{128,160},{160,128},{192,224},{224,1... | collective-permute-start | bytes 12582920 | tf_op jit(solution)/shard_map/ppermute | solution.py:447
  89.7 3.5 %prepare.1 = (bf16[2,2,4,512,256]{4,3,2,1,0:T(8,128)(2,1)S(1)}, f32[4,128,256]{2,1,0:T(8,128)S(1)}) custom-call(bf16[4,128,256]{2,1,0:T(8,128)(2,1)S(1)} %copy-done, bf16[4,128,256]{2,1,0:T(8,128)(2,1)} %get-tuple-element.27.partner_ref, f32[1,256]{1,0:T(1,128)S(1)} %bitcast.11, f32[1,256]{1,0:T(1,128)S(1)} %bitcast.13, bf16[256,256]{1,0:T(8,128)(2,1)S(1)} %copy-done.2, ...), custom_call_target="tpu_custom_call" | custom-call | flops 1000 | bytes 1000 | tf_op jit(solution)/shard_map/prepare/pallas_call | solution.py:99
  93.2 0.8 copy-done.1
  93.9 1.9 copy-done.8
  95.9 0.8 collective-permute-done.4.far_hbm
  96.7 14.7 %attend.3 = bf16[4,144,256]{2,1,0:T(8,128)(2,1)} custom-call(s32[32,32]{1,0:T(8,128)} %mask_ref.3, bf16[16,4,128,256]{3,2,1,0:T(8,128)(2,1)} %bitcast.17, bf16[256,256]{1,0:T(8,128)(2,1)} %value_w_ref.3, bf16[2,2,4,512,256]{4,3,2,1,0:T(8,128)(2,1)} %copy-done.8, bf16[8,8,128,256]{3,2,1,0:T(8,128)(2,1)} %all_to_all.5.near_hbm, ...), custom_call_target="tpu_custom_call" | custom-call | flops 8000000000 | bytes 10485760 | tf_op jit(solution)/shard_map/attend/pallas_call | solution.py:337
  111.4 5.0 %collective-permute-start.5 = (bf16[4,144,256]{2,1,0:T(8,128)(2,1)}, bf16[4,144,256]{2,1,0:T(8,128)(2,1)S(1)}, u32[]{:S(2)}, u32[]{:S(2)}) collective-permute-start(bf16[4,144,256]{2,1,0:T(8,128)(2,1)} %attend.3), channel_id=1, source_target_pairs={{0,16},{1,17},{2,18},{3,19},{4,20},{5,21},{6,22},{7,23},{8,24},{9,... | collective-permute-start | bytes 884744 | tf_op jit(solution)/shard_map/ppermute | solution.py:453
  116.5 197.3 %attend.2.own_ref = f32[4,136,256]{2,1,0:T(8,128)} custom-call(s32[32,32]{1,0:T(8,128)} %mask_ref.3, bf16[16,4,128,256]{3,2,1,0:T(8,128)(2,1)} %bitcast.18, bf16[256,256]{1,0:T(8,128)(2,1)} %value_w_ref.3, bf16[2,2,4,512,256]{4,3,2,1,0:T(8,128)(2,1)} %copy-done.8, bf16[8,8,128,256]{3,2,1,0:T(8,128)(2,1)} %all_to_all.5.near_hbm, ...), custom_call_target="tpu_custom_call" | custom-call | flops 8000000000 | bytes 10485760 | tf_op jit(solution)/shard_map/attend/pallas_call | solution.py:337
  313.8 0.7 copy-done.9
  314.5 2.6 finish.1
  (16 shorter events, 0.0 us)
Async XLA Ops:
  6.5 89.3 %all-gather.3.cloned.1.call-start = ((), (), s32[]{:S(2)}) async-start(), calls=%async_computation.1 | async-start | bytes 4456448 | tf_op jit(solution)/shard_map/all_gather | solution.py:422
  10.4 14.9 %collective-permute-start.2 = (bf16[8,128,256]{2,1,0:T(8,128)(2,1)}, bf16[8,128,256]{2,1,0:T(8,128)(2,1)}, u32[]{:S(2)}, u32[]{:S(2)}) collective-permute-start(bf16[8,128,256]{2,1,0:T(8,128)(2,1)} %get-tuple-element.15), channel_id=1, source_target_pairs={{0,0},{1,1},{2,2},{3,3},{4,4},{5,5},{6,6},{7,7},{8,8},{9,9},{10,10... | collective-permute-start | bytes 1572872 | tf_op jit(solution)/shard_map/cond/branch_1_fun/ppermute | solution.py:427
  15.8 9.5 %collective-permute-start.3 = (bf16[4,128,256]{2,1,0:T(8,128)(2,1)}, bf16[4,128,256]{2,1,0:T(8,128)(2,1)}, u32[]{:S(2)}, u32[]{:S(2)}) collective-permute-start(bf16[4,128,256]{2,1,0:T(8,128)(2,1)} %get-tuple-element.16), channel_id=1, source_target_pairs={{0,16},{1,17},{2,18},{3,19},{4,20},{5,21},{6,22},{7,23},{8,24},{9,... | collective-permute-start | bytes 786440 | tf_op jit(solution)/shard_map/cond/branch_1_fun/ppermute | solution.py:428
  26.9 62.7 %copy-start = (bf16[4,128,256]{2,1,0:T(8,128)(2,1)S(1)}, bf16[4,128,256]{2,1,0:T(8,128)(2,1)}, u32[]{:S(2)}) copy-start(bf16[4,128,256]{2,1,0:T(8,128)(2,1)} %normalize.1.normed_ref) | copy-start | bytes 786436
  26.9 62.7 %copy-start.2 = (bf16[256,256]{1,0:T(8,128)(2,1)S(1)}, bf16[256,256]{1,0:T(8,128)(2,1)}, u32[]{:S(2)}) copy-start(bf16[256,256]{1,0:T(8,128)(2,1)} %query_w_ref.1) | copy-start | bytes 393220
  26.9 62.7 %copy-start.3 = (bf16[256,256]{1,0:T(8,128)(2,1)S(1)}, bf16[256,256]{1,0:T(8,128)(2,1)}, u32[]{:S(2)}) copy-start(bf16[256,256]{1,0:T(8,128)(2,1)} %key_w_ref.1) | copy-start | bytes 393220
  27.0 62.7 %copy-start.4 = (bf16[256,256]{1,0:T(8,128)(2,1)S(1)}, bf16[256,256]{1,0:T(8,128)(2,1)}, u32[]{:S(2)}) copy-start(bf16[256,256]{1,0:T(8,128)(2,1)} %gate_w_ref.1) | copy-start | bytes 393220
  27.0 62.7 %copy-start.5 = (f32[256]{0:T(256)S(1)}, f32[256]{0:T(256)}, u32[]{:S(2)}) copy-start(f32[256]{0:T(256)} %param.17) | copy-start | bytes 3076
  27.0 62.7 %copy-start.6 = (f32[256]{0:T(256)S(1)}, f32[256]{0:T(256)}, u32[]{:S(2)}) copy-start(f32[256]{0:T(256)} %param.18) | copy-start | bytes 3076
  27.0 62.7 %copy-start.7 = (f32[256]{0:T(256)S(1)}, f32[256]{0:T(256)}, u32[]{:S(2)}) copy-start(f32[256]{0:T(256)} %param.23) | copy-start | bytes 3076
  84.3 12.4 %collective-permute-start.4 = (bf16[8,8,128,256]{3,2,1,0:T(8,128)(2,1)}, bf16[8,8,128,256]{3,2,1,0:T(8,128)(2,1)}, u32[]{:S(2)}, u32[]{:S(2)}) collective-permute-start(bf16[8,8,128,256]{3,2,1,0:T(8,128)(2,1)} %all_to_all.5.near_hbm), channel_id=1, source_target_pairs={{0,32},{32,0},{64,96},{96,64},{128,160},{160,128},{192,224},{224,1... | collective-permute-start | bytes 12582920 | tf_op jit(solution)/shard_map/ppermute | solution.py:447
  93.1 0.8 copy-start.1
  93.9 1.9 copy-start.8
  111.4 202.3 %collective-permute-start.5 = (bf16[4,144,256]{2,1,0:T(8,128)(2,1)}, bf16[4,144,256]{2,1,0:T(8,128)(2,1)S(1)}, u32[]{:S(2)}, u32[]{:S(2)}) collective-permute-start(bf16[4,144,256]{2,1,0:T(8,128)(2,1)} %attend.3), channel_id=1, source_target_pairs={{0,16},{1,17},{2,18},{3,19},{4,20},{5,21},{6,22},{7,23},{8,24},{9,... | collective-permute-start | bytes 884744 | tf_op jit(solution)/shard_map/ppermute | solution.py:453
  313.8 0.7 copy-start.9
Sparse Core Ops, SparseCore 0:
  9.4 66.8 all-gather.2
